TPU v7x, 32 devices: a whole 2x2x4 slice. The times are simulated.
32 devices in a mesh: seq: 8 (over z, x), head: 4 (over y, core).
Axes of the slice: x: 2, y: 2, z: 4, core: 2. Of those that a mesh axis runs over, the one named last changes fastest.
Arguments:
- activations: bfloat16 [2, 2, 1024, 1792], P(None, None, 'seq'), may hold values from -6 to 6
- offsets: int32 [2, 2], replicated, may hold values from 1 to 1023, as said below
- cotangent: bfloat16 [2, 2, 1024, 1792], P(None, None, 'seq'), may hold values from -6 to 6
- attn_query: bfloat16 [1792, 256], P('seq', 'head'), may hold values from -0.125 to 0.125
- attn_key: bfloat16 [1792, 256], P('seq', 'head'), may hold values from -0.125 to 0.125
- attn_value: bfloat16 [1792, 1792], P('seq', 'head'), may hold values from -0.125 to 0.125
- attn_output: bfloat16 [1792, 1792], P('head', 'seq'), may hold values from -3 to 3
- ffn1_gate: bfloat16 [1792, 4608], P('seq', 'head'), may hold values from -0.125 to 0.125
- ffn1_up: bfloat16 [1792, 4608], P('seq', 'head'), may hold values from -0.125 to 0.125
- ffn1_down: bfloat16 [4608, 1792], P('head', 'seq'), may hold values from -0.09375 to 0.09375
- conv_input: bfloat16 [1792, 1792], P('seq', 'head'), may hold values from -0.125 to 0.125
- conv_gate: bfloat16 [1792, 1792], P('seq', 'head'), may hold values from -0.125 to 0.125
- conv_output: bfloat16 [1792, 1792], P('head', 'seq'), may hold values from -0.125 to 0.125
- conv_kernel: bfloat16 [3, 1792], P(None, 'head'), may hold values from -3.5 to 3.5
- ffn2_gate: bfloat16 [1792, 4608], P('seq', 'head'), may hold values from -0.125 to 0.125
- ffn2_up: bfloat16 [1792, 4608], P('seq', 'head'), may hold values from -0.125 to 0.125
- ffn2_down: bfloat16 [4608, 1792], P('head', 'seq'), may hold values from -0.09375 to 0.09375
- norm_gains: bfloat16 [4, 1792], replicated, may hold values from 0.099609375 to 1.8984375
Outputs:
- block_output: bfloat16 [2, 2, 1024, 1792], P(None, None, 'seq')
- input_grad: float32 [2, 2, 1024, 1792], P(None, None, 'seq')
- query_grad: float32 [1792, 256], P('seq', 'head')
- key_grad: float32 [1792, 256], P('seq', 'head')
- value_grad: float32 [1792, 1792], P('seq', 'head')
- output_grad: float32 [1792, 1792], P('head', 'seq')
- ffn1_gate_grad: float32 [1792, 4608], P('seq', 'head')
- ffn1_up_grad: float32 [1792, 4608], P('seq', 'head')
- ffn1_down_grad: float32 [4608, 1792], P('head', 'seq')
- conv_input_grad: float32 [1792, 1792], P('seq', 'head')
- conv_gate_grad: float32 [1792, 1792], P('seq', 'head')
- conv_output_grad: float32 [1792, 1792], P('head', 'seq')
- conv_kernel_grad: float32 [3, 1792], P(None, 'head')
- ffn2_gate_grad: float32 [1792, 4608], P('seq', 'head')
- ffn2_up_grad: float32 [1792, 4608], P('seq', 'head')
- ffn2_down_grad: float32 [4608, 1792], P('head', 'seq')
- gains_grad: float32 [4, 1792], replicated
Inputs may be any that keep to these rules, and one draw needn't show every extreme that they name: In micro-batch m, sequence r holds one document at positions before offsets[m, r] and a second from there on; in every micro-batch some sequence's second document begins before position 128.
All inputs are finite; a program needn't handle non-finite values.
Results may differ from a plain program's by a relative error of at most 0.03.
Values may be sent and summed in bfloat16 or wider, within the bound.
A program may use at most 256 MiB of HBM per device.

v0:
```python
from functools import partial
import math

import jax
import jax.numpy as jnp
from jax import lax
from jax.sharding import PartitionSpec as P

QK = 16
VH = 112


EPSILON = 1e-05
PRECISE = lax.Precision.HIGHEST


def carried_in(shard, axis, combine, identity):
    length, here = (lax.axis_size(axis), lax.axis_index(axis))
    everything = jax.tree.map(
        lambda part, kind: lax.all_gather(part.astype(kind), axis),
        shard,
        (jnp.bfloat16, jnp.bfloat16, jnp.bfloat16),
    )
    start = jax.tree.map(
        lambda part, zero: jnp.broadcast_to(jnp.asarray(zero, part.dtype), part.shape),
        shard,
        identity,
    )

    def hop(k, before):
        reached = k < here
        new = combine(
            before, jax.tree.map(lambda part, own: part[k].astype(own.dtype), everything, shard)
        )
        return jax.tree.map(lambda a, b: jnp.where(reached, a, b), new, before)

    return lax.fori_loop(0, length, hop, start)


def passed_along(block, axis, distance):
    devices = range(lax.axis_size(axis))
    route = [(i - distance, i) for i in devices if i - distance in devices]
    return lax.ppermute(block, axis, route)


def entering(shard, axis, join, neutral):
    count = lax.axis_size(axis)
    place = lax.axis_index(axis)
    ahead = count - 1 - place
    gathered = jax.tree.map(
        lambda a, kind: lax.all_gather(a.astype(kind), axis),
        shard,
        jax.tree.map(lambda a: jnp.bfloat16 if a.dtype == jnp.float32 else a.dtype, shard),
    )
    state = jax.tree.map(lambda a, e: jnp.zeros_like(a) + jnp.asarray(e, a.dtype), shard, neutral)

    def one(hop, state):
        source = count - 1 - hop
        return join(
            state,
            jax.tree.map(
                lambda a, own: lax.dynamic_index_in_dim(a, source, 0, False).astype(own.dtype),
                gathered,
                shard,
            ),
        )

    return lax.fori_loop(0, ahead, one, state)


def rms_norm(values, gain):
    scale = lax.rsqrt(jnp.mean(values * values, axis=-1, keepdims=True) + EPSILON)
    return values * scale * gain


def taylor_map(feature):
    width = feature.shape[-1]
    square = (feature[..., :, None] * feature[..., None, :]).reshape(
        feature.shape[:-1] + (width * width,)
    )
    ones_col = jnp.ones(feature.shape[:-1] + (1,), jnp.float32)
    return jnp.concatenate(
        [ones_col, feature / width**0.25, square / math.sqrt(2.0 * width)], axis=-1
    )


def doc_masks(offsets, start_pos, tok_count):
    position = start_pos + jnp.arange(tok_count, dtype=jnp.int32)
    current = position[None, :] >= offsets[:, None]
    before = start_pos - 1 >= offsets
    last_doc = current[:, -1]
    use_in = (current == before[:, None]).astype(jnp.float32)
    end_mask = (current == last_doc[:, None]).astype(jnp.float32)
    carry_on = (last_doc == before).astype(jnp.float32)
    causal = position[:, None] >= position[None, :]
    pair_mask = (causal[None, :, :] & (current[:, :, None] == current[:, None, :])).astype(
        jnp.float32
    )
    return (use_in, end_mask, carry_on, pair_mask)


def local_state(keys_f, values_f, end_mask):
    feats = taylor_map(keys_f) * end_mask[:, :, None, None]
    state = jnp.einsum("rthf,rthv->rhfv", feats, values_f, precision=PRECISE)
    return (state, jnp.sum(feats, axis=1))


def attend_local(query_f, keys_f, values_f, state_in, norm_in, use_in, pair_mask):
    qk_width = query_f.shape[-1]
    scores = jnp.einsum("rphf,rjhf->rhpj", query_f, keys_f, precision=PRECISE) / math.sqrt(qk_width)
    weights = (1.0 + scores + 0.5 * scores * scores) * pair_mask[:, None, :, :]
    feats = taylor_map(query_f)
    numer = jnp.einsum("rhpj,rjhv->rphv", weights, values_f, precision=PRECISE)
    numer = numer + use_in[:, :, None, None] * jnp.einsum(
        "rphf,rhfv->rphv", feats, state_in, precision=PRECISE
    )
    denom = jnp.swapaxes(jnp.sum(weights, axis=-1), 1, 2)
    denom = denom + use_in[:, :, None] * jnp.einsum(
        "rphf,rhf->rph", feats, norm_in, precision=PRECISE
    )
    return numer / denom[..., None]


def chain_combine(earlier, later):
    keep_on = 1.0 - later[0]
    return (
        jnp.maximum(earlier[0], later[0]),
        later[1] + keep_on[:, None, None, None] * earlier[1],
        later[2] + keep_on[:, None, None] * earlier[2],
    )


def conv_local(start_pos, offsets, extended, kernel):
    tap_count = kernel.shape[0]
    length = extended.shape[1] - (tap_count - 1)
    position = start_pos + jnp.arange(length, dtype=jnp.int32)
    current = position[None, :] >= offsets[:, None]
    total = jnp.zeros((extended.shape[0], length, extended.shape[2]), jnp.float32)
    for shift_by in range(tap_count):
        source = position - shift_by
        valid = (source[None, :] >= 0) & ((source[None, :] >= offsets[:, None]) == current)
        piece = extended[:, tap_count - 1 - shift_by : tap_count - 1 - shift_by + length, :]
        total = total + kernel[shift_by][None, None, :] * piece * valid[:, :, None].astype(
            jnp.float32
        )
    return total


def swish_product(gate_val, up_val):
    return jax.nn.silu(gate_val) * up_val


def project(left, weight):
    return jnp.einsum("rtd,dn->rtn", left, weight, preferred_element_type=jnp.float32)


def back_project(grad, weight):
    return jnp.einsum("rtn,dn->rtd", grad, weight, preferred_element_type=jnp.float32)


def outer_grad(left, grad):
    return jnp.einsum("rtd,rtn->dn", left, grad, preferred_element_type=jnp.float32)


def head_total(partial_sum):
    return lax.psum(partial_sum.astype(jnp.bfloat16), "head").astype(jnp.float32)


def head_back_total(partial_sum):
    return lax.psum(partial_sum.astype(jnp.bfloat16), "head").astype(jnp.float32)


def gather_weights(shards):
    return (
        lax.all_gather(shards[0], "seq", axis=0, tiled=True),
        lax.all_gather(shards[1], "seq", axis=0, tiled=True),
        lax.all_gather(shards[2], "seq", axis=0, tiled=True),
        lax.all_gather(shards[3], "seq", axis=1, tiled=True),
        lax.all_gather(shards[4], "seq", axis=0, tiled=True),
        lax.all_gather(shards[5], "seq", axis=0, tiled=True),
        lax.all_gather(shards[6], "seq", axis=1, tiled=True),
        lax.all_gather(shards[7], "seq", axis=0, tiled=True),
        lax.all_gather(shards[8], "seq", axis=0, tiled=True),
        lax.all_gather(shards[9], "seq", axis=1, tiled=True),
        lax.all_gather(shards[10], "seq", axis=0, tiled=True),
        lax.all_gather(shards[11], "seq", axis=0, tiled=True),
        lax.all_gather(shards[12], "seq", axis=1, tiled=True),
    )


def scatter_grads(grads):
    return (
        lax.psum_scatter(
            grads[0].astype(jnp.bfloat16), "seq", scatter_dimension=0, tiled=True
        ).astype(jnp.float32),
        lax.psum_scatter(
            grads[1].astype(jnp.bfloat16), "seq", scatter_dimension=0, tiled=True
        ).astype(jnp.float32),
        lax.psum_scatter(
            grads[2].astype(jnp.bfloat16), "seq", scatter_dimension=0, tiled=True
        ).astype(jnp.float32),
        lax.psum_scatter(
            grads[3].astype(jnp.bfloat16), "seq", scatter_dimension=1, tiled=True
        ).astype(jnp.float32),
        lax.psum_scatter(
            grads[4].astype(jnp.bfloat16), "seq", scatter_dimension=0, tiled=True
        ).astype(jnp.float32),
        lax.psum_scatter(
            grads[5].astype(jnp.bfloat16), "seq", scatter_dimension=0, tiled=True
        ).astype(jnp.float32),
        lax.psum_scatter(
            grads[6].astype(jnp.bfloat16), "seq", scatter_dimension=1, tiled=True
        ).astype(jnp.float32),
        lax.psum_scatter(
            grads[7].astype(jnp.bfloat16), "seq", scatter_dimension=0, tiled=True
        ).astype(jnp.float32),
        lax.psum_scatter(
            grads[8].astype(jnp.bfloat16), "seq", scatter_dimension=0, tiled=True
        ).astype(jnp.float32),
        lax.psum_scatter(
            grads[9].astype(jnp.bfloat16), "seq", scatter_dimension=1, tiled=True
        ).astype(jnp.float32),
        lax.psum_scatter(
            grads[10].astype(jnp.bfloat16), "seq", scatter_dimension=0, tiled=True
        ).astype(jnp.float32),
        lax.psum_scatter(
            grads[11].astype(jnp.bfloat16), "seq", scatter_dimension=0, tiled=True
        ).astype(jnp.float32),
        lax.psum_scatter(
            grads[12].astype(jnp.bfloat16), "seq", scatter_dimension=1, tiled=True
        ).astype(jnp.float32),
    )


def mlp_forward(resid, gain, gate_w, up_w, down_w):
    normed = rms_norm(resid, gain).astype(jnp.bfloat16)
    gate_val = project(normed, gate_w)
    up_val = project(normed, up_w)
    hidden = swish_product(gate_val, up_val).astype(jnp.bfloat16)
    return (resid + head_total(project(hidden, down_w)), (normed, gate_val, up_val, hidden))


def mlp_backward(resid, grad_out, gain, saved, gate_w, up_w, down_w):
    normed, gate_val, up_val, hidden = saved
    grad_b = grad_out.astype(jnp.bfloat16)
    down_grad = outer_grad(hidden, grad_b)
    grad_hidden = back_project(grad_b, down_w)
    swish_back = jax.vjp(swish_product, gate_val, up_val)[1]
    grad_gate, grad_up = swish_back(grad_hidden)
    grad_gate_b = grad_gate.astype(jnp.bfloat16)
    grad_up_b = grad_up.astype(jnp.bfloat16)
    gate_grad = outer_grad(normed, grad_gate_b)
    up_grad = outer_grad(normed, grad_up_b)
    grad_normed = head_back_total(back_project(grad_gate_b, gate_w) + back_project(grad_up_b, up_w))
    norm_back = jax.vjp(rms_norm, resid, gain)[1]
    grad_resid, gain_grad = norm_back(grad_normed)
    return (grad_out + grad_resid, gain_grad, (gate_grad, up_grad, down_grad))


def forward_batch(inputs, offsets, full, gains_f, kernel_f):
    (
        query_w,
        key_w,
        value_w,
        output_w,
        gate_one,
        up_one,
        down_one,
        inner_w,
        gate_conv_w,
        out_conv_w,
        gate_two,
        up_two,
        down_two,
    ) = full
    row_count, tok_count, model_width = inputs.shape
    start_pos = lax.axis_index("seq") * tok_count
    use_in, end_mask, carry_on, pair_mask = doc_masks(offsets, start_pos, tok_count)
    normed_a = rms_norm(inputs, gains_f[0]).astype(jnp.bfloat16)
    query_b = project(normed_a, query_w).astype(jnp.bfloat16)
    keys_b = project(normed_a, key_w).astype(jnp.bfloat16)
    values_b = project(normed_a, value_w).astype(jnp.bfloat16)
    head_count = query_b.shape[-1] // QK
    query_f = query_b.astype(jnp.float32).reshape(row_count, tok_count, head_count, QK)
    keys_f = keys_b.astype(jnp.float32).reshape(row_count, tok_count, head_count, QK)
    values_f = values_b.astype(jnp.float32).reshape(row_count, tok_count, head_count, VH)
    state_loc, norm_loc = local_state(keys_f, values_f, end_mask)
    reset_flags = 1.0 - carry_on
    scan_zero = (jnp.zeros_like(reset_flags), jnp.zeros_like(state_loc), jnp.zeros_like(norm_loc))
    prefix = carried_in((reset_flags, state_loc, norm_loc), "seq", chain_combine, scan_zero)
    attended = attend_local(query_f, keys_f, values_f, prefix[1], prefix[2], use_in, pair_mask)
    mixed_b = attended.reshape(row_count, tok_count, head_count * VH).astype(jnp.bfloat16)
    resid_one = inputs + head_total(project(mixed_b, output_w))
    resid_two, kept_one = mlp_forward(resid_one, gains_f[1], gate_one, up_one, down_one)
    normed_c = rms_norm(resid_two, gains_f[2]).astype(jnp.bfloat16)
    inner_val = project(normed_c, inner_w)
    gate_c = project(normed_c, gate_conv_w)
    tap_count = kernel_f.shape[0]
    edge_rows = passed_along(inner_val[:, tok_count - (tap_count - 1) :, :], "seq", 1)
    extended = jnp.concatenate([edge_rows, inner_val], axis=1)
    mixed_conv = conv_local(start_pos, offsets, extended, kernel_f)
    product_b = (mixed_conv * gate_c).astype(jnp.bfloat16)
    resid_three = resid_two + head_total(project(product_b, out_conv_w))
    resid_four, kept_two = mlp_forward(resid_three, gains_f[3], gate_two, up_two, down_two)
    saved = dict(
        inputs=inputs,
        start_pos=start_pos,
        use_in=use_in,
        end_mask=end_mask,
        pair_mask=pair_mask,
        reset_flags=reset_flags,
        scan_zero=scan_zero,
        normed_a=normed_a,
        query_f=query_f,
        keys_f=keys_f,
        values_f=values_f,
        prefix=prefix,
        mixed_b=mixed_b,
        resid_one=resid_one,
        kept_one=kept_one,
        resid_two=resid_two,
        normed_c=normed_c,
        gate_c=gate_c,
        extended=extended,
        mixed_conv=mixed_conv,
        product_b=product_b,
        resid_three=resid_three,
        kept_two=kept_two,
    )
    return (resid_four, saved)


def backward_batch(grad_four, offsets, saved, full, gains_f, kernel_f):
    (
        query_w,
        key_w,
        value_w,
        output_w,
        gate_one,
        up_one,
        down_one,
        inner_w,
        gate_conv_w,
        out_conv_w,
        gate_two,
        up_two,
        down_two,
    ) = full
    row_count, tok_count, model_width = grad_four.shape
    start_pos = saved["start_pos"]
    grad_three, gain_four, grads_two = mlp_backward(
        saved["resid_three"], grad_four, gains_f[3], saved["kept_two"], gate_two, up_two, down_two
    )
    grad_b = grad_three.astype(jnp.bfloat16)
    conv_out_grad = outer_grad(saved["product_b"], grad_b)
    grad_product = back_project(grad_b, out_conv_w)
    grad_mixed = grad_product * saved["gate_c"]
    grad_gate_c = (grad_product * saved["mixed_conv"]).astype(jnp.bfloat16)
    conv_back = jax.vjp(partial(conv_local, start_pos, offsets), saved["extended"], kernel_f)[1]
    grad_ext, kernel_grad = conv_back(grad_mixed)
    tap_count = kernel_f.shape[0]
    back_rows = passed_along(grad_ext[:, : tap_count - 1, :], "seq", -1)
    grad_inner = grad_ext[:, tap_count - 1 :, :] + jnp.pad(
        back_rows, ((0, 0), (tok_count - (tap_count - 1), 0), (0, 0))
    )
    grad_inner_b = grad_inner.astype(jnp.bfloat16)
    conv_in_grad = outer_grad(saved["normed_c"], grad_inner_b)
    conv_gate_grad = outer_grad(saved["normed_c"], grad_gate_c)
    grad_normed = head_back_total(
        back_project(grad_inner_b, inner_w) + back_project(grad_gate_c, gate_conv_w)
    )
    norm_back = jax.vjp(rms_norm, saved["resid_two"], gains_f[2])[1]
    grad_resid, gain_three = norm_back(grad_normed)
    grad_two = grad_three + grad_resid
    grad_one, gain_two, grads_one = mlp_backward(
        saved["resid_one"], grad_two, gains_f[1], saved["kept_one"], gate_one, up_one, down_one
    )
    grad_b = grad_one.astype(jnp.bfloat16)
    output_grad = outer_grad(saved["mixed_b"], grad_b)
    head_count = saved["query_f"].shape[2]
    grad_att = back_project(grad_b, output_w).reshape(row_count, tok_count, head_count, VH)
    prefix = saved["prefix"]
    attend_back = jax.vjp(
        partial(attend_local, use_in=saved["use_in"], pair_mask=saved["pair_mask"]),
        saved["query_f"],
        saved["keys_f"],
        saved["values_f"],
        prefix[1],
        prefix[2],
    )[1]
    grad_query, grad_keys, grad_values, grad_state, grad_norm = attend_back(grad_att)
    suffix = entering(
        (saved["reset_flags"], grad_state, grad_norm), "seq", chain_combine, saved["scan_zero"]
    )
    state_back = jax.vjp(
        partial(local_state, end_mask=saved["end_mask"]), saved["keys_f"], saved["values_f"]
    )[1]
    more_keys, more_values = state_back((suffix[1], suffix[2]))
    query_gb = grad_query.reshape(row_count, tok_count, head_count * QK).astype(jnp.bfloat16)
    keys_gb = (
        (grad_keys + more_keys).reshape(row_count, tok_count, head_count * QK).astype(jnp.bfloat16)
    )
    values_gb = (
        (grad_values + more_values)
        .reshape(row_count, tok_count, head_count * VH)
        .astype(jnp.bfloat16)
    )
    normed_a = saved["normed_a"]
    query_grad = outer_grad(normed_a, query_gb)
    key_grad = outer_grad(normed_a, keys_gb)
    value_grad = outer_grad(normed_a, values_gb)
    part_sum = (
        back_project(query_gb, query_w)
        + back_project(keys_gb, key_w)
        + back_project(values_gb, value_w)
    )
    grad_normed = head_back_total(part_sum)
    norm_back = jax.vjp(rms_norm, saved["inputs"], gains_f[0])[1]
    grad_resid, gain_one = norm_back(grad_normed)
    grad_inputs = grad_one + grad_resid
    weight_grads = (
        query_grad,
        key_grad,
        value_grad,
        output_grad,
        grads_one[0],
        grads_one[1],
        grads_one[2],
        conv_in_grad,
        conv_gate_grad,
        conv_out_grad,
        grads_two[0],
        grads_two[1],
        grads_two[2],
    )
    gain_grads = jnp.stack([gain_one, gain_two, gain_three, gain_four])
    return (grad_inputs, weight_grads, gain_grads, kernel_grad)


def per_device(
    activations,
    offsets,
    cotangent,
    attn_query,
    attn_key,
    attn_value,
    attn_output,
    ffn1_gate,
    ffn1_up,
    ffn1_down,
    conv_input,
    conv_gate,
    conv_output,
    conv_kernel,
    ffn2_gate,
    ffn2_up,
    ffn2_down,
    norm_gains,
):
    shards = (
        attn_query,
        attn_key,
        attn_value,
        attn_output,
        ffn1_gate,
        ffn1_up,
        ffn1_down,
        conv_input,
        conv_gate,
        conv_output,
        ffn2_gate,
        ffn2_up,
        ffn2_down,
    )
    gains_f = norm_gains.astype(jnp.float32)
    kernel_f = conv_kernel.astype(jnp.float32)
    micro_count = activations.shape[0]
    outputs = []
    input_grads = []
    gain_total = jnp.zeros(norm_gains.shape, jnp.float32)
    kernel_total = jnp.zeros(conv_kernel.shape, jnp.float32)
    shard_sums = None
    for batch_index in range(micro_count):
        forward_full = gather_weights(shards)
        inputs = activations[batch_index].astype(jnp.float32)
        resid_four, saved = forward_batch(
            inputs, offsets[batch_index], forward_full, gains_f, kernel_f
        )
        outputs.append(resid_four.astype(jnp.bfloat16))
        backward_full = gather_weights(shards)
        grad_four = cotangent[batch_index].astype(jnp.float32)
        grad_inputs, weight_grads, gain_grads, kernel_grad = backward_batch(
            grad_four, offsets[batch_index], saved, backward_full, gains_f, kernel_f
        )
        input_grads.append(grad_inputs)
        gain_total = gain_total + gain_grads
        kernel_total = kernel_total + kernel_grad
        pieces = scatter_grads(weight_grads)
        if shard_sums is None:
            shard_sums = pieces
        else:
            shard_sums = tuple((left + right for left, right in zip(shard_sums, pieces)))
    small_sums = (
        lax.psum(gain_total.astype(jnp.bfloat16), "seq").astype(jnp.float32),
        lax.psum(kernel_total.astype(jnp.bfloat16), "seq").astype(jnp.float32),
    )
    return (
        jnp.stack(outputs),
        jnp.stack(input_grads),
        shard_sums[0],
        shard_sums[1],
        shard_sums[2],
        shard_sums[3],
        shard_sums[4],
        shard_sums[5],
        shard_sums[6],
        shard_sums[7],
        shard_sums[8],
        shard_sums[9],
        small_sums[1],
        shard_sums[10],
        shard_sums[11],
        shard_sums[12],
        small_sums[0],
    )


def solution(mesh):
    in_specs = (
        P(None, None, "seq", None),
        P(),
        P(None, None, "seq", None),
        P("seq", "head"),
        P("seq", "head"),
        P("seq", "head"),
        P("head", "seq"),
        P("seq", "head"),
        P("seq", "head"),
        P("head", "seq"),
        P("seq", "head"),
        P("seq", "head"),
        P("head", "seq"),
        P(None, "head"),
        P("seq", "head"),
        P("seq", "head"),
        P("head", "seq"),
        P(),
    )
    out_specs = (
        P(None, None, "seq", None),
        P(None, None, "seq", None),
        P("seq", "head"),
        P("seq", "head"),
        P("seq", "head"),
        P("head", "seq"),
        P("seq", "head"),
        P("seq", "head"),
        P("head", "seq"),
        P("seq", "head"),
        P("seq", "head"),
        P("head", "seq"),
        P(None, "head"),
        P("seq", "head"),
        P("seq", "head"),
        P("head", "seq"),
        P(),
    )
    return jax.shard_map(
        per_device, mesh=mesh, in_specs=in_specs, out_specs=out_specs, check_vma=False
    )
```

profile of v0, /device:TPU:0, one launch (start us, length us, event | category | flops | bytes accessed | tf_op | source)
XLA Modules:
  0.0 3591.4 jit_solution(12637310382889141597)
XLA Ops:
  8.7 33.1 all-gather.9
  49.3 10.6 all-gather.28.cloned.1.call-done
  75.3 31.6 all-gather.8
  110.7 18.8 all-gather.11
  131.4 32.6 all-gather.3
  167.5 16.6 all-gather.10
  186.0 33.2 all-gather.1
  226.3 50.0 %while.67 = (s32[]{:T(128)}, f32[2,4,273,112]{3,2,1,0:T(8,128)}, f32[2,4,273]{2,1,0:T(4,128)}, s32[]{:T(128)}, bf16[8,2,4,273,112]{4,2,3,1,0:T(4,128)(2,1)}, /*i...) while((s32[]{:T(128)}, f32[2,4,273,112]{3,2,1,0:T(8,128)}, ...), condition=%wide.region_15.16_spmd.clone, body=%wide.region_14.15_spmd.clone.sunk | while | flops 1233968 | bytes 3516519 | solution.py:37
  276.3 34.8 while.66
  332.6 43.8 %all-reduce.42.cloned.1.call-done = (bf16[2,128,1792]{2,1,0:T(8,128)(2,1)}, bf16[2,128,1792]{2,1,0:T(8,128)(2,1)}) async-done(((bf16[2,128,1792]{2,1,0:T(8,128)(2,1)}, bf16[2,128,1792]{2,1,0:T(8,128)(2,1)}), (bf16[2,128,1792]{2,1,0:T(8,128)(2,1)}, bf16[2,128,1792]{2,1,0:T(8,128)(2,1)})) %all-reduce.42.cloned.1.call-update) | async-done | bytes 1835024 | tf_op jit(solution)/shard_map/psum | solution.py:166
  381.2 69.9 %all-gather.32.cloned.1.call-done = bf16[1792,1152]{1,0:T(8,128)(2,1)} async-done(((bf16[224,1152]{1,0:T(8,128)(2,1)}), bf16[1792,1152]{1,0:T(8,128)(2,1)}) %all-gather.32.cloned.1.call-update) | async-done | bytes 4128784 | tf_op jit(solution)/shard_map/all_gather | solution.py:179
  451.0 5.0 fusion.72
  458.4 65.7 %all-gather.34.cloned.1.call-done = bf16[1792,1152]{1,0:T(8,128)(2,1)} async-done(((bf16[224,1152]{1,0:T(8,128)(2,1)}), bf16[1792,1152]{1,0:T(8,128)(2,1)}) %all-gather.34.cloned.1.call-update) | async-done | bytes 4128784 | tf_op jit(solution)/shard_map/all_gather | solution.py:180
  524.1 5.5 multiply_convert_fusion.11
  532.2 64.9 %all-gather.36.cloned.1.call-done = bf16[1152,1792]{0,1:T(8,128)(2,1)} async-done(((bf16[1152,224]{0,1:T(8,128)(2,1)}), bf16[1152,1792]{0,1:T(8,128)(2,1)}) %all-gather.36.cloned.1.call-update) | async-done | bytes 4128784 | tf_op jit(solution)/shard_map/all_gather | solution.py:181
  607.9 42.2 %all-reduce.40.cloned.1.call-done = (bf16[2,128,1792]{2,1,0:T(8,128)(2,1)}, bf16[2,128,1792]{2,1,0:T(8,128)(2,1)}) async-done(((bf16[2,128,1792]{2,1,0:T(8,128)(2,1)}, bf16[2,128,1792]{2,1,0:T(8,128)(2,1)}), (bf16[2,128,1792]{2,1,0:T(8,128)(2,1)}, bf16[2,128,1792]{2,1,0:T(8,128)(2,1)})) %all-reduce.40.cloned.1.call-update) | async-done | bytes 1835024 | tf_op jit(solution)/shard_map/psum | solution.py:166
  656.5 42.0 %all-gather.38.cloned.1.call-done = bf16[1792,448]{1,0:T(8,128)(2,1)} async-done(((bf16[224,448]{1,0:T(8,128)(2,1)}), bf16[1792,448]{1,0:T(8,128)(2,1)}) %all-gather.38.cloned.1.call-update) | async-done | bytes 1605648 | tf_op jit(solution)/shard_map/all_gather | solution.py:182
  707.2 4.9 collective-permute-start
  712.1 40.9 %all-gather.40.cloned.1.call-done = bf16[1792,448]{1,0:T(8,128)(2,1)} async-done(((bf16[224,448]{1,0:T(8,128)(2,1)}), bf16[1792,448]{1,0:T(8,128)(2,1)}) %all-gather.40.cloned.1.call-update) | async-done | bytes 1605648 | tf_op jit(solution)/shard_map/all_gather | solution.py:183
  757.5 42.7 %all-gather.42.cloned.1.call-done = bf16[448,1792]{0,1:T(8,128)(2,1)} async-done(((bf16[448,224]{0,1:T(8,128)(2,1)}), bf16[448,1792]{0,1:T(8,128)(2,1)}) %all-gather.42.cloned.1.call-update) | async-done | bytes 1605648 | tf_op jit(solution)/shard_map/all_gather | solution.py:184
  810.9 63.1 %all-gather.48.cloned.1.call-done = bf16[1152,1792]{0,1:T(8,128)(2,1)} async-done(((bf16[1152,224]{0,1:T(8,128)(2,1)}), bf16[1152,1792]{0,1:T(8,128)(2,1)}) %all-gather.48.cloned.1.call-update) | async-done | bytes 4128784 | tf_op jit(solution)/shard_map/all_gather | solution.py:187
  874.0 5.0 fusion.28
  881.4 41.1 %all-reduce.38.cloned.1.call-done = (bf16[2,128,1792]{2,1,0:T(8,128)(2,1)}, bf16[2,128,1792]{2,1,0:T(8,128)(2,1)}) async-done(((bf16[2,128,1792]{2,1,0:T(8,128)(2,1)}, bf16[2,128,1792]{2,1,0:T(8,128)(2,1)}), (bf16[2,128,1792]{2,1,0:T(8,128)(2,1)}, bf16[2,128,1792]{2,1,0:T(8,128)(2,1)})) %all-reduce.38.cloned.1.call-update) | async-done | bytes 1835024 | tf_op jit(solution)/shard_map/psum | solution.py:166
  928.4 68.7 %all-gather.46.cloned.1.call-done = bf16[1792,1152]{1,0:T(8,128)(2,1)} async-done(((bf16[224,1152]{1,0:T(8,128)(2,1)}), bf16[1792,1152]{1,0:T(8,128)(2,1)}) %all-gather.46.cloned.1.call-update) | async-done | bytes 4128784 | tf_op jit(solution)/shard_map/all_gather | solution.py:186
  997.2 5.0 fusion.40
  1004.6 65.5 %all-gather.44.cloned.1.call-done = bf16[1792,1152]{1,0:T(8,128)(2,1)} async-done(((bf16[224,1152]{1,0:T(8,128)(2,1)}), bf16[1792,1152]{1,0:T(8,128)(2,1)}) %all-gather.44.cloned.1.call-update) | async-done | bytes 4128784 | tf_op jit(solution)/shard_map/all_gather | solution.py:185
  1070.1 5.8 fusion.240
  1088.5 45.7 %all-reduce.36.cloned.1.call-done = (bf16[2,128,1792]{2,1,0:T(8,128)(2,1)}, bf16[2,128,1792]{2,1,0:T(8,128)(2,1)}) async-done(((bf16[2,128,1792]{2,1,0:T(8,128)(2,1)}, bf16[2,128,1792]{2,1,0:T(8,128)(2,1)}), (bf16[2,128,1792]{2,1,0:T(8,128)(2,1)}, bf16[2,128,1792]{2,1,0:T(8,128)(2,1)})) %all-reduce.36.cloned.1.call-update) | async-done | bytes 1835024 | tf_op jit(solution)/shard_map/psum | solution.py:170
  1155.5 10.7 collective-permute-done.3
  1166.5 8.3 collective-permute-done.2
  1178.7 47.4 %all-reduce.34.cloned.1.call-done = (bf16[2,128,1792]{2,1,0:T(8,128)(2,1)}, bf16[2,128,1792]{2,1,0:T(8,128)(2,1)}) async-done(((bf16[2,128,1792]{2,1,0:T(8,128)(2,1)}, bf16[2,128,1792]{2,1,0:T(8,128)(2,1)}), (bf16[2,128,1792]{2,1,0:T(8,128)(2,1)}, bf16[2,128,1792]{2,1,0:T(8,128)(2,1)})) %all-reduce.34.cloned.1.call-update) | async-done | bytes 1835024 | tf_op jit(solution)/shard_map/psum | solution.py:170
  1247.9 47.1 %all-reduce.32.cloned.1.call-done = (bf16[2,128,1792]{2,1,0:T(8,128)(2,1)}, bf16[2,128,1792]{2,1,0:T(8,128)(2,1)}) async-done(((bf16[2,128,1792]{2,1,0:T(8,128)(2,1)}, bf16[2,128,1792]{2,1,0:T(8,128)(2,1)}), (bf16[2,128,1792]{2,1,0:T(8,128)(2,1)}, bf16[2,128,1792]{2,1,0:T(8,128)(2,1)})) %all-reduce.32.cloned.1.call-update) | async-done | bytes 1835024 | tf_op jit(solution)/shard_map/psum | solution.py:170
  1404.7 30.9 all-gather.7
  1435.6 30.8 all-gather.5
  1466.5 16.1 while.65
  1487.4 16.1 while.64
  1539.4 4.8 fusion.97
  1565.8 25.4 reduce-scatter.79.cloned.1.call-done
  1592.8 67.0 %reduce-scatter.93.cloned.1.call-done = bf16[224,448]{1,0:T(8,128)(2,1)} async-done(((bf16[1792,448]{1,0:T(8,128)(2,1)}), bf16[224,448]{1,0:T(8,128)(2,1)}) %reduce-scatter.93.cloned.1.call-update) | async-done | bytes 200720
  1660.9 68.1 %reduce-scatter.91.cloned.1.call-done = bf16[224,448]{1,0:T(8,128)(2,1)} async-done(((bf16[1792,448]{1,0:T(8,128)(2,1)}), bf16[224,448]{1,0:T(8,128)(2,1)}) %reduce-scatter.91.cloned.1.call-update) | async-done | bytes 200720
  1730.9 66.9 %reduce-scatter.65.cloned.1.call-done = bf16[224,448]{1,0:T(8,128)(2,1)} async-done(((bf16[1792,448]{1,0:T(8,128)(2,1)}), bf16[224,448]{1,0:T(8,128)(2,1)}) %reduce-scatter.65.cloned.1.call-update) | async-done | bytes 200720 | tf_op jit(solution)/shard_map/reduce_scatter | solution.py:217
  1797.8 68.6 %reduce-scatter.63.cloned.1.call-done = bf16[224,448]{1,0:T(8,128)(2,1)} async-done(((bf16[1792,448]{1,0:T(8,128)(2,1)}), bf16[224,448]{1,0:T(8,128)(2,1)}) %reduce-scatter.63.cloned.1.call-update) | async-done | bytes 200720 | tf_op jit(solution)/shard_map/reduce_scatter | solution.py:217
  1868.3 66.8 %reduce-scatter.61.cloned.1.call-done = bf16[224,448]{1,0:T(8,128)(2,1)} async-done(((bf16[1792,448]{1,0:T(8,128)(2,1)}), bf16[224,448]{1,0:T(8,128)(2,1)}) %reduce-scatter.61.cloned.1.call-update) | async-done | bytes 200720 | tf_op jit(solution)/shard_map/reduce_scatter | solution.py:214
  1935.1 69.2 %reduce-scatter.59.cloned.1.call-done = bf16[224,448]{1,0:T(8,128)(2,1)} async-done(((bf16[1792,448]{1,0:T(8,128)(2,1)}), bf16[224,448]{1,0:T(8,128)(2,1)}) %reduce-scatter.59.cloned.1.call-update) | async-done | bytes 200720 | tf_op jit(solution)/shard_map/reduce_scatter | solution.py:214
  2006.2 67.2 %reduce-scatter.89.cloned.1.call-done = bf16[224,448]{1,0:T(8,128)(2,1)} async-done(((bf16[1792,448]{1,0:T(8,128)(2,1)}), bf16[224,448]{1,0:T(8,128)(2,1)}) %reduce-scatter.89.cloned.1.call-update) | async-done | bytes 200720
  2074.4 67.9 %reduce-scatter.87.cloned.1.call-done = bf16[224,448]{1,0:T(8,128)(2,1)} async-done(((bf16[1792,448]{1,0:T(8,128)(2,1)}), bf16[224,448]{1,0:T(8,128)(2,1)}) %reduce-scatter.87.cloned.1.call-update) | async-done | bytes 200720
  2144.2 88.2 %reduce-scatter.69.cloned.1.call-done = bf16[224,1152]{1,0:T(8,128)(2,1)} async-done(((bf16[1792,1152]{1,0:T(8,128)(2,1)}), bf16[224,1152]{1,0:T(8,128)(2,1)}) %reduce-scatter.69.cloned.1.call-update) | async-done | bytes 516112 | tf_op jit(solution)/shard_map/reduce_scatter | solution.py:223
  2232.4 91.2 %reduce-scatter.67.cloned.1.call-done = bf16[224,1152]{1,0:T(8,128)(2,1)} async-done(((bf16[1792,1152]{1,0:T(8,128)(2,1)}), bf16[224,1152]{1,0:T(8,128)(2,1)}) %reduce-scatter.67.cloned.1.call-update) | async-done | bytes 516112 | tf_op jit(solution)/shard_map/reduce_scatter | solution.py:223
  2325.9 88.8 %reduce-scatter.73.cloned.1.call-done = bf16[224,1152]{1,0:T(8,128)(2,1)} async-done(((bf16[1792,1152]{1,0:T(8,128)(2,1)}), bf16[224,1152]{1,0:T(8,128)(2,1)}) %reduce-scatter.73.cloned.1.call-update) | async-done | bytes 516112 | tf_op jit(solution)/shard_map/reduce_scatter | solution.py:226
  2414.7 91.4 %reduce-scatter.71.cloned.1.call-done = bf16[224,1152]{1,0:T(8,128)(2,1)} async-done(((bf16[1792,1152]{1,0:T(8,128)(2,1)}), bf16[224,1152]{1,0:T(8,128)(2,1)}) %reduce-scatter.71.cloned.1.call-update) | async-done | bytes 516112 | tf_op jit(solution)/shard_map/reduce_scatter | solution.py:226
  2508.4 88.6 %reduce-scatter.77.cloned.1.call-done = bf16[1152,224]{0,1:T(8,128)(2,1)} async-done(((bf16[1152,1792]{0,1:T(8,128)(2,1)}), bf16[1152,224]{0,1:T(8,128)(2,1)}) %reduce-scatter.77.cloned.1.call-update) | async-done | bytes 516112 | tf_op jit(solution)/shard_map/reduce_scatter | solution.py:229
  2596.9 91.3 %reduce-scatter.75.cloned.1.call-done = bf16[1152,224]{0,1:T(8,128)(2,1)} async-done(((bf16[1152,1792]{0,1:T(8,128)(2,1)}), bf16[1152,224]{0,1:T(8,128)(2,1)}) %reduce-scatter.75.cloned.1.call-update) | async-done | bytes 516112 | tf_op jit(solution)/shard_map/reduce_scatter | solution.py:229
  2692.6 61.0 %reduce-scatter.85.cloned.1.call-done = bf16[224,64]{1,0:T(8,128)(2,1)} async-done(((bf16[1792,64]{1,0:T(8,128)(2,1)}), bf16[224,64]{1,0:T(8,128)(2,1)}) %reduce-scatter.85.cloned.1.call-update) | async-done | bytes 28688
  2754.6 64.0 %reduce-scatter.83.cloned.1.call-done = bf16[224,64]{1,0:T(8,128)(2,1)} async-done(((bf16[1792,64]{1,0:T(8,128)(2,1)}), bf16[224,64]{1,0:T(8,128)(2,1)}) %reduce-scatter.83.cloned.1.call-update) | async-done | bytes 28688
  2820.1 88.7 %reduce-scatter.49.cloned.1.call-done = bf16[224,1152]{1,0:T(8,128)(2,1)} async-done(((bf16[1792,1152]{1,0:T(8,128)(2,1)}), bf16[224,1152]{1,0:T(8,128)(2,1)}) %reduce-scatter.49.cloned.1.call-update) | async-done | bytes 516112 | tf_op jit(solution)/shard_map/reduce_scatter | solution.py:205
  2908.9 91.4 %reduce-scatter.47.cloned.1.call-done = bf16[224,1152]{1,0:T(8,128)(2,1)} async-done(((bf16[1792,1152]{1,0:T(8,128)(2,1)}), bf16[224,1152]{1,0:T(8,128)(2,1)}) %reduce-scatter.47.cloned.1.call-update) | async-done | bytes 516112 | tf_op jit(solution)/shard_map/reduce_scatter | solution.py:205
  3002.5 88.7 %reduce-scatter.53.cloned.1.call-done = bf16[224,1152]{1,0:T(8,128)(2,1)} async-done(((bf16[1792,1152]{1,0:T(8,128)(2,1)}), bf16[224,1152]{1,0:T(8,128)(2,1)}) %reduce-scatter.53.cloned.1.call-update) | async-done | bytes 516112 | tf_op jit(solution)/shard_map/reduce_scatter | solution.py:208
  3091.2 91.3 %reduce-scatter.51.cloned.1.call-done = bf16[224,1152]{1,0:T(8,128)(2,1)} async-done(((bf16[1792,1152]{1,0:T(8,128)(2,1)}), bf16[224,1152]{1,0:T(8,128)(2,1)}) %reduce-scatter.51.cloned.1.call-update) | async-done | bytes 516112 | tf_op jit(solution)/shard_map/reduce_scatter | solution.py:208
  3184.7 88.7 %reduce-scatter.57.cloned.1.call-done = bf16[1152,224]{0,1:T(8,128)(2,1)} async-done(((bf16[1152,1792]{0,1:T(8,128)(2,1)}), bf16[1152,224]{0,1:T(8,128)(2,1)}) %reduce-scatter.57.cloned.1.call-update) | async-done | bytes 516112 | tf_op jit(solution)/shard_map/reduce_scatter | solution.py:211
  3273.4 91.3 %reduce-scatter.55.cloned.1.call-done = bf16[1152,224]{0,1:T(8,128)(2,1)} async-done(((bf16[1152,1792]{0,1:T(8,128)(2,1)}), bf16[1152,224]{0,1:T(8,128)(2,1)}) %reduce-scatter.55.cloned.1.call-update) | async-done | bytes 516112 | tf_op jit(solution)/shard_map/reduce_scatter | solution.py:211
  3367.0 77.5 %all-reduce.30.cloned.1.call-done = (bf16[2,128,1792]{2,1,0:T(8,128)(2,1)}, bf16[2,128,1792]{2,1,0:T(8,128)(2,1)}, bf16[2,128,1792]{2,1,0:T(8,128)(2,1)}, bf16[2,128,1792]{2,1,0:T(8,128)(2,1)}) async-done(((bf16[2,128,1792]{2,1,0:T(8,128)(2,1)}, bf16[2,128,1792]{2,1,0:T(8,128)(2,1)}, bf16[2,128,1792]{2,1,0:T(8,128)(2,1)}, bf16[2,128,1792]{2,1,0:T(8,128)(2,1)}), (bf16[2,128,1792]{2,1,0:T(8,128)(2,1)}, ...) | async-done | bytes 3670032 | tf_op jit(solution)/shard_map/psum | solution.py:166
  3447.6 37.2 %all-reduce.14 = (bf16[3,448]{1,0:T(4,128)(2,1)S(1)}, bf16[4,1792]{1,0:T(4,128)(2,1)S(1)}) all-reduce(bf16[3,448]{1,0:T(4,128)(2,1)S(1)} %add_convert_fusion.2, bf16[4,1792]{1,0:T(4,128)(2,1)S(1)} %fusion.324), channel_id=1, replica_groups=mesh['seq'=8,'head'=4] {'seq'}, use_global_device_ids=true, to_apply=%region_80.81 | all-reduce | flops 8512 | bytes 34048 | tf_op jit(solution)/shard_map/psum | solution.py:505
  3494.9 19.0 reduce-scatter.45.cloned.1.call-done
  3513.9 68.9 %reduce-scatter.43.cloned.1.call-done = bf16[224,448]{1,0:T(8,128)(2,1)} async-done(((bf16[1792,448]{1,0:T(8,128)(2,1)}), bf16[224,448]{1,0:T(8,128)(2,1)}) %reduce-scatter.43.cloned.1.call-update) | async-done | bytes 200720 | tf_op jit(solution)/shard_map/reduce_scatter | solution.py:199
  (1081 shorter events, 515.3 us)
Async XLA Ops:
  7.2 52.6 %all-gather.28.cloned.1.call-start = ((), (), s32[]{:S(2)}) async-start(), calls=%async_computation.26 | async-start | bytes 2064384 | tf_op jit(solution)/shard_map/all_gather | solution.py:177
  7.9 218.3 %all-gather.52.cloned.1.call-start = ((), (), s32[]{:S(2)}) async-start(), calls=%async_computation.56 | async-start | bytes 5031936 | tf_op jit(solution)/shard_map/all_gather | solution.py:20
  44.8 63.7 %copy-start.172 = (f32[1792]{0:T(1024)}, f32[1792]{0:T(1024)S(1)}, u32[]{:S(2)}) copy-start(f32[1792]{0:T(1024)S(1)} %get-tuple-element.674) | copy-start | bytes 21508
  46.7 60.6 %copy-start.223 = (f32[2,128]{1,0:T(2,128)}, f32[2,128]{1,0:T(2,128)S(1)}, u32[]{:S(2)}) copy-start(f32[2,128]{1,0:T(2,128)S(1)} %get-tuple-element.860) | copy-start | bytes 3076
  46.7 61.7 %copy-start.221 = (f32[2,128]{1,0:T(2,128)}, f32[2,128]{1,0:T(2,128)S(1)}, u32[]{:S(2)}) copy-start(f32[2,128]{1,0:T(2,128)S(1)} %get-tuple-element.859) | copy-start | bytes 3076
  62.2 161.5 %copy-start.81 = (bf16[2,128,448]{1,2,0:T(8,128)(2,1)}, bf16[2,128,448]{1,2,0:T(8,128)(2,1)S(1)}, u32[]{:S(2)}) copy-start(bf16[2,128,448]{1,2,0:T(8,128)(2,1)S(1)} %fusion.229) | copy-start | bytes 688132
  64.4 211.8 %all-gather.50.cloned.1.call-start = ((), (), s32[]{:S(2)}) async-start(), calls=%async_computation.55 | async-start | bytes 5031936 | tf_op jit(solution)/shard_map/all_gather | solution.py:20
  67.0 158.1 %copy-start.78 = (bf16[2,128,448]{1,2,0:T(8,128)(2,1)}, bf16[2,128,448]{1,2,0:T(8,128)(2,1)S(1)}, u32[]{:S(2)}) copy-start(bf16[2,128,448]{1,2,0:T(8,128)(2,1)S(1)} %fusion.226) | copy-start | bytes 688132
  69.2 256.1 %all-gather.30.cloned.1.call-start = ((), (), s32[]{:S(2)}) async-start(), calls=%async_computation.27 | async-start | bytes 2064384 | tf_op jit(solution)/shard_map/all_gather | solution.py:178
  71.0 305.3 %all-reduce.42.cloned.1.call-start = ((), (), s32[]{:S(2)}) async-start(), calls=%async_computation.73 | async-start | bytes 3670016 | tf_op jit(solution)/shard_map/psum | solution.py:166
  109.0 113.8 %copy-start.110 = (f32[2,128,4,16]{1,3,2,0:T(8,128)}, f32[2,128,4,16]{1,3,2,0:T(8,128)S(1)}, u32[]{:S(2)}) copy-start(f32[2,128,4,16]{1,3,2,0:T(8,128)S(1)} %get-tuple-element.843) | copy-start | bytes 196612
  109.0 113.8 %copy-start.164 = (bf16[2,128,64]{1,2,0:T(8,128)(2,1)}, bf16[2,128,64]{1,2,0:T(8,128)(2,1)S(1)}, u32[]{:S(2)}) copy-start(bf16[2,128,64]{1,2,0:T(8,128)(2,1)S(1)} %get-tuple-element.844) | copy-start | bytes 98308
  330.2 120.8 %all-gather.32.cloned.1.call-start = ((), (), s32[]{:S(2)}) async-start(), calls=%async_computation.28 | async-start | bytes 4644864 | tf_op jit(solution)/shard_map/all_gather | solution.py:179
  330.8 193.3 %all-gather.34.cloned.1.call-start = ((), (), s32[]{:S(2)}) async-start(), calls=%async_computation.29 | async-start | bytes 4644864 | tf_op jit(solution)/shard_map/all_gather | solution.py:180
  331.6 265.6 %all-gather.36.cloned.1.call-start = ((), (), s32[]{:S(2)}) async-start(), calls=%async_computation.30 | async-start | bytes 4644864 | tf_op jit(solution)/shard_map/all_gather | solution.py:181
  332.3 317.8 %all-reduce.40.cloned.1.call-start = ((), (), s32[]{:S(2)}) async-start(), calls=%async_computation.72 | async-start | bytes 3670016 | tf_op jit(solution)/shard_map/psum | solution.py:166
  604.3 94.1 %all-gather.38.cloned.1.call-start = ((), (), s32[]{:S(2)}) async-start(), calls=%async_computation.31 | async-start | bytes 2064384 | tf_op jit(solution)/shard_map/all_gather | solution.py:182
  604.9 148.1 %all-gather.40.cloned.1.call-start = ((), (), s32[]{:S(2)}) async-start(), calls=%async_computation.32 | async-start | bytes 2064384 | tf_op jit(solution)/shard_map/all_gather | solution.py:183
  605.6 194.6 %all-gather.42.cloned.1.call-start = ((), (), s32[]{:S(2)}) async-start(), calls=%async_computation.33 | async-start | bytes 2064384 | tf_op jit(solution)/shard_map/all_gather | solution.py:184
  606.5 267.5 %all-gather.48.cloned.1.call-start = ((), (), s32[]{:S(2)}) async-start(), calls=%async_computation.36 | async-start | bytes 4644864 | tf_op jit(solution)/shard_map/all_gather | solution.py:187
  607.3 315.2 %all-reduce.38.cloned.1.call-start = ((), (), s32[]{:S(2)}) async-start(), calls=%async_computation.71 | async-start | bytes 3670016 | tf_op jit(solution)/shard_map/psum | solution.py:166
  607.9 195.7 %copy-start.176 = (f32[1,448]{1,0:T(1,128)}, f32[1,448]{1,0:T(1,128)S(1)}, u32[]{:S(2)}) copy-start(f32[1,448]{1,0:T(1,128)S(1)} %get-tuple-element.814) | copy-start | bytes 5380
  607.9 195.7 %copy-start.178 = (f32[1,448]{1,0:T(1,128)}, f32[1,448]{1,0:T(1,128)S(1)}, u32[]{:S(2)}) copy-start(f32[1,448]{1,0:T(1,128)S(1)} %get-tuple-element.815) | copy-start | bytes 5380
  702.2 50.9 %collective-permute-start.1 = (f32[2,2,448]{1,2,0:T(8,128)}, f32[2,2,448]{1,2,0:T(8,128)}, u32[]{:S(2)}, u32[]{:S(2)}) collective-permute-start(f32[2,2,448]{1,2,0:T(8,128)} %slice.143), channel_id=1, source_target_pairs={{0,4},{4,8},{8,12},{12,16},{16,20},{20,24},{24,28},{1,5},{5,9},{9,... | collective-permute-start | bytes 21512 | tf_op jit(solution)/shard_map/ppermute | solution.py:43
  707.2 96.4 %collective-permute-start = (f32[2,2,448]{1,2,0:T(8,128)}, f32[2,2,448]{1,2,0:T(8,128)}, u32[]{:S(2)}, u32[]{:S(2)}) collective-permute-start(f32[2,2,448]{1,2,0:T(8,128)} %slice.138), channel_id=1, source_target_pairs={{0,4},{4,8},{8,12},{12,16},{16,20},{20,24},{24,28},{1,5},{5,9},{9,... | collective-permute-start | bytes 21512 | tf_op jit(solution)/shard_map/ppermute | solution.py:43
  809.3 187.8 %all-gather.46.cloned.1.call-start = ((), (), s32[]{:S(2)}) async-start(), calls=%async_computation.35 | async-start | bytes 4644864 | tf_op jit(solution)/shard_map/all_gather | solution.py:186
  809.9 260.2 %all-gather.44.cloned.1.call-start = ((), (), s32[]{:S(2)}) async-start(), calls=%async_computation.34 | async-start | bytes 4644864 | tf_op jit(solution)/shard_map/all_gather | solution.py:185
  810.5 323.7 %all-reduce.36.cloned.1.call-start = ((), (), s32[]{:S(2)}) async-start(), calls=%async_computation.70 | async-start | bytes 3670016 | tf_op jit(solution)/shard_map/psum | solution.py:170
  1088.5 137.6 %all-reduce.34.cloned.1.call-start = ((), (), s32[]{:S(2)}) async-start(), calls=%async_computation.69 | async-start | bytes 3670016 | tf_op jit(solution)/shard_map/psum | solution.py:170
  1150.7 15.4 collective-permute-start.3
  1152.7 22.0 collective-permute-start.2
  1178.4 47.7 %copy-start.198 = (f32[2,128]{1,0:T(2,128)S(1)}, f32[2,128]{1,0:T(2,128)}, u32[]{:S(2)}) copy-start(f32[2,128]{1,0:T(2,128)} %copy-done.197) | copy-start | bytes 3076
  1178.4 47.7 %copy-start.200 = (f32[2,128]{1,0:T(2,128)S(1)}, f32[2,128]{1,0:T(2,128)}, u32[]{:S(2)}) copy-start(f32[2,128]{1,0:T(2,128)} %copy-done.199) | copy-start | bytes 3076
  1178.4 116.5 %all-reduce.32.cloned.1.call-start = ((), (), s32[]{:S(2)}) async-start(), calls=%async_computation.68 | async-start | bytes 3670016 | tf_op jit(solution)/shard_map/psum | solution.py:170
  1247.4 47.6 %copy-start.204 = (f32[2,128]{1,0:T(2,128)S(1)}, f32[2,128]{1,0:T(2,128)}, u32[]{:S(2)}) copy-start(f32[2,128]{1,0:T(2,128)} %copy-done.203) | copy-start | bytes 3076
  1247.4 219.0 %all-gather.56.cloned.1.call-start = ((), (), s32[]{:S(2)}) async-start(), calls=%async_computation.58 | async-start | bytes 5031936 | tf_op jit(solution)/shard_map/all_gather | solution.py:51
  1306.8 180.4 %all-gather.54.cloned.1.call-start = ((), (), s32[]{:S(2)}) async-start(), calls=%async_computation.57 | async-start | bytes 5031936 | tf_op jit(solution)/shard_map/all_gather | solution.py:51
  1316.7 248.3 %reduce-scatter.81.cloned.1.call-start = ((), (), s32[]{:S(2)}) async-start(), calls=%async_computation.60 | async-start | bytes 516096
  1333.5 257.7 %reduce-scatter.79.cloned.1.call-start = ((), (), s32[]{:S(2)}) async-start(), calls=%async_computation.59 | async-start | bytes 516096
  1336.4 323.4 %reduce-scatter.93.cloned.1.call-start = ((), (), s32[]{:S(2)}) async-start(), calls=%async_computation.66 | async-start | bytes 2064384
  1341.0 388.0 %reduce-scatter.91.cloned.1.call-start = ((), (), s32[]{:S(2)}) async-start(), calls=%async_computation.65 | async-start | bytes 2064384
  1346.1 451.6 %reduce-scatter.65.cloned.1.call-start = ((), (), s32[]{:S(2)}) async-start(), calls=%async_computation.48 | async-start | bytes 2064384 | tf_op jit(solution)/shard_map/reduce_scatter | solution.py:217
  1350.2 516.2 %reduce-scatter.63.cloned.1.call-start = ((), (), s32[]{:S(2)}) async-start(), calls=%async_computation.47 | async-start | bytes 2064384 | tf_op jit(solution)/shard_map/reduce_scatter | solution.py:217
  1352.2 582.9 %reduce-scatter.61.cloned.1.call-start = ((), (), s32[]{:S(2)}) async-start(), calls=%async_computation.46 | async-start | bytes 2064384 | tf_op jit(solution)/shard_map/reduce_scatter | solution.py:214
  1355.8 648.5 %reduce-scatter.59.cloned.1.call-start = ((), (), s32[]{:S(2)}) async-start(), calls=%async_computation.45 | async-start | bytes 2064384 | tf_op jit(solution)/shard_map/reduce_scatter | solution.py:214
  1357.9 715.4 %reduce-scatter.89.cloned.1.call-start = ((), (), s32[]{:S(2)}) async-start(), calls=%async_computation.64 | async-start | bytes 2064384
  1362.5 779.8 %reduce-scatter.87.cloned.1.call-start = ((), (), s32[]{:S(2)}) async-start(), calls=%async_computation.63 | async-start | bytes 2064384
  1370.6 861.9 %reduce-scatter.69.cloned.1.call-start = ((), (), s32[]{:S(2)}) async-start(), calls=%async_computation.50 | async-start | bytes 4644864 | tf_op jit(solution)/shard_map/reduce_scatter | solution.py:223
  1374.0 949.7 %reduce-scatter.67.cloned.1.call-start = ((), (), s32[]{:S(2)}) async-start(), calls=%async_computation.49 | async-start | bytes 4644864 | tf_op jit(solution)/shard_map/reduce_scatter | solution.py:223
  1378.7 1036.0 %reduce-scatter.73.cloned.1.call-start = ((), (), s32[]{:S(2)}) async-start(), calls=%async_computation.52 | async-start | bytes 4644864 | tf_op jit(solution)/shard_map/reduce_scatter | solution.py:226
  1384.2 1121.8 %reduce-scatter.71.cloned.1.call-start = ((), (), s32[]{:S(2)}) async-start(), calls=%async_computation.51 | async-start | bytes 4644864 | tf_op jit(solution)/shard_map/reduce_scatter | solution.py:226
  1388.7 1208.2 %reduce-scatter.77.cloned.1.call-start = ((), (), s32[]{:S(2)}) async-start(), calls=%async_computation.54 | async-start | bytes 4644864 | tf_op jit(solution)/shard_map/reduce_scatter | solution.py:229
  1394.3 1293.9 %reduce-scatter.75.cloned.1.call-start = ((), (), s32[]{:S(2)}) async-start(), calls=%async_computation.53 | async-start | bytes 4644864 | tf_op jit(solution)/shard_map/reduce_scatter | solution.py:229
  1399.8 1353.8 %reduce-scatter.85.cloned.1.call-start = ((), (), s32[]{:S(2)}) async-start(), calls=%async_computation.62 | async-start | bytes 516096
  1506.7 1311.9 %reduce-scatter.83.cloned.1.call-start = ((), (), s32[]{:S(2)}) async-start(), calls=%async_computation.61 | async-start | bytes 516096
  1510.4 1398.5 %reduce-scatter.49.cloned.1.call-start = ((), (), s32[]{:S(2)}) async-start(), calls=%async_computation.40 | async-start | bytes 4644864 | tf_op jit(solution)/shard_map/reduce_scatter | solution.py:205
  1515.1 1485.1 %reduce-scatter.47.cloned.1.call-start = ((), (), s32[]{:S(2)}) async-start(), calls=%async_computation.39 | async-start | bytes 4644864 | tf_op jit(solution)/shard_map/reduce_scatter | solution.py:205
  1519.9 1571.3 %reduce-scatter.53.cloned.1.call-start = ((), (), s32[]{:S(2)}) async-start(), calls=%async_computation.42 | async-start | bytes 4644864 | tf_op jit(solution)/shard_map/reduce_scatter | solution.py:208
  1524.7 1657.8 %reduce-scatter.51.cloned.1.call-start = ((), (), s32[]{:S(2)}) async-start(), calls=%async_computation.41 | async-start | bytes 4644864 | tf_op jit(solution)/shard_map/reduce_scatter | solution.py:208
  1529.4 1744.0 %reduce-scatter.57.cloned.1.call-start = ((), (), s32[]{:S(2)}) async-start(), calls=%async_computation.44 | async-start | bytes 4644864 | tf_op jit(solution)/shard_map/reduce_scatter | solution.py:211
  1534.2 1830.5 %reduce-scatter.55.cloned.1.call-start = ((), (), s32[]{:S(2)}) async-start(), calls=%async_computation.43 | async-start | bytes 4644864 | tf_op jit(solution)/shard_map/reduce_scatter | solution.py:211
  1539.0 1905.5 %all-reduce.30.cloned.1.call-start = ((), (), s32[]{:S(2)}) async-start(), calls=%async_computation.67 | async-start | bytes 7340032 | tf_op jit(solution)/shard_map/psum | solution.py:166
  1561.8 1952.1 %reduce-scatter.45.cloned.1.call-start = ((), (), s32[]{:S(2)}) async-start(), calls=%async_computation.38 | async-start | bytes 2064384 | tf_op jit(solution)/shard_map/reduce_scatter | solution.py:199
  1564.7 2018.1 %reduce-scatter.43.cloned.1.call-start = ((), (), s32[]{:S(2)}) async-start(), calls=%async_computation.37 | async-start | bytes 2064384 | tf_op jit(solution)/shard_map/reduce_scatter | solution.py:199
  (288 other events, 1360.7 us)
Sparse Core Ops, SparseCore 0:
  10.2 49.5 all-gather.27
  64.6 78.3 all-gather.51
  145.7 76.2 all-gather.49
  224.6 44.4 all-gather.29
  330.4 45.9 all-reduce.41
  378.4 72.5 all-gather.31
  453.2 70.8 all-gather.33
  526.3 70.8 all-gather.35
  604.4 45.6 all-reduce.39
  652.1 46.2 all-gather.37
  700.6 52.3 all-gather.39
  755.7 44.5 all-gather.41
  802.4 71.5 all-gather.47
  876.8 45.6 all-reduce.37
  924.5 72.5 all-gather.45
  999.2 70.8 all-gather.43
  1088.6 45.6 all-reduce.35
  1178.5 47.4 all-reduce.33
  1247.5 47.3 all-reduce.31
  1306.9 76.8 all-gather.55
  1386.1 76.1 all-gather.53
  1466.1 60.0 reduce-scatter.80
  1530.5 60.7 reduce-scatter.78
  1594.6 65.2 reduce-scatter.92
  1663.7 65.2 reduce-scatter.90
  1732.3 65.3 reduce-scatter.64
  1801.5 64.8 reduce-scatter.62
  1869.9 65.1 reduce-scatter.60
  1939.0 65.2 reduce-scatter.58
  2008.2 65.1 reduce-scatter.88
  2077.2 65.0 reduce-scatter.86
  2145.9 86.4 reduce-scatter.68
  2236.3 87.3 reduce-scatter.66
  2327.2 87.4 reduce-scatter.72
  2418.7 87.3 reduce-scatter.70
  2509.5 87.3 reduce-scatter.76
  2600.8 87.3 reduce-scatter.74
  2692.1 61.5 reduce-scatter.84
  2757.7 60.8 reduce-scatter.82
  2822.1 86.6 reduce-scatter.48
  2912.8 87.3 reduce-scatter.46
  3003.8 87.3 reduce-scatter.52
  3095.1 87.3 reduce-scatter.50
  3186.1 87.3 reduce-scatter.56
  3277.3 87.3 reduce-scatter.54
  3367.1 77.2 all-reduce.29
  3447.7 66.1 reduce-scatter.44
  3517.6 65.1 reduce-scatter.42
where the time goes:
time: 3600 us; the launch traced here: 3590 us
  waiting for transfers between devices  2760 us (77%)
  blocking collectives  265 us (7%)
  matrix products  238 us (7%)
  other arithmetic  176 us (5%)
  local copies, waits for them, and re-layouts  115 us (3%)
    unnamed x56, waiting for transfers between devices  427 us
    psum x4, waiting for transfers between devices, head_total(): lax.psum(partial_sum.astype(jnp.bfloat16), 'head').astype(jnp.float32)  204 us
    reduce_scatter x2, waiting for transfers between devices, scatter_grads(): lax.psum_scatter(grads[11].astype(jnp.bfloat16), 'seq', scatter_dimension...  180 us
    reduce_scatter x2, waiting for transfers between devices, scatter_grads(): lax.psum_scatter(grads[4].astype(jnp.bfloat16), 'seq', scatter_dimension=...  180 us
    reduce_scatter x2, waiting for transfers between devices, scatter_grads(): lax.psum_scatter(grads[5].astype(jnp.bfloat16), 'seq', scatter_dimension=...  180 us
    reduce_scatter x2, waiting for transfers between devices, scatter_grads(): lax.psum_scatter(grads[6].astype(jnp.bfloat16), 'seq', scatter_dimension=...  180 us
    reduce_scatter x2, waiting for transfers between devices, scatter_grads(): lax.psum_scatter(grads[12].astype(jnp.bfloat16), 'seq', scatter_dimension...  180 us
    reduce_scatter x2, waiting for transfers between devices, scatter_grads(): lax.psum_scatter(grads[10].astype(jnp.bfloat16), 'seq', scatter_dimension...  179 us
  transfers between devices with their start and end apart: 52, of which 44 were waited for; matrix products, arithmetic and copies ran while one was open for 11% of the time, Pallas kernels for 0%

commit v1 on v0

v1 whole, which is shorter than its diff:
```python
from functools import partial

import jax
import jax.numpy as jnp
from jax import lax
from jax.experimental import pallas as pl
from jax.experimental.pallas import tpu as pltpu
from jax.sharding import PartitionSpec as P

QK = 16
VH = 112
EPSILON = 1e-05
BF = jnp.bfloat16
F32 = jnp.float32


def ring_order(n):
    if n % 4:
        return list(range(n))
    inner = n // 4
    if inner == 2:
        return [0, 2, 4, 6, 7, 5, 3, 1]
    return list(range(n))


class Ring:
    def __init__(self, n):
        self.n = n
        self.hops = n <= 8
        self.order = ring_order(n)
        place = [0] * n
        for position, device in enumerate(self.order):
            place[device] = position
        self.place = place
        self.pos = jnp.asarray(place, jnp.int32)[lax.axis_index("seq")] if self.hops else jnp.int32(0)

    def hop(self, block, step):
        n = self.n
        route = [(self.order[i], self.order[(i + step) % n]) for i in range(n)]
        return lax.ppermute(block, "seq", route)

    def owners(self):
        return jnp.asarray(self.order, jnp.int32)[(self.pos + jnp.arange(self.n)) % self.n]

    def to_relative(self, x):
        if not self.hops:
            return x
        width = x.shape[-1] // self.n
        parts = [x[..., b * width : (b + 1) * width] for b in self.order]
        twice = jnp.concatenate(parts + parts, axis=-1)
        return lax.dynamic_slice_in_dim(twice, self.pos * width, x.shape[-1], axis=x.ndim - 1)

    def from_relative(self, x):
        if not self.hops:
            return x
        width = x.shape[-1] // self.n
        twice = jnp.concatenate([x, x], axis=-1)
        start = ((self.n - self.pos) % self.n) * width
        ring = lax.dynamic_slice_in_dim(twice, start, x.shape[-1], axis=x.ndim - 1)
        parts = [ring[..., p * width : (p + 1) * width] for p in self.place]
        return jnp.concatenate(parts, axis=-1)

    def gather(self, arrays, after=None):
        n = self.n
        if not self.hops:
            whole = [lax.all_gather(a, "seq") for a in arrays]
            return [[w[k] for k in range(n)] for w in whole], None
        right = list(arrays)
        left = list(arrays)
        if after is not None:
            ties_r, ties_l = after
            for j in range(len(arrays)):
                right[j], _ = lax.optimization_barrier((arrays[j], ties_r[j % len(ties_r)]))
                left[j], _ = lax.optimization_barrier((arrays[j], ties_l[j % len(ties_l)]))
        blocks = [{0: a} for a in arrays]
        both = (n - 1) // 2
        for k in range(1, both + 1):
            for j in range(len(arrays)):
                right[j] = self.hop(right[j], 1)
                left[j] = self.hop(left[j], -1)
                blocks[j][n - k] = right[j]
                blocks[j][k] = left[j]
        ties = (list(right), list(left))
        if n % 2 == 0:
            for j in range(len(arrays)):
                blocks[j][n // 2] = self.hop(right[j], 1) if j % 2 == 0 else self.hop(left[j], -1)
        return [[b[k] for k in range(n)] for b in blocks], ties

    def scatter(self, full, flip):
        n = self.n
        height = full.shape[0] // n
        if not self.hops:
            return lax.psum_scatter(full, "seq", scatter_dimension=0, tiled=True).astype(F32)

        def term(k):
            return full[k * height : (k + 1) * height]

        direction = -1 if flip else 1
        long_hops, short_hops = n // 2, (n - 1) // 2
        total = term(0).astype(F32)
        for d, hops in ((direction, long_hops), (-direction, short_hops)):
            if hops == 0:
                continue
            acc = term((d * hops) % n)
            for k in range(hops - 1, -1, -1):
                acc = self.hop(acc, d)
                if k:
                    acc = (acc.astype(F32) + term((d * k) % n).astype(F32)).astype(BF)
            total = total + acc.astype(F32)
        return total


def dot(a, b, ca, cb):
    return lax.dot_general(a, b, (((ca,), (cb,)), ((), ())), preferred_element_type=F32)


def head_masks(query_width, value_width):
    lane_q = lax.broadcasted_iota(jnp.int32, (1, query_width), 1)
    lane_v = lax.broadcasted_iota(jnp.int32, (1, value_width), 1)
    heads = query_width // QK
    return [
        (
            (lane_q >= h * QK) & (lane_q < (h + 1) * QK),
            (lane_v >= h * VH) & (lane_v < (h + 1) * VH),
        )
        for h in range(heads)
    ]


def query_mask(scal_ref, place_ref, tok):
    offset = scal_ref[1 + pl.program_id(0)]
    pos = scal_ref[0] + lax.broadcasted_iota(jnp.int32, (tok, 1), 0)
    low = jnp.where(pos >= offset, offset, 0)
    other = place_ref[...]
    return (other >= low) & (other <= pos)


def key_mask(scal_ref, place_ref, tok):
    offset = scal_ref[1 + pl.program_id(0)]
    pos = scal_ref[0] + lax.broadcasted_iota(jnp.int32, (tok, 1), 0)
    high = jnp.where(pos >= offset, jnp.int32(1 << 30), offset)
    other = place_ref[...]
    return (other >= pos) & (other < high)


def attend_kernel(scal_ref, place_ref, q_ref, k_ref, v_ref, out_ref):
    q, k, v = q_ref[0], k_ref[0], v_ref[0]
    mask = query_mask(scal_ref, place_ref, q.shape[0])
    total = jnp.zeros((q.shape[0], v.shape[1]), F32)
    for in_q, in_v in head_masks(q.shape[1], v.shape[1]):
        s = dot(jnp.where(in_q, q, jnp.zeros_like(q)), k, 1, 1) * (QK**-0.5)
        w = jnp.where(mask, 1.0 + s + 0.5 * s * s, 0.0)
        den = jnp.sum(w, axis=1, keepdims=True)
        total = total + jnp.where(in_v, dot(w.astype(BF), v, 1, 0) / den, 0.0)
    out_ref[0] = total.astype(BF)


def query_back_kernel(scal_ref, place_ref, q_ref, k_ref, v_ref, da_ref, dq_ref, dan_ref, extra_ref):
    q, k, v = q_ref[0], k_ref[0], v_ref[0]
    da = da_ref[0]
    tok = q.shape[0]
    mask = query_mask(scal_ref, place_ref, tok)
    lane = lax.broadcasted_iota(jnp.int32, (1, q.shape[1]), 1)
    heads = q.shape[1] // QK
    dq = jnp.zeros(q.shape, F32)
    dan_all = jnp.zeros(da.shape, F32)
    extra = jnp.zeros(q.shape, F32)
    for h, (in_q, in_v) in enumerate(head_masks(q.shape[1], v.shape[1])):
        s = dot(jnp.where(in_q, q, jnp.zeros_like(q)), k, 1, 1) * (QK**-0.5)
        w = jnp.where(mask, 1.0 + s + 0.5 * s * s, 0.0)
        den = jnp.sum(w, axis=1, keepdims=True)
        att = dot(w.astype(BF), v, 1, 0) / den
        dan = jnp.where(in_v, da / den, 0.0).astype(BF)
        dan_f = dan.astype(F32)
        delta = jnp.sum(dan_f * att, axis=1, keepdims=True)
        d_kernel = dot(dan, v, 1, 1) - delta
        ds = jnp.where(mask, d_kernel * (1.0 + s), 0.0).astype(BF)
        dq = dq + jnp.where(in_q, dot(ds, k, 1, 0) * (QK**-0.5), 0.0)
        dan_all = dan_all + dan_f
        high = delta.astype(BF).astype(F32)
        extra = extra + jnp.where(lane == h, high, 0.0)
        extra = extra + jnp.where(lane == heads + h, delta - high, 0.0)
    dq_ref[0] = dq.astype(BF)
    dan_ref[0] = dan_all.astype(BF)
    extra_ref[0] = extra.astype(BF)


def key_back_kernel(scal_ref, place_ref, k_ref, v_ref, q_ref, dan_ref, extra_ref, dk_ref, dv_ref):
    k, v = k_ref[0], v_ref[0]
    q, dan, extra = q_ref[0], dan_ref[0], extra_ref[0]
    tok = k.shape[0]
    mask = key_mask(scal_ref, place_ref, tok)
    lane = lax.broadcasted_iota(jnp.int32, (tok, k.shape[1]), 1)
    heads = k.shape[1] // QK
    dk = jnp.zeros(k.shape, F32)
    dv = jnp.zeros(v.shape, F32)
    for h, (in_q, in_v) in enumerate(head_masks(k.shape[1], v.shape[1])):
        s = dot(jnp.where(in_q, k, jnp.zeros_like(k)), q, 1, 1) * (QK**-0.5)
        w = jnp.where(mask, 1.0 + s + 0.5 * s * s, 0.0).astype(BF)
        dv = dv + jnp.where(in_v, dot(w, dan, 1, 0), 0.0)
        pick = jnp.where((lane == h) | (lane == heads + h), 1.0, 0.0).astype(BF)
        d_kernel = dot(jnp.where(in_v, v, jnp.zeros_like(v)), dan, 1, 1) - dot(pick, extra, 1, 1)
        ds = jnp.where(mask, d_kernel * (1.0 + s), 0.0).astype(BF)
        dk = dk + jnp.where(in_q, dot(ds, q, 1, 0) * (QK**-0.5), 0.0)
    dk_ref[0] = dk.astype(BF)
    dv_ref[0] = dv.astype(BF)


def by_rows(kernel, scal, place, operands, widths, kinds):
    rows = operands[0].shape[0]
    tok = operands[0].shape[1]
    specs = [
        pl.BlockSpec(memory_space=pltpu.SMEM),
        pl.BlockSpec(place.shape, lambda r: (0, 0)),
    ]
    specs += [pl.BlockSpec((1,) + a.shape[1:], lambda r: (r, 0, 0)) for a in operands]
    return pl.pallas_call(
        kernel,
        grid=(rows,),
        in_specs=specs,
        out_specs=[pl.BlockSpec((1, tok, w), lambda r: (r, 0, 0)) for w in widths],
        out_shape=[jax.ShapeDtypeStruct((rows, tok, w), t) for w, t in zip(widths, kinds)],
        compiler_params=pltpu.CompilerParams(vmem_limit_bytes=48 * 1024 * 1024),
    )(scal, place, *operands)


def rms_scale(x):
    return lax.rsqrt(jnp.mean(x * x, axis=-1, keepdims=True) + EPSILON)


def rms_norm(x, gain):
    return x * rms_scale(x) * gain


def rms_back(x, gain, dn):
    scale = rms_scale(x)
    unit = x * scale
    gain_grad = jnp.sum(dn * unit, axis=0)
    dg = dn * gain
    dx = scale * (dg - unit * jnp.mean(dg * unit, axis=-1, keepdims=True))
    return dx, gain_grad


def head_total(partial_sum):
    return lax.psum(partial_sum.astype(BF), "head").astype(F32)


def mlp_forward(resid, gain, weights):
    gate_w, up_w, down_t = weights
    normed = rms_norm(resid, gain).astype(BF)
    gate_val = dot(normed, gate_w, 1, 0)
    up_val = dot(normed, up_w, 1, 0)
    hidden = (gate_val * jax.nn.sigmoid(gate_val) * up_val).astype(BF)
    result = resid + head_total(dot(hidden, down_t, 1, 1))
    return result, (normed, gate_val, up_val, hidden)


def mlp_backward(resid, grad_out, gain, saved, weights):
    gate_w, up_w, down_t = weights
    normed, gate_val, up_val, hidden = saved
    grad_b = grad_out.astype(BF)
    down_grad = dot(grad_b, hidden, 0, 0).astype(BF)
    dh = dot(grad_b, down_t, 1, 0)
    sig = jax.nn.sigmoid(gate_val)
    silu = gate_val * sig
    d_gate = (dh * up_val * (sig * (1.0 + gate_val * (1.0 - sig)))).astype(BF)
    d_up = (dh * silu).astype(BF)
    gate_grad = dot(normed, d_gate, 0, 0).astype(BF)
    up_grad = dot(normed, d_up, 0, 0).astype(BF)
    dn = head_total(dot(d_gate, gate_w, 1, 1) + dot(d_up, up_w, 1, 1))
    dx, gain_grad = rms_back(resid, gain, dn)
    return grad_out + dx, gain_grad, (gate_grad, up_grad, down_grad)


def shifted(block, before, shift):
    if shift == 0:
        return block
    return jnp.concatenate([before[:, before.shape[1] - shift :], block[:, :-shift]], axis=1)


def advanced(block, after, shift):
    if shift == 0:
        return block
    return jnp.concatenate([block[:, shift:], after[:, :shift]], axis=1)


def per_device(
    activations,
    offsets,
    cotangent,
    attn_query,
    attn_key,
    attn_value,
    attn_output,
    ffn1_gate,
    ffn1_up,
    ffn1_down,
    conv_input,
    conv_gate,
    conv_output,
    conv_kernel,
    ffn2_gate,
    ffn2_up,
    ffn2_down,
    norm_gains,
):
    n = lax.axis_size("seq")
    ring = Ring(n)
    micro, row_count, tok, width = activations.shape
    rows = micro * row_count
    count = rows * tok
    qw, vw = attn_query.shape[1], attn_value.shape[1]
    cw = conv_input.shape[1]
    taps = conv_kernel.shape[0]
    here = lax.axis_index("seq")
    start = here * tok
    off = offsets.reshape(rows)

    qkv_s = jnp.concatenate([attn_query, attn_key, attn_value], axis=1)
    groups = (
        (qkv_s, attn_output.T),
        (ffn1_gate, ffn1_up, ffn1_down.T),
        (conv_input, conv_gate, conv_output.T),
        (ffn2_gate, ffn2_up, ffn2_down.T),
    )
    gathered = []
    ties = None
    for group in groups:
        blocks, ties = ring.gather(list(group), ties)
        gathered.append([jnp.concatenate(b, axis=0) for b in blocks])
    (qkv_w, out_t), ffn1, (inner_w, gate_w, conv_out_t), ffn2 = gathered

    gains = ring.to_relative(norm_gains).astype(F32)
    kernel_f = conv_kernel.astype(F32)
    inputs = ring.to_relative(activations.reshape(count, width)).astype(F32)
    grad_four = ring.to_relative(cotangent.reshape(count, width)).astype(F32)

    scal = jnp.concatenate([start[None].astype(jnp.int32), off])
    place = (ring.owners()[:, None] * tok + jnp.arange(tok, dtype=jnp.int32)[None]).reshape(1, n * tok)
    normed_a = rms_norm(inputs, gains[0]).astype(BF)
    qkv = dot(normed_a, qkv_w, 1, 0).astype(BF)
    (qkv_blocks,), _ = ring.gather([qkv])
    qkv_all = jnp.concatenate([b.reshape(rows, tok, -1) for b in qkv_blocks], axis=1)
    own = qkv.reshape(rows, tok, -1)
    q_own, k_own, v_own = own[..., :qw], own[..., qw : 2 * qw], own[..., 2 * qw :]
    q_all, k_all, v_all = qkv_all[..., :qw], qkv_all[..., qw : 2 * qw], qkv_all[..., 2 * qw :]
    (mixed,) = by_rows(attend_kernel, scal, place, (q_own, k_all, v_all), (vw,), (BF,))
    mixed = mixed.reshape(count, vw)
    resid_one = inputs + head_total(dot(mixed, out_t, 1, 1))

    resid_two, kept_one = mlp_forward(resid_one, gains[1], ffn1)

    normed_c = rms_norm(resid_two, gains[2]).astype(BF)
    inner = dot(normed_c, inner_w, 1, 0).reshape(rows, tok, cw)
    gate_c = dot(normed_c, gate_w, 1, 0).reshape(rows, tok, cw)
    pos = start + jnp.arange(tok + taps - 1, dtype=jnp.int32)
    current = pos[None, :] >= off[:, None]

    def valid(t, first, length):
        p = pos[None, first : first + length]
        source = p - t
        same = (source >= off[:, None]) == current[:, first : first + length]
        return ((source >= 0) & same).astype(F32)[:, :, None]

    edge = lax.ppermute(inner[:, tok - (taps - 1) :], "seq", [(i, i + 1) for i in range(n - 1)])
    moved = [shifted(inner, edge, t) * valid(t, 0, tok) for t in range(taps)]
    conv = sum(kernel_f[t][None, None, :] * moved[t] for t in range(taps))
    product = (conv * gate_c).astype(BF).reshape(count, cw)
    resid_three = resid_two + head_total(dot(product, conv_out_t, 1, 1))

    resid_four, kept_two = mlp_forward(resid_three, gains[3], ffn2)
    block_output = ring.from_relative(resid_four.astype(BF)).reshape(activations.shape)

    grad_three, gain_four, grads_two = mlp_backward(resid_three, grad_four, gains[3], kept_two, ffn2)
    sums_two = [ring.scatter(g, i % 2 == 1) for i, g in enumerate(grads_two)]

    grad_b = grad_three.astype(BF)
    conv_out_grad = dot(grad_b, product, 0, 0).astype(BF)
    d_product = dot(grad_b, conv_out_t, 1, 0).reshape(rows, tok, cw)
    d_gate_c = (d_product * conv).astype(BF).reshape(count, cw)
    d_conv = d_product * gate_c
    next_rows = lax.ppermute(d_conv[:, : taps - 1], "seq", [(i + 1, i) for i in range(n - 1)])
    d_inner = sum(
        kernel_f[t][None, None, :] * advanced(d_conv, next_rows, t) * valid(t, t, tok)
        for t in range(taps)
    )
    d_inner = d_inner.astype(BF).reshape(count, cw)
    kernel_grad = jnp.stack([jnp.sum(d_conv * moved[t], axis=(0, 1)) for t in range(taps)])
    conv_in_grad = dot(normed_c, d_inner, 0, 0).astype(BF)
    conv_gate_grad = dot(normed_c, d_gate_c, 0, 0).astype(BF)
    dn = head_total(dot(d_inner, inner_w, 1, 1) + dot(d_gate_c, gate_w, 1, 1))
    dx, gain_three = rms_back(resid_two, gains[2], dn)
    grad_two = grad_three + dx
    sums_conv = [
        ring.scatter(g, i % 2 == 0) for i, g in enumerate((conv_in_grad, conv_gate_grad, conv_out_grad))
    ]

    grad_one, gain_two, grads_one = mlp_backward(resid_one, grad_two, gains[1], kept_one, ffn1)
    sums_one = [ring.scatter(g, i % 2 == 1) for i, g in enumerate(grads_one)]

    grad_b = grad_one.astype(BF)
    output_grad = dot(grad_b, mixed, 0, 0).astype(BF)
    da = dot(grad_b, out_t, 1, 0).reshape(rows, tok, vw)
    dq, dan, extra = by_rows(
        query_back_kernel, scal, place, (q_own, k_all, v_all, da), (qw, vw, qw), (BF, BF, BF)
    )
    back = jnp.concatenate([dan, extra], axis=-1).reshape(count, vw + qw)
    (back_blocks,), _ = ring.gather([back])
    back_all = jnp.concatenate([b.reshape(rows, tok, -1) for b in back_blocks], axis=1)
    dk, dv = by_rows(
        key_back_kernel,
        scal,
        place,
        (k_own, v_own, q_all, back_all[..., :vw], back_all[..., vw:]),
        (qw, vw),
        (BF, BF),
    )
    d_qkv = jnp.concatenate([dq, dk, dv], axis=-1).reshape(count, 2 * qw + vw)
    qkv_grad = dot(normed_a, d_qkv, 0, 0).astype(BF)
    dn = head_total(dot(d_qkv, qkv_w, 1, 1))
    dx, gain_one = rms_back(inputs, gains[0], dn)
    input_grad = ring.from_relative(grad_one + dx).reshape(activations.shape)
    sums_attn = [ring.scatter(g, i % 2 == 0) for i, g in enumerate((qkv_grad, output_grad))]

    gains_grad = ring.from_relative(jnp.stack([gain_one, gain_two, gain_three, gain_four]))
    gains_grad = lax.psum(gains_grad.astype(BF), "seq").astype(F32)
    kernel_grad = lax.psum(kernel_grad.astype(BF), "seq").astype(F32)
    return (
        block_output,
        input_grad,
        sums_attn[0][:, :qw],
        sums_attn[0][:, qw : 2 * qw],
        sums_attn[0][:, 2 * qw :],
        sums_attn[1].T,
        sums_one[0],
        sums_one[1],
        sums_one[2].T,
        sums_conv[0],
        sums_conv[1],
        sums_conv[2].T,
        kernel_grad,
        sums_two[0],
        sums_two[1],
        sums_two[2].T,
        gains_grad,
    )


def solution(mesh):
    rows_in = P("seq", "head")
    rows_out = P("head", "seq")
    tokens = P(None, None, "seq", None)
    in_specs = (
        (tokens, P(), tokens)
        + (rows_in, rows_in, rows_in, rows_out)
        + (rows_in, rows_in, rows_out)
        + (rows_in, rows_in, rows_out)
        + (P(None, "head"),)
        + (rows_in, rows_in, rows_out)
        + (P(),)
    )
    out_specs = (
        (tokens, tokens)
        + (rows_in, rows_in, rows_in, rows_out)
        + (rows_in, rows_in, rows_out)
        + (rows_in, rows_in, rows_out)
        + (P(None, "head"),)
        + (rows_in, rows_in, rows_out)
        + (P(),)
    )
    return jax.shard_map(
        per_device, mesh=mesh, in_specs=in_specs, out_specs=out_specs, check_vma=False
    )
```

time: 3600 us -> 1250 us (0.35)
  waiting for transfers between devices: 2760 us -> 470 us
  blocking collectives: 265 us -> 37.1 us
  starting transfers between devices: 15.4 us -> 195 us
  local copies, waits for them, and re-layouts: 115 us -> 232 us
  matrix products: 238 us -> 123 us
  other arithmetic: 176 us -> 122 us
  Pallas kernels: 0 us -> 38 us
    reduce_scatter x18 -> x0, waiting for transfers between devices: 1440 us -> none  [the longest x2 180 us: scatter_grads(): lax.psum_scatter(grads[11].astype(jnp.bfloat16), 'seq', scatter_dimension...]
    all_gather x15 -> x0, waiting for transfers between devices: 534 us -> none  [the longest x1 69.9 us: gather_weights(): lax.all_gather(shards[4], 'seq', axis=0, tiled=True)]
    unnamed x56 -> x7, waiting for transfers between devices: 427 us -> 0.11 us
    ppermute x4 -> x170, waiting for transfers between devices: 19 us -> 378 us  [the longest x168 378 us: hop(): return lax.ppermute(block, 'seq', route)]
    psum x7, waiting for transfers between devices: 345 us -> 91.2 us  [head_total(): return lax.psum(partial_sum.astype(BF), 'head').astype(F32)]
    all_gather x8 -> x0, blocking collectives: 228 us -> none  [the longest x4 101 us: carried_in(): lax.all_gather(part.astype(kind), axis)]
    ppermute x4 -> x170, starting transfers between devices: 10.9 us -> 195 us  [the longest x168 190 us: hop(): return lax.ppermute(block, 'seq', route)]
    dot_general x106 -> x33, matrix products: 238 us -> 123 us  [dot(): lax.dot_general(a, b, (((ca,), (cb,)), ((), ())), preferred_element_type=...]
  transfers between devices with their start and end apart: 52 -> 177, of which waited for: 44 -> 70; matrix products, arithmetic and copies ran while one was open for 11% -> 31% of each run, Pallas kernels for 0% -> 3%
where the time goes in v1:
time: 1250 us; the launch traced here: 1230 us
  waiting for transfers between devices  470 us (38%)
  local copies, waits for them, and re-layouts  232 us (19%)
  starting transfers between devices  195 us (16%)
  matrix products  123 us (10%)
  other arithmetic  122 us (10%)
  Pallas kernels  38 us (3%)
  blocking collectives  37.1 us (3%)
  between operations  17.5 us (1%)
    ppermute x168, waiting for transfers between devices, hop(): return lax.ppermute(block, 'seq', route)  378 us
    ppermute x168, starting transfers between devices, hop(): return lax.ppermute(block, 'seq', route)  190 us
    unnamed x304, local copies, waits for them, and re-layouts  127 us
    dot_general x33, matrix products, dot(): lax.dot_general(a, b, (((ca,), (cb,)), ((), ())), preferred_element_type=...  123 us
    psum x7, waiting for transfers between devices, head_total(): return lax.psum(partial_sum.astype(BF), 'head').astype(F32)  91.2 us
    pallas_call x3, Pallas kernels, by_rows(): pl.pallas_call(kernel, grid=(rows,), in_specs=specs, out_specs=[pl.BlockS...  38 us
    psum x1, blocking collectives, per_device(): kernel_grad = lax.psum(kernel_grad.astype(BF), 'seq').astype(F32)  37.1 us
    convert_element_type x33, other arithmetic, scatter(): acc = (acc.astype(F32) + term(d * k % n).astype(F32)).astype(BF)  33.4 us
  transfers between devices with their start and end apart: 177, of which 70 were waited for; matrix products, arithmetic and copies ran while one was open for 31% of the time, Pallas kernels for 3%

profile of v1, /device:TPU:0, one launch (start us, length us, event | category | flops | bytes accessed | tf_op | source)
XLA Modules:
  0.0 1234.8 jit_solution(2776249229738790612)
XLA Ops:
  38.6 6.0 concatenate.105
  67.5 4.8 concatenate.127
  103.9 5.4 collective-permute-done.24
  113.2 4.9 collective-permute-done.35
  123.6 7.1 collective-permute-done.7
  134.2 7.6 collective-permute-done.29
  149.6 14.2 %collective-permute-done.22 = bf16[224,1152]{1,0:T(8,128)(2,1)S(1)} collective-permute-done((bf16[224,1152]{1,0:T(8,128)(2,1)}, bf16[224,1152]{1,0:T(8,128)(2,1)S(1)}, u32[]{:S(2)}, u32[]{:S(2)}) %collective-permute-start.22) | collective-permute-done | bytes 516128 | tf_op jit(solution)/shard_map/ppermute | solution.py:40
  166.7 8.2 collective-permute-done.30
  183.0 4.6 collective-permute-done.8
  193.5 5.1 collective-permute-done.23
  201.9 7.8 collective-permute-done.37
  217.7 12.8 %collective-permute-done.42 = bf16[224,448]{1,0:T(8,128)(2,1)S(1)} collective-permute-done((bf16[224,448]{1,0:T(8,128)(2,1)S(1)}, bf16[224,448]{1,0:T(8,128)(2,1)S(1)}, u32[]{:S(2)}, u32[]{:S(2)}) %collective-permute-start.42) | collective-permute-done | bytes 200736 | tf_op jit(solution)/shard_map/ppermute | solution.py:40
  245.0 5.9 collective-permute-done.43
  310.1 25.2 %collective-permute-done.63 = bf16[224,448]{0,1:T(8,128)(2,1)S(1)} collective-permute-done((bf16[224,448]{0,1:T(8,128)(2,1)S(1)}, bf16[224,448]{0,1:T(8,128)(2,1)S(1)}, u32[]{:S(2)}, u32[]{:S(2)}) %collective-permute-start.63) | collective-permute-done | bytes 200736 | tf_op jit(solution)/shard_map/ppermute | solution.py:40
  364.6 7.1 shard_map.323
  389.2 8.5 collective-permute-done.65
  399.3 9.6 collective-permute-done.79
  413.4 4.4 collective-permute-done.73
  429.0 5.4 fusion.88
  454.1 4.7 collective-permute-done.77
  463.3 16.0 %collective-permute-done.84 = bf16[224,1152]{1,0:T(8,128)(2,1)S(1)} collective-permute-done((bf16[224,1152]{1,0:T(8,128)(2,1)}, bf16[224,1152]{1,0:T(8,128)(2,1)S(1)}, u32[]{:S(2)}, u32[]{:S(2)}) %collective-permute-start.84) | collective-permute-done | bytes 516128 | tf_op jit(solution)/shard_map/ppermute | solution.py:40
  485.6 5.0 all-reduce.12.cloned.1.call-done
  490.6 4.4 multiply_reduce_fusion.1
  518.4 4.2 multiply_convert_fusion.10
  529.8 7.1 fusion.35
  536.9 36.5 %all-reduce.14.cloned.1.call-done = bf16[512,1792]{1,0:T(8,128)(2,1)} async-done(((bf16[512,1792]{1,0:T(8,128)(2,1)}), bf16[512,1792]{1,0:T(8,128)(2,1)}) %all-reduce.14.cloned.1.call-update) | async-done | bytes 1835024 | tf_op jit(solution)/shard_map/psum | solution.py:245
  582.7 6.6 multiply_convert_fusion.6
  591.9 4.6 convolution_convert_fusion.1
  596.5 4.8 convolution_convert_fusion.2
  601.2 6.0 add_convert_fusion.2
  607.4 4.9 convolution_convert_fusion
  630.2 8.7 collective-permute-done.149
  642.7 7.4 collective-permute-done.156
  671.3 4.5 fusion.92
  712.1 6.5 collective-permute-done.157
  726.8 4.7 collective-permute-done.128
  732.8 7.2 collective-permute-done.143
  743.4 5.2 collective-permute-done.136
  750.0 5.7 collective-permute-done.129
  791.0 8.4 collective-permute-done.158
  803.2 4.6 collective-permute-done.141
  827.2 4.7 convolution_convert_fusion.3
  839.4 4.6 convolution_convert_fusion.4
  843.9 4.9 convolution_convert_fusion.5
  848.9 6.0 add_convert_fusion
  871.6 4.7 collective-permute-done.162
  878.5 8.8 collective-permute-done.121
  889.8 8.6 collective-permute-done.107
  903.6 5.0 fusion.24
  908.7 4.8 fusion.15
  915.5 15.4 %shard_map.324 = (bf16[4,128,64]{2,1,0:T(8,128)(2,1)S(1)}, bf16[4,128,448]{2,1,0:T(8,128)(2,1)S(1)}, bf16[4,128,64]{2,1,0:T(8,128)(2,1)S(1)}) custom-call(s32[5]{0:T(128)S(1)} %pad_add_fusion.scal_ref, s32[1,1024]{1,0:T(1,128)S(1)} %bitcast.165, bf16[4,128,64]{2,1,0:T(8,128)(2,1)S(1)} %get-tuple-element.243.q_ref, bf16[4,1024,64]{2,1,0:T(8,128)(2,1)S(1)} %copy-done.2, ...), custom_call_target="tpu_custom_call" | custom-call | tf_op jit(solution)/shard_map/pallas_call | solution.py:217
  944.3 7.8 collective-permute-done.104
  956.6 6.6 collective-permute-done.86
  965.2 12.7 %collective-permute-done.102 = bf16[224,448]{0,1:T(8,128)(2,1)S(1)} collective-permute-done((bf16[224,448]{0,1:T(8,128)(2,1)S(1)}, bf16[224,448]{0,1:T(8,128)(2,1)S(1)}, u32[]{:S(2)}, u32[]{:S(2)}) %collective-permute-start.102) | collective-permute-done | bytes 200736 | tf_op jit(solution)/shard_map/ppermute | solution.py:40
  984.7 7.8 collective-permute-done.109
  995.6 19.2 %collective-permute-done.90 = bf16[512,512]{1,0:T(8,128)(2,1)S(1)} collective-permute-done((bf16[512,512]{1,0:T(8,128)(2,1)S(1)}, bf16[512,512]{1,0:T(8,128)(2,1)S(1)}, u32[]{:S(2)}, u32[]{:S(2)}) %collective-permute-start.90) | collective-permute-done | bytes 524320 | tf_op jit(solution)/shard_map/ppermute | solution.py:40
  1020.1 10.9 collective-permute-done.91
  1037.3 16.0 %collective-permute-done.92 = bf16[512,512]{1,0:T(8,128)(2,1)S(1)} collective-permute-done((bf16[512,512]{1,0:T(8,128)(2,1)S(1)}, bf16[512,512]{1,0:T(8,128)(2,1)S(1)}, u32[]{:S(2)}, u32[]{:S(2)}) %collective-permute-start.92) | collective-permute-done | bytes 524320 | tf_op jit(solution)/shard_map/ppermute | solution.py:40
  1057.4 15.6 %shard_map.325 = (bf16[4,128,64]{2,1,0:T(8,128)(2,1)S(1)}, bf16[4,128,448]{2,1,0:T(8,128)(2,1)S(1)}) custom-call(s32[5]{0:T(128)S(1)} %pad_add_fusion.scal_ref, s32[1,1024]{1,0:T(1,128)S(1)} %bitcast.166, bf16[4,128,64]{2,1,0:T(8,128)(2,1)S(1)} %get-tuple-element.242.k_ref, bf16[4,128,448]{2,1,0:T(8,128)(2,1)S(1)} %slice.728.v_ref, ...), custom_call_target="tpu_custom_call" | custom-call | tf_op jit(solution)/shard_map/pallas_call | solution.py:217
  1096.0 5.0 collective-permute-done.95
  1117.6 46.5 %all-reduce.22.cloned.1.call-done = (bf16[512,1792]{1,0:T(8,128)(2,1)}, bf16[512,1792]{1,0:T(8,128)(2,1)}) async-done(((bf16[512,1792]{1,0:T(8,128)(2,1)}, bf16[512,1792]{1,0:T(8,128)(2,1)}), (bf16[512,1792]{1,0:T(8,128)(2,1)}, bf16[512,1792]{1,0:T(8,128)(2,1)})) %all-reduce.22.cloned.1.call-update) | async-done | bytes 3670032 | tf_op jit(solution)/shard_map/psum | solution.py:245
  1164.1 4.4 fusion.27
  1180.9 37.1 %all-reduce = (bf16[3,448]{1,0:T(4,128)(2,1)S(1)}, bf16[4,1792]{1,0:T(4,128)(2,1)S(1)}) all-reduce(bf16[3,448]{1,0:T(4,128)(2,1)S(1)} %pad_maximum_fusion.7, bf16[4,1792]{1,0:T(4,128)(2,1)S(1)} %concatenate.138), channel_id=1, replica_groups=mesh['seq'=8,'head'=4] {'seq'}, use_global_device_ids=true, to_apply=%region_19.20 | all-reduce | flops 8512 | bytes 34048 | tf_op jit(solution)/shard_map/psum | solution.py:427
  1223.3 4.5 concatenate.136
  (811 shorter events, 633.4 us)
Async XLA Ops:
  7.2 414.7 %all-reduce.10.cloned.1.call-start = ((), (), s32[]{:S(2)}) async-start(), calls=%async_computation | async-start | bytes 3670016 | tf_op jit(solution)/shard_map/psum | solution.py:245
  7.3 52.6 %collective-permute-start.18 = (bf16[224,448]{0,1:T(8,128)(2,1)}, bf16[224,448]{0,1:T(8,128)(2,1)}, u32[]{:S(2)}, u32[]{:S(2)}) collective-permute-start(bf16[224,448]{0,1:T(8,128)(2,1)} %bitcast.206), channel_id=1, source_target_pairs={{0,8},{8,16},{16,24},{24,28},{28,20},{20,12},{12,4},{4,0},{1,9},{9... | collective-permute-start | bytes 602120 | tf_op jit(solution)/shard_map/ppermute | solution.py:40
  10.4 42.4 %collective-permute-start.14 = (bf16[224,448]{0,1:T(8,128)(2,1)}, bf16[224,448]{0,1:T(8,128)(2,1)}, u32[]{:S(2)}, u32[]{:S(2)}) collective-permute-start(bf16[224,448]{0,1:T(8,128)(2,1)} %bitcast.207), channel_id=1, source_target_pairs={{0,4},{8,0},{16,8},{24,16},{28,24},{20,28},{12,20},{4,12},{1,5},{9... | collective-permute-start | bytes 602120 | tf_op jit(solution)/shard_map/ppermute | solution.py:40
  14.0 37.2 %collective-permute-start = (bf16[224,576]{1,0:T(8,128)(2,1)}, bf16[224,576]{1,0:T(8,128)(2,1)}, u32[]{:S(2)}, u32[]{:S(2)}) collective-permute-start(bf16[224,576]{1,0:T(8,128)(2,1)} %get-tuple-element.143), channel_id=1, source_target_pairs={{0,4},{8,0},{16,8},{24,16},{28,24},{20,28},{12,20},{4,12},{1,5},{9... | collective-permute-start | bytes 774152 | tf_op jit(solution)/shard_map/ppermute | solution.py:40
  15.9 32.5 %collective-permute-start.3 = (bf16[224,576]{1,0:T(8,128)(2,1)}, bf16[224,576]{1,0:T(8,128)(2,1)}, u32[]{:S(2)}, u32[]{:S(2)}) collective-permute-start(bf16[224,576]{1,0:T(8,128)(2,1)} %get-tuple-element.143), channel_id=1, source_target_pairs={{0,8},{8,16},{16,24},{24,28},{28,20},{20,12},{12,4},{4,0},{1,9},{9... | collective-permute-start | bytes 774152 | tf_op jit(solution)/shard_map/ppermute | solution.py:40
  109.3 32.5 %collective-permute-start.29 = (bf16[224,1152]{1,0:T(8,128)(2,1)}, bf16[224,1152]{1,0:T(8,128)(2,1)}, u32[]{:S(2)}, u32[]{:S(2)}) collective-permute-start(bf16[224,1152]{1,0:T(8,128)(2,1)} %copy-done.56), channel_id=1, source_target_pairs={{0,4},{8,0},{16,8},{24,16},{28,24},{20,28},{12,20},{4,12},{1,5},{9... | collective-permute-start | bytes 1548296 | tf_op jit(solution)/shard_map/ppermute | solution.py:40
  110.9 32.2 %collective-permute-start.33 = (bf16[224,1152]{1,0:T(8,128)(2,1)}, bf16[224,1152]{1,0:T(8,128)(2,1)}, u32[]{:S(2)}, u32[]{:S(2)}) collective-permute-start(bf16[224,1152]{1,0:T(8,128)(2,1)} %collective-permute-done.32), channel_id=1, source_target_pairs={{0,8},{8,16},{16,24},{24,28},{28,20},{20,12},{12,4},{4,0},{1,9},{9... | collective-permute-start | bytes 1548296 | tf_op jit(solution)/shard_map/ppermute | solution.py:40
  122.0 43.4 %collective-permute-start.36 = (bf16[224,1152]{1,0:T(8,128)(2,1)}, bf16[224,1152]{1,0:T(8,128)(2,1)S(1)}, u32[]{:S(2)}, u32[]{:S(2)}) collective-permute-start(bf16[224,1152]{1,0:T(8,128)(2,1)} %collective-permute-done.35), channel_id=1, source_target_pairs={{0,4},{8,0},{16,8},{24,16},{28,24},{20,28},{12,20},{4,12},{1,5},{9... | collective-permute-start | bytes 1548296 | tf_op jit(solution)/shard_map/ppermute | solution.py:40
  130.6 33.2 %collective-permute-start.22 = (bf16[224,1152]{1,0:T(8,128)(2,1)}, bf16[224,1152]{1,0:T(8,128)(2,1)S(1)}, u32[]{:S(2)}, u32[]{:S(2)}) collective-permute-start(bf16[224,1152]{1,0:T(8,128)(2,1)} %collective-permute-done.21), channel_id=1, source_target_pairs={{0,4},{8,0},{16,8},{24,16},{28,24},{20,28},{12,20},{4,12},{1,5},{9... | collective-permute-start | bytes 1548296 | tf_op jit(solution)/shard_map/ppermute | solution.py:40
  141.8 33.2 %collective-permute-start.30 = (bf16[224,1152]{1,0:T(8,128)(2,1)}, bf16[224,1152]{1,0:T(8,128)(2,1)}, u32[]{:S(2)}, u32[]{:S(2)}) collective-permute-start(bf16[224,1152]{1,0:T(8,128)(2,1)} %collective-permute-done.29), channel_id=1, source_target_pairs={{0,4},{8,0},{16,8},{24,16},{28,24},{20,28},{12,20},{4,12},{1,5},{9... | collective-permute-start | bytes 1548296 | tf_op jit(solution)/shard_map/ppermute | solution.py:40
  143.2 33.4 %collective-permute-start.34 = (bf16[224,1152]{1,0:T(8,128)(2,1)}, bf16[224,1152]{1,0:T(8,128)(2,1)}, u32[]{:S(2)}, u32[]{:S(2)}) collective-permute-start(bf16[224,1152]{1,0:T(8,128)(2,1)} %collective-permute-done.33), channel_id=1, source_target_pairs={{0,8},{8,16},{16,24},{24,28},{28,20},{20,12},{12,4},{4,0},{1,9},{9... | collective-permute-start | bytes 1548296 | tf_op jit(solution)/shard_map/ppermute | solution.py:40
  146.1 32.8 %collective-permute-start.25 = (bf16[224,1152]{1,0:T(8,128)(2,1)}, bf16[224,1152]{1,0:T(8,128)(2,1)}, u32[]{:S(2)}, u32[]{:S(2)}) collective-permute-start(bf16[224,1152]{1,0:T(8,128)(2,1)} %collective-permute-done.24), channel_id=1, source_target_pairs={{0,8},{8,16},{16,24},{24,28},{28,20},{20,12},{12,4},{4,0},{1,9},{9... | collective-permute-start | bytes 1548296 | tf_op jit(solution)/shard_map/ppermute | solution.py:40
  178.9 30.8 %collective-permute-start.37 = (bf16[224,1152]{1,0:T(8,128)(2,1)}, bf16[224,1152]{1,0:T(8,128)(2,1)}, u32[]{:S(2)}, u32[]{:S(2)}) collective-permute-start(bf16[224,1152]{1,0:T(8,128)(2,1)} %copy-done.55), channel_id=1, source_target_pairs={{0,4},{8,0},{16,8},{24,16},{28,24},{20,28},{12,20},{4,12},{1,5},{9... | collective-permute-start | bytes 1548296 | tf_op jit(solution)/shard_map/ppermute | solution.py:40
  198.7 39.1 %collective-permute-start.31 = (bf16[224,1152]{1,0:T(8,128)(2,1)}, bf16[224,1152]{1,0:T(8,128)(2,1)S(1)}, u32[]{:S(2)}, u32[]{:S(2)}) collective-permute-start(bf16[224,1152]{1,0:T(8,128)(2,1)} %collective-permute-done.30), channel_id=1, source_target_pairs={{0,4},{8,0},{16,8},{24,16},{28,24},{20,28},{12,20},{4,12},{1,5},{9... | collective-permute-start | bytes 1548296 | tf_op jit(solution)/shard_map/ppermute | solution.py:40
  213.6 53.5 %collective-permute-start.12 = (bf16[512,576]{0,1:T(8,128)(2,1)S(1)}, bf16[512,576]{0,1:T(8,128)(2,1)}, u32[]{:S(2)}, u32[]{:S(2)}) collective-permute-start(bf16[512,576]{0,1:T(8,128)(2,1)S(1)} %collective-permute-done.11), channel_id=1, source_target_pairs={{0,8},{8,16},{16,24},{24,28},{28,20},{20,12},{12,4},{4,0},{1,9},{9... | collective-permute-start | bytes 1769480 | tf_op jit(solution)/shard_map/ppermute | solution.py:40
  230.5 33.3 %collective-permute-start.9 = (bf16[512,576]{0,1:T(8,128)(2,1)}, bf16[512,576]{0,1:T(8,128)(2,1)}, u32[]{:S(2)}, u32[]{:S(2)}) collective-permute-start(bf16[512,576]{0,1:T(8,128)(2,1)} %copy-done.52), channel_id=1, source_target_pairs={{0,4},{8,0},{16,8},{24,16},{28,24},{20,28},{12,20},{4,12},{1,5},{9... | collective-permute-start | bytes 1769480 | tf_op jit(solution)/shard_map/ppermute | solution.py:40
  300.2 47.3 %collective-permute-start.71 = (bf16[224,1152]{1,0:T(8,128)(2,1)}, bf16[224,1152]{1,0:T(8,128)(2,1)}, u32[]{:S(2)}, u32[]{:S(2)}) collective-permute-start(bf16[224,1152]{1,0:T(8,128)(2,1)} %param.35), channel_id=1, source_target_pairs={{0,4},{8,0},{16,8},{24,16},{28,24},{20,28},{12,20},{4,12},{1,5},{9... | collective-permute-start | bytes 1548296 | tf_op jit(solution)/shard_map/ppermute | solution.py:40
  302.4 75.9 %collective-permute-start.75 = (bf16[224,1152]{1,0:T(8,128)(2,1)}, bf16[224,1152]{1,0:T(8,128)(2,1)}, u32[]{:S(2)}, u32[]{:S(2)}) collective-permute-start(bf16[224,1152]{1,0:T(8,128)(2,1)} %param.35), channel_id=1, source_target_pairs={{0,8},{8,16},{16,24},{24,28},{28,20},{20,12},{12,4},{4,0},{1,9},{9... | collective-permute-start | bytes 1548296 | tf_op jit(solution)/shard_map/ppermute | solution.py:40
  302.5 48.0 %collective-permute-start.13 = (bf16[512,576]{0,1:T(8,128)(2,1)}, bf16[512,576]{0,1:T(8,128)(2,1)}, u32[]{:S(2)}, u32[]{:S(2)}) collective-permute-start(bf16[512,576]{0,1:T(8,128)(2,1)} %collective-permute-done.12), channel_id=1, source_target_pairs={{0,8},{8,16},{16,24},{24,28},{28,20},{20,12},{12,4},{4,0},{1,9},{9... | collective-permute-start | bytes 1769480 | tf_op jit(solution)/shard_map/ppermute | solution.py:40
  303.5 37.3 %collective-permute-start.48 = (bf16[224,448]{1,0:T(8,128)(2,1)}, bf16[224,448]{1,0:T(8,128)(2,1)}, u32[]{:S(2)}, u32[]{:S(2)}) collective-permute-start(bf16[224,448]{1,0:T(8,128)(2,1)} %collective-permute-done.47), channel_id=1, source_target_pairs={{0,8},{8,16},{16,24},{24,28},{28,20},{20,12},{12,4},{4,0},{1,9},{9... | collective-permute-start | bytes 602120 | tf_op jit(solution)/shard_map/ppermute | solution.py:40
  336.0 46.0 %collective-permute-start.67 = (bf16[224,1152]{1,0:T(8,128)(2,1)}, bf16[224,1152]{1,0:T(8,128)(2,1)}, u32[]{:S(2)}, u32[]{:S(2)}) collective-permute-start(bf16[224,1152]{1,0:T(8,128)(2,1)} %param.34), channel_id=1, source_target_pairs={{0,8},{8,16},{16,24},{24,28},{28,20},{20,12},{12,4},{4,0},{1,9},{9... | collective-permute-start | bytes 1548296 | tf_op jit(solution)/shard_map/ppermute | solution.py:40
  340.8 41.5 %collective-permute-start.81 = (bf16[224,1152]{1,0:T(8,128)(2,1)}, bf16[224,1152]{1,0:T(8,128)(2,1)}, u32[]{:S(2)}, u32[]{:S(2)}) collective-permute-start(bf16[224,1152]{1,0:T(8,128)(2,1)} %bitcast.204), channel_id=1, source_target_pairs={{0,8},{8,16},{16,24},{24,28},{28,20},{20,12},{12,4},{4,0},{1,9},{9... | collective-permute-start | bytes 1548296 | tf_op jit(solution)/shard_map/ppermute | solution.py:40
  374.8 115.8 %all-reduce.12.cloned.1.call-start = ((), (), s32[]{:S(2)}) async-start(), calls=%async_computation.1 | async-start | bytes 3670016 | tf_op jit(solution)/shard_map/psum | solution.py:245
  382.3 30.7 %collective-permute-start.82 = (bf16[224,1152]{1,0:T(8,128)(2,1)}, bf16[224,1152]{1,0:T(8,128)(2,1)S(1)}, u32[]{:S(2)}, u32[]{:S(2)}) collective-permute-start(bf16[224,1152]{1,0:T(8,128)(2,1)} %collective-permute-done.81), channel_id=1, source_target_pairs={{0,8},{8,16},{16,24},{24,28},{28,20},{20,12},{12,4},{4,0},{1,9},{9... | collective-permute-start | bytes 1548296 | tf_op jit(solution)/shard_map/ppermute | solution.py:40
  386.7 31.0 %collective-permute-start.73 = (bf16[224,1152]{1,0:T(8,128)(2,1)}, bf16[224,1152]{1,0:T(8,128)(2,1)}, u32[]{:S(2)}, u32[]{:S(2)}) collective-permute-start(bf16[224,1152]{1,0:T(8,128)(2,1)} %collective-permute-done.72), channel_id=1, source_target_pairs={{0,4},{8,0},{16,8},{24,16},{28,24},{20,28},{12,20},{4,12},{1,5},{9... | collective-permute-start | bytes 1548296 | tf_op jit(solution)/shard_map/ppermute | solution.py:40
  397.7 40.7 %collective-permute-start.76 = (bf16[224,1152]{1,0:T(8,128)(2,1)}, bf16[224,1152]{1,0:T(8,128)(2,1)}, u32[]{:S(2)}, u32[]{:S(2)}) collective-permute-start(bf16[224,1152]{1,0:T(8,128)(2,1)} %collective-permute-done.75), channel_id=1, source_target_pairs={{0,8},{8,16},{16,24},{24,28},{28,20},{20,12},{12,4},{4,0},{1,9},{9... | collective-permute-start | bytes 1548296 | tf_op jit(solution)/shard_map/ppermute | solution.py:40
  408.8 41.4 %collective-permute-start.66 = (bf16[224,1152]{1,0:T(8,128)(2,1)S(1)}, bf16[224,1152]{1,0:T(8,128)(2,1)}, u32[]{:S(2)}, u32[]{:S(2)}) collective-permute-start(bf16[224,1152]{1,0:T(8,128)(2,1)S(1)} %collective-permute-done.65), channel_id=1, source_target_pairs={{0,4},{8,0},{16,8},{24,16},{28,24},{20,28},{12,20},{4,12},{1,5},{9... | collective-permute-start | bytes 1548296 | tf_op jit(solution)/shard_map/ppermute | solution.py:40
  411.3 35.0 %collective-permute-start.80 = (bf16[224,1152]{1,0:T(8,128)(2,1)}, bf16[224,1152]{1,0:T(8,128)(2,1)}, u32[]{:S(2)}, u32[]{:S(2)}) collective-permute-start(bf16[224,1152]{1,0:T(8,128)(2,1)} %collective-permute-done.79), channel_id=1, source_target_pairs={{0,4},{8,0},{16,8},{24,16},{28,24},{20,28},{12,20},{4,12},{1,5},{9... | collective-permute-start | bytes 1548296 | tf_op jit(solution)/shard_map/ppermute | solution.py:40
  413.0 30.8 %collective-permute-start.69 = (bf16[224,1152]{1,0:T(8,128)(2,1)S(1)}, bf16[224,1152]{1,0:T(8,128)(2,1)}, u32[]{:S(2)}, u32[]{:S(2)}) collective-permute-start(bf16[224,1152]{1,0:T(8,128)(2,1)S(1)} %collective-permute-done.68), channel_id=1, source_target_pairs={{0,8},{8,16},{16,24},{24,28},{28,20},{20,12},{12,4},{4,0},{1,9},{9... | collective-permute-start | bytes 1548296 | tf_op jit(solution)/shard_map/ppermute | solution.py:40
  443.7 129.7 %all-reduce.14.cloned.1.call-start = ((), (), s32[]{:S(2)}) async-start(), calls=%async_computation.2 | async-start | bytes 3670016 | tf_op jit(solution)/shard_map/psum | solution.py:245
  444.9 39.9 %collective-permute-start.70 = (bf16[224,1152]{1,0:T(8,128)(2,1)}, bf16[224,1152]{1,0:T(8,128)(2,1)S(1)}, u32[]{:S(2)}, u32[]{:S(2)}) collective-permute-start(bf16[224,1152]{1,0:T(8,128)(2,1)} %collective-permute-done.69), channel_id=1, source_target_pairs={{0,8},{8,16},{16,24},{24,28},{28,20},{20,12},{12,4},{4,0},{1,9},{9... | collective-permute-start | bytes 1548296 | tf_op jit(solution)/shard_map/ppermute | solution.py:40
  446.4 33.0 %collective-permute-start.84 = (bf16[224,1152]{1,0:T(8,128)(2,1)}, bf16[224,1152]{1,0:T(8,128)(2,1)S(1)}, u32[]{:S(2)}, u32[]{:S(2)}) collective-permute-start(bf16[224,1152]{1,0:T(8,128)(2,1)} %collective-permute-done.83), channel_id=1, source_target_pairs={{0,8},{8,16},{16,24},{24,28},{28,20},{20,12},{12,4},{4,0},{1,9},{9... | collective-permute-start | bytes 1548296 | tf_op jit(solution)/shard_map/ppermute | solution.py:40
  525.8 128.9 %all-reduce.16.cloned.1.call-start = ((), (), s32[]{:S(2)}) async-start(), calls=%async_computation.3 | async-start | bytes 3670016 | tf_op jit(solution)/shard_map/psum | solution.py:245
  607.3 212.4 %all-reduce.18.cloned.1.call-start = ((), (), s32[]{:S(2)}) async-start(), calls=%async_computation.4 | async-start | bytes 3670016 | tf_op jit(solution)/shard_map/psum | solution.py:245
  614.6 88.9 %collective-permute-start.167 = (bf16[224,1152]{1,0:T(8,128)(2,1)}, bf16[224,1152]{1,0:T(8,128)(2,1)}, u32[]{:S(2)}, u32[]{:S(2)}) collective-permute-start(bf16[224,1152]{1,0:T(8,128)(2,1)} %get-tuple-element.156), channel_id=1, source_target_pairs={{0,4},{8,0},{16,8},{24,16},{28,24},{20,28},{12,20},{4,12},{1,5},{9... | collective-permute-start | bytes 1548296 | tf_op jit(solution)/shard_map/ppermute | solution.py:40
  619.1 88.0 %collective-permute-start.153 = (bf16[224,1152]{1,0:T(8,128)(2,1)}, bf16[224,1152]{1,0:T(8,128)(2,1)}, u32[]{:S(2)}, u32[]{:S(2)}) collective-permute-start(bf16[224,1152]{1,0:T(8,128)(2,1)} %get-tuple-element.168), channel_id=1, source_target_pairs={{0,4},{8,0},{16,8},{24,16},{28,24},{20,28},{12,20},{4,12},{1,5},{9... | collective-permute-start | bytes 1548296 | tf_op jit(solution)/shard_map/ppermute | solution.py:40
  627.8 83.9 %collective-permute-start.160 = (bf16[224,1152]{1,0:T(8,128)(2,1)}, bf16[224,1152]{1,0:T(8,128)(2,1)}, u32[]{:S(2)}, u32[]{:S(2)}) collective-permute-start(bf16[224,1152]{1,0:T(8,128)(2,1)} %get-tuple-element.162), channel_id=1, source_target_pairs={{0,8},{8,16},{16,24},{24,28},{28,20},{20,12},{12,4},{4,0},{1,9},{9... | collective-permute-start | bytes 1548296 | tf_op jit(solution)/shard_map/ppermute | solution.py:40
  638.9 64.8 %collective-permute-start.164 = (bf16[224,1152]{1,0:T(8,128)(2,1)}, bf16[224,1152]{1,0:T(8,128)(2,1)}, u32[]{:S(2)}, u32[]{:S(2)}) collective-permute-start(bf16[224,1152]{1,0:T(8,128)(2,1)} %add_convert_fusion.8), channel_id=1, source_target_pairs={{0,8},{8,16},{16,24},{24,28},{28,20},{20,12},{12,4},{4,0},{1,9},{9... | collective-permute-start | bytes 1548296 | tf_op jit(solution)/shard_map/ppermute | solution.py:40
  700.7 202.9 %all-reduce.20.cloned.1.call-start = ((), (), s32[]{:S(2)}) async-start(), calls=%async_computation.5 | async-start | bytes 3670016 | tf_op jit(solution)/shard_map/psum | solution.py:245
  725.1 53.6 %collective-permute-start.165 = (bf16[224,1152]{1,0:T(8,128)(2,1)S(1)}, bf16[224,1152]{1,0:T(8,128)(2,1)S(1)}, u32[]{:S(2)}, u32[]{:S(2)}) collective-permute-start(bf16[224,1152]{1,0:T(8,128)(2,1)S(1)} %get-tuple-element.153), channel_id=1, source_target_pairs={{0,8},{8,16},{16,24},{24,28},{28,20},{20,12},{12,4},{4,0},{1,9},{9... | collective-permute-start | bytes 1548296 | tf_op jit(solution)/shard_map/ppermute | solution.py:40
  731.9 48.2 %collective-permute-start.168 = (bf16[224,1152]{1,0:T(8,128)(2,1)S(1)}, bf16[224,1152]{1,0:T(8,128)(2,1)S(1)}, u32[]{:S(2)}, u32[]{:S(2)}) collective-permute-start(bf16[224,1152]{1,0:T(8,128)(2,1)S(1)} %get-tuple-element.154), channel_id=1, source_target_pairs={{0,4},{8,0},{16,8},{24,16},{28,24},{20,28},{12,20},{4,12},{1,5},{9... | collective-permute-start | bytes 1548296 | tf_op jit(solution)/shard_map/ppermute | solution.py:40
  741.8 41.3 %collective-permute-start.151 = (bf16[224,1152]{1,0:T(8,128)(2,1)S(1)}, bf16[224,1152]{1,0:T(8,128)(2,1)S(1)}, u32[]{:S(2)}, u32[]{:S(2)}) collective-permute-start(bf16[224,1152]{1,0:T(8,128)(2,1)S(1)} %get-tuple-element.165), channel_id=1, source_target_pairs={{0,8},{8,16},{16,24},{24,28},{28,20},{20,12},{12,4},{4,0},{1,9},{9... | collective-permute-start | bytes 1548296 | tf_op jit(solution)/shard_map/ppermute | solution.py:40
  780.2 32.0 %collective-permute-start.145 = (bf16[224,448]{0,1:T(8,128)(2,1)}, bf16[224,448]{0,1:T(8,128)(2,1)}, u32[]{:S(2)}, u32[]{:S(2)}) collective-permute-start(bf16[224,448]{0,1:T(8,128)(2,1)} %get-tuple-element.217), channel_id=1, source_target_pairs={{0,4},{8,0},{16,8},{24,16},{28,24},{20,28},{12,20},{4,12},{1,5},{9... | collective-permute-start | bytes 602120 | tf_op jit(solution)/shard_map/ppermute | solution.py:40
  807.8 53.6 %collective-permute-start.166 = (bf16[224,1152]{1,0:T(8,128)(2,1)}, bf16[224,1152]{1,0:T(8,128)(2,1)}, u32[]{:S(2)}, u32[]{:S(2)}) collective-permute-start(bf16[224,1152]{1,0:T(8,128)(2,1)} %get-tuple-element.151), channel_id=1, source_target_pairs={{0,8},{8,16},{16,24},{24,28},{28,20},{20,12},{12,4},{4,0},{1,9},{9... | collective-permute-start | bytes 1548296 | tf_op jit(solution)/shard_map/ppermute | solution.py:40
  812.1 50.5 %collective-permute-start.169 = (bf16[224,1152]{1,0:T(8,128)(2,1)}, bf16[224,1152]{1,0:T(8,128)(2,1)}, u32[]{:S(2)}, u32[]{:S(2)}) collective-permute-start(bf16[224,1152]{1,0:T(8,128)(2,1)} %get-tuple-element.152), channel_id=1, source_target_pairs={{0,4},{8,0},{16,8},{24,16},{28,24},{20,28},{12,20},{4,12},{1,5},{9... | collective-permute-start | bytes 1548296 | tf_op jit(solution)/shard_map/ppermute | solution.py:40
  812.7 54.0 %collective-permute-start.152 = (bf16[224,1152]{1,0:T(8,128)(2,1)}, bf16[224,1152]{1,0:T(8,128)(2,1)}, u32[]{:S(2)}, u32[]{:S(2)}) collective-permute-start(bf16[224,1152]{1,0:T(8,128)(2,1)} %get-tuple-element.163), channel_id=1, source_target_pairs={{0,8},{8,16},{16,24},{24,28},{28,20},{20,12},{12,4},{4,0},{1,9},{9... | collective-permute-start | bytes 1548296 | tf_op jit(solution)/shard_map/ppermute | solution.py:40
  816.1 51.1 %collective-permute-start.155 = (bf16[224,1152]{1,0:T(8,128)(2,1)}, bf16[224,1152]{1,0:T(8,128)(2,1)S(1)}, u32[]{:S(2)}, u32[]{:S(2)}) collective-permute-start(bf16[224,1152]{1,0:T(8,128)(2,1)} %get-tuple-element.164), channel_id=1, source_target_pairs={{0,4},{8,0},{16,8},{24,16},{28,24},{20,28},{12,20},{4,12},{1,5},{9... | collective-permute-start | bytes 1548296 | tf_op jit(solution)/shard_map/ppermute | solution.py:40
  816.6 54.4 %collective-permute-start.159 = (bf16[224,1152]{1,0:T(8,128)(2,1)}, bf16[224,1152]{1,0:T(8,128)(2,1)S(1)}, u32[]{:S(2)}, u32[]{:S(2)}) collective-permute-start(bf16[224,1152]{1,0:T(8,128)(2,1)} %get-tuple-element.157), channel_id=1, source_target_pairs={{0,4},{8,0},{16,8},{24,16},{28,24},{20,28},{12,20},{4,12},{1,5},{9... | collective-permute-start | bytes 1548296 | tf_op jit(solution)/shard_map/ppermute | solution.py:40
  854.9 309.2 %all-reduce.22.cloned.1.call-start = ((), (), s32[]{:S(2)}) async-start(), calls=%async_computation.6 | async-start | bytes 7340032 | tf_op jit(solution)/shard_map/psum | solution.py:245
  866.6 65.7 %collective-permute-start.125 = (bf16[224,1152]{1,0:T(8,128)(2,1)}, bf16[224,1152]{1,0:T(8,128)(2,1)}, u32[]{:S(2)}, u32[]{:S(2)}) collective-permute-start(bf16[224,1152]{1,0:T(8,128)(2,1)} %get-tuple-element.174), channel_id=1, source_target_pairs={{0,4},{8,0},{16,8},{24,16},{28,24},{20,28},{12,20},{4,12},{1,5},{9... | collective-permute-start | bytes 1548296 | tf_op jit(solution)/shard_map/ppermute | solution.py:40
  867.2 31.2 %collective-permute-start.107 = (bf16[224,1152]{1,0:T(8,128)(2,1)S(1)}, bf16[224,1152]{1,0:T(8,128)(2,1)S(1)}, u32[]{:S(2)}, u32[]{:S(2)}) collective-permute-start(bf16[224,1152]{1,0:T(8,128)(2,1)S(1)} %get-tuple-element.185), channel_id=1, source_target_pairs={{0,8},{8,16},{16,24},{24,28},{28,20},{20,12},{12,4},{4,0},{1,9},{9... | collective-permute-start | bytes 1548296 | tf_op jit(solution)/shard_map/ppermute | solution.py:40
  871.0 69.7 %collective-permute-start.111 = (bf16[224,1152]{1,0:T(8,128)(2,1)}, bf16[224,1152]{1,0:T(8,128)(2,1)}, u32[]{:S(2)}, u32[]{:S(2)}) collective-permute-start(bf16[224,1152]{1,0:T(8,128)(2,1)} %get-tuple-element.186), channel_id=1, source_target_pairs={{0,4},{8,0},{16,8},{24,16},{28,24},{20,28},{12,20},{4,12},{1,5},{9... | collective-permute-start | bytes 1548296 | tf_op jit(solution)/shard_map/ppermute | solution.py:40
  887.3 67.2 %collective-permute-start.118 = (bf16[224,1152]{1,0:T(8,128)(2,1)}, bf16[224,1152]{1,0:T(8,128)(2,1)}, u32[]{:S(2)}, u32[]{:S(2)}) collective-permute-start(bf16[224,1152]{1,0:T(8,128)(2,1)} %get-tuple-element.180), channel_id=1, source_target_pairs={{0,8},{8,16},{16,24},{24,28},{28,20},{20,12},{12,4},{4,0},{1,9},{9... | collective-permute-start | bytes 1548296 | tf_op jit(solution)/shard_map/ppermute | solution.py:40
  898.4 34.6 %collective-permute-start.122 = (bf16[224,1152]{1,0:T(8,128)(2,1)S(1)}, bf16[224,1152]{1,0:T(8,128)(2,1)}, u32[]{:S(2)}, u32[]{:S(2)}) collective-permute-start(bf16[224,1152]{1,0:T(8,128)(2,1)S(1)} %add_convert_fusion.23), channel_id=1, source_target_pairs={{0,8},{8,16},{16,24},{24,28},{28,20},{20,12},{12,4},{4,0},{1,9},{9... | collective-permute-start | bytes 1548296 | tf_op jit(solution)/shard_map/ppermute | solution.py:40
  900.9 41.4 %collective-permute-start.108 = (bf16[224,1152]{1,0:T(8,128)(2,1)S(1)}, bf16[224,1152]{1,0:T(8,128)(2,1)}, u32[]{:S(2)}, u32[]{:S(2)}) collective-permute-start(bf16[224,1152]{1,0:T(8,128)(2,1)S(1)} %add_convert_fusion.33), channel_id=1, source_target_pairs={{0,8},{8,16},{16,24},{24,28},{28,20},{20,12},{12,4},{4,0},{1,9},{9... | collective-permute-start | bytes 1548296 | tf_op jit(solution)/shard_map/ppermute | solution.py:40
  980.1 37.8 %collective-permute-start.116 = (bf16[224,1152]{1,0:T(8,128)(2,1)S(1)}, bf16[224,1152]{1,0:T(8,128)(2,1)S(1)}, u32[]{:S(2)}, u32[]{:S(2)}) collective-permute-start(bf16[224,1152]{1,0:T(8,128)(2,1)S(1)} %get-tuple-element.177), channel_id=1, source_target_pairs={{0,4},{8,0},{16,8},{24,16},{28,24},{20,28},{12,20},{4,12},{1,5},{9... | collective-permute-start | bytes 1548296 | tf_op jit(solution)/shard_map/ppermute | solution.py:40
  982.0 36.1 %collective-permute-start.119 = (bf16[224,1152]{1,0:T(8,128)(2,1)S(1)}, bf16[224,1152]{1,0:T(8,128)(2,1)S(1)}, u32[]{:S(2)}, u32[]{:S(2)}) collective-permute-start(bf16[224,1152]{1,0:T(8,128)(2,1)S(1)} %get-tuple-element.178), channel_id=1, source_target_pairs={{0,8},{8,16},{16,24},{24,28},{28,20},{20,12},{12,4},{4,0},{1,9},{9... | collective-permute-start | bytes 1548296 | tf_op jit(solution)/shard_map/ppermute | solution.py:40
  982.6 32.2 %collective-permute-start.90 = (bf16[512,512]{1,0:T(8,128)(2,1)S(1)}, bf16[512,512]{1,0:T(8,128)(2,1)S(1)}, u32[]{:S(2)}, u32[]{:S(2)}) collective-permute-start(bf16[512,512]{1,0:T(8,128)(2,1)S(1)} %collective-permute-done.89), channel_id=1, source_target_pairs={{0,8},{8,16},{16,24},{24,28},{28,20},{20,12},{12,4},{4,0},{1,9},{9... | collective-permute-start | bytes 1572872 | tf_op jit(solution)/shard_map/ppermute | solution.py:40
  994.4 39.7 %collective-permute-start.103 = (bf16[224,448]{0,1:T(8,128)(2,1)S(1)}, bf16[224,448]{0,1:T(8,128)(2,1)S(1)}, u32[]{:S(2)}, u32[]{:S(2)}) collective-permute-start(bf16[224,448]{0,1:T(8,128)(2,1)S(1)} %get-tuple-element.235), channel_id=1, source_target_pairs={{0,8},{8,16},{16,24},{24,28},{28,20},{20,12},{12,4},{4,0},{1,9},{9... | collective-permute-start | bytes 602120 | tf_op jit(solution)/shard_map/ppermute | solution.py:40
  1018.1 57.6 %collective-permute-start.124 = (bf16[224,1152]{1,0:T(8,128)(2,1)S(1)}, bf16[224,1152]{1,0:T(8,128)(2,1)S(1)}, u32[]{:S(2)}, u32[]{:S(2)}) collective-permute-start(bf16[224,1152]{1,0:T(8,128)(2,1)S(1)} %get-tuple-element.169), channel_id=1, source_target_pairs={{0,8},{8,16},{16,24},{24,28},{28,20},{20,12},{12,4},{4,0},{1,9},{9... | collective-permute-start | bytes 1548296 | tf_op jit(solution)/shard_map/ppermute | solution.py:40
  1034.1 43.1 %collective-permute-start.127 = (bf16[224,1152]{1,0:T(8,128)(2,1)S(1)}, bf16[224,1152]{1,0:T(8,128)(2,1)S(1)}, u32[]{:S(2)}, u32[]{:S(2)}) collective-permute-start(bf16[224,1152]{1,0:T(8,128)(2,1)S(1)} %get-tuple-element.170), channel_id=1, source_target_pairs={{0,4},{8,0},{16,8},{24,16},{28,24},{20,28},{12,20},{4,12},{1,5},{9... | collective-permute-start | bytes 1548296 | tf_op jit(solution)/shard_map/ppermute | solution.py:40
  1034.3 59.0 %collective-permute-start.110 = (bf16[224,1152]{1,0:T(8,128)(2,1)}, bf16[224,1152]{1,0:T(8,128)(2,1)S(1)}, u32[]{:S(2)}, u32[]{:S(2)}) collective-permute-start(bf16[224,1152]{1,0:T(8,128)(2,1)} %get-tuple-element.181), channel_id=1, source_target_pairs={{0,8},{8,16},{16,24},{24,28},{28,20},{20,12},{12,4},{4,0},{1,9},{9... | collective-permute-start | bytes 1548296 | tf_op jit(solution)/shard_map/ppermute | solution.py:40
  1037.0 56.8 %collective-permute-start.113 = (bf16[224,1152]{1,0:T(8,128)(2,1)}, bf16[224,1152]{1,0:T(8,128)(2,1)S(1)}, u32[]{:S(2)}, u32[]{:S(2)}) collective-permute-start(bf16[224,1152]{1,0:T(8,128)(2,1)} %get-tuple-element.182), channel_id=1, source_target_pairs={{0,4},{8,0},{16,8},{24,16},{28,24},{20,28},{12,20},{4,12},{1,5},{9... | collective-permute-start | bytes 1548296 | tf_op jit(solution)/shard_map/ppermute | solution.py:40
  1053.3 55.3 %collective-permute-start.117 = (bf16[224,1152]{1,0:T(8,128)(2,1)}, bf16[224,1152]{1,0:T(8,128)(2,1)S(1)}, u32[]{:S(2)}, u32[]{:S(2)}) collective-permute-start(bf16[224,1152]{1,0:T(8,128)(2,1)} %get-tuple-element.175), channel_id=1, source_target_pairs={{0,4},{8,0},{16,8},{24,16},{28,24},{20,28},{12,20},{4,12},{1,5},{9... | collective-permute-start | bytes 1548296 | tf_op jit(solution)/shard_map/ppermute | solution.py:40
  (224 other events, 3169.4 us)
Sparse Core Ops, SparseCore 0:
  374.9 46.9 all-reduce.9
  443.9 46.7 all-reduce.11
  525.9 47.5 all-reduce.13
  607.4 47.1 all-reduce.15
  700.8 45.3 all-reduce.17
  855.0 46.7 all-reduce.19
  1087.8 76.2 all-reduce.21

commit v2 on v1

--- a/solution.py
+++ b/solution.py
@@ -14,100 +14,245 @@
 F32 = jnp.float32
 
 
-def ring_order(n):
-    if n % 4:
-        return list(range(n))
-    inner = n // 4
-    if inner == 2:
-        return [0, 2, 4, 6, 7, 5, 3, 1]
-    return list(range(n))
-
-
-class Ring:
-    def __init__(self, n):
-        self.n = n
-        self.hops = n <= 8
-        self.order = ring_order(n)
-        place = [0] * n
-        for position, device in enumerate(self.order):
-            place[device] = position
-        self.place = place
-        self.pos = jnp.asarray(place, jnp.int32)[lax.axis_index("seq")] if self.hops else jnp.int32(0)
-
-    def hop(self, block, step):
-        n = self.n
-        route = [(self.order[i], self.order[(i + step) % n]) for i in range(n)]
-        return lax.ppermute(block, "seq", route)
-
-    def owners(self):
-        return jnp.asarray(self.order, jnp.int32)[(self.pos + jnp.arange(self.n)) % self.n]
-
-    def to_relative(self, x):
-        if not self.hops:
-            return x
-        width = x.shape[-1] // self.n
-        parts = [x[..., b * width : (b + 1) * width] for b in self.order]
-        twice = jnp.concatenate(parts + parts, axis=-1)
-        return lax.dynamic_slice_in_dim(twice, self.pos * width, x.shape[-1], axis=x.ndim - 1)
-
-    def from_relative(self, x):
-        if not self.hops:
-            return x
-        width = x.shape[-1] // self.n
-        twice = jnp.concatenate([x, x], axis=-1)
-        start = ((self.n - self.pos) % self.n) * width
-        ring = lax.dynamic_slice_in_dim(twice, start, x.shape[-1], axis=x.ndim - 1)
-        parts = [ring[..., p * width : (p + 1) * width] for p in self.place]
-        return jnp.concatenate(parts, axis=-1)
-
-    def gather(self, arrays, after=None):
-        n = self.n
-        if not self.hops:
-            whole = [lax.all_gather(a, "seq") for a in arrays]
-            return [[w[k] for k in range(n)] for w in whole], None
-        right = list(arrays)
-        left = list(arrays)
-        if after is not None:
-            ties_r, ties_l = after
-            for j in range(len(arrays)):
-                right[j], _ = lax.optimization_barrier((arrays[j], ties_r[j % len(ties_r)]))
-                left[j], _ = lax.optimization_barrier((arrays[j], ties_l[j % len(ties_l)]))
-        blocks = [{0: a} for a in arrays]
-        both = (n - 1) // 2
-        for k in range(1, both + 1):
-            for j in range(len(arrays)):
-                right[j] = self.hop(right[j], 1)
-                left[j] = self.hop(left[j], -1)
-                blocks[j][n - k] = right[j]
-                blocks[j][k] = left[j]
-        ties = (list(right), list(left))
-        if n % 2 == 0:
-            for j in range(len(arrays)):
-                blocks[j][n // 2] = self.hop(right[j], 1) if j % 2 == 0 else self.hop(left[j], -1)
-        return [[b[k] for k in range(n)] for b in blocks], ties
-
-    def scatter(self, full, flip):
-        n = self.n
-        height = full.shape[0] // n
-        if not self.hops:
-            return lax.psum_scatter(full, "seq", scatter_dimension=0, tiled=True).astype(F32)
-
-        def term(k):
-            return full[k * height : (k + 1) * height]
-
-        direction = -1 if flip else 1
-        long_hops, short_hops = n // 2, (n - 1) // 2
-        total = term(0).astype(F32)
-        for d, hops in ((direction, long_hops), (-direction, short_hops)):
-            if hops == 0:
+MESH = pl.DeviceIdType.MESH
+ANY = pl.BlockSpec(memory_space=pl.ANY)
+
+
+def ring_device(p):
+    return jnp.where(p < 4, 2 * p, 15 - 2 * p)
+
+
+def ring_position(s):
+    return jnp.where(lax.rem(s, 2) == 0, s // 2, 7 - s // 2)
+
+
+def ring_size(n):
+    return n == 8
+
+
+def greet(n):
+    pos = ring_position(lax.axis_index("seq"))
+    right = ring_device(lax.rem(pos + 1, n))
+    left = ring_device(lax.rem(pos + n - 1, n))
+    barrier = pltpu.get_barrier_semaphore()
+    for neighbour in (left, right):
+        pl.semaphore_signal(barrier, inc=1, device_id={"seq": neighbour}, device_id_type=MESH)
+    pl.semaphore_wait(barrier, 2)
+    return pos, right, left
+
+
+class GatherRing:
+    def __init__(self, n, where, src, out, send, recv, flip):
+        self.n, self.src, self.out, self.send, self.recv = n, src, out, send, recv
+        self.pos, self.right, self.left = where
+        self.height = src.shape[0]
+        self.started = []
+        self.flip = flip
+        self.steps = n // 2
+        self.done = 0
+
+    def rows(self, r):
+        owner = ring_device(lax.rem(self.pos + (r % self.n), self.n))
+        return pl.ds(pl.multiple_of(owner * self.height, 32), self.height)
+
+    def copy(self, k, d):
+        rows = self.rows(-d * (k - 1))
+        i = 0 if d == 1 else 1
+        return pltpu.make_async_remote_copy(
+            src_ref=self.src if k == 1 else self.out.at[rows],
+            dst_ref=self.out.at[rows],
+            send_sem=self.send.at[i, k - 1],
+            recv_sem=self.recv.at[i, k - 1],
+            device_id={"seq": self.right if d == 1 else self.left},
+            device_id_type=MESH,
+        )
+
+    def begin(self, local):
+        self.own = pltpu.make_async_copy(self.src, self.out.at[self.rows(0)], local)
+        self.own.start()
+
+    def ways(self, k):
+        if k <= (self.n - 1) // 2:
+            return (1, -1)
+        return (-1,) if self.flip else (1,)
+
+    def step(self):
+        if self.done == self.steps:
+            return
+        self.done += 1
+        k = self.done
+        for d in self.ways(k):
+            if k > 1:
+                self.copy(k - 1, d).wait_recv()
+            self.copy(k, d).start()
+
+    def finish(self):
+        while self.done < self.steps:
+            self.step()
+        self.own.wait()
+        last = {d: max(k for k in range(1, self.steps + 1) if d in self.ways(k)) for d in (1, -1)}
+        for d in (1, -1):
+            self.copy(last[d], d).wait_recv()
+        for k in range(1, self.steps + 1):
+            for d in self.ways(k):
+                self.copy(k, d).wait_send()
+
+
+def gather_kernel(n, flips, *refs):
+    count = len(flips)
+    srcs, outs, sems = refs[:count], refs[count : 2 * count], refs[2 * count :]
+    send, recv, local = sems
+    where = greet(n)
+    rings = [
+        GatherRing(n, where, srcs[j], outs[j], send.at[j], recv.at[j], flips[j]) for j in range(count)
+    ]
+    for j, ring in enumerate(rings):
+        ring.begin(local.at[j])
+    for _ in range(n // 2):
+        for ring in rings:
+            ring.step()
+    for ring in rings:
+        ring.finish()
+
+
+def gather_all(arrays, call_id, flip=0):
+    n = lax.axis_size("seq")
+    if not ring_size(n):
+        return [lax.all_gather(a, "seq", axis=0, tiled=True) for a in arrays]
+    count = len(arrays)
+    return pl.pallas_call(
+        partial(gather_kernel, n, [(j + flip) % 2 == 1 for j in range(count)]),
+        in_specs=[ANY] * count,
+        out_specs=[ANY] * count,
+        out_shape=[jax.ShapeDtypeStruct((n * a.shape[0], a.shape[1]), a.dtype) for a in arrays],
+        scratch_shapes=[
+            pltpu.SemaphoreType.DMA((count, 2, n // 2)),
+            pltpu.SemaphoreType.DMA((count, 2, n // 2)),
+            pltpu.SemaphoreType.DMA((count,)),
+        ],
+        compiler_params=pltpu.CompilerParams(collective_id=call_id, has_side_effects=True),
+    )(*arrays)
+
+
+class ScatterRing:
+    def __init__(self, n, where, full, out, terms, slots, send, recv, load, flip):
+        self.n, self.full, self.out, self.terms, self.slots = n, full, out, terms, slots
+        self.send, self.recv, self.load = send, recv, load
+        self.pos, self.right, self.left = where
+        self.height = out.shape[0]
+        d = -1 if flip else 1
+        self.hops = {d: n // 2, -d: (n - 1) // 2}
+        self.order = (d, -d)
+        self.done = 0
+        self.steps = n // 2
+
+    def source(self, r):
+        owner = ring_device(lax.rem(self.pos + (r % self.n), self.n))
+        return self.full.at[pl.ds(pl.multiple_of(owner * self.height, 32), self.height)]
+
+    def term(self, d, h):
+        r = d * (self.hops[d] - h)
+        return pltpu.make_async_copy(self.source(r), self.terms.at[r % self.n], self.load.at[r % self.n])
+
+    def copy(self, d, h):
+        i = 0 if d == 1 else 1
+        r = d * (self.hops[d] - h + 1)
+        return pltpu.make_async_remote_copy(
+            src_ref=self.source(r) if h == 1 else self.terms.at[r % self.n],
+            dst_ref=self.slots.at[i, h - 1],
+            send_sem=self.send.at[i, h - 1],
+            recv_sem=self.recv.at[i, h - 1],
+            device_id={"seq": self.right if d == 1 else self.left},
+            device_id_type=MESH,
+        )
+
+    def step(self):
+        if self.done == self.steps:
+            return
+        self.done += 1
+        h = self.done
+        for d in self.order:
+            if h > self.hops[d]:
                 continue
-            acc = term((d * hops) % n)
-            for k in range(hops - 1, -1, -1):
-                acc = self.hop(acc, d)
-                if k:
-                    acc = (acc.astype(F32) + term((d * k) % n).astype(F32)).astype(BF)
-            total = total + acc.astype(F32)
-        return total
+            if h > 1:
+                self.copy(d, h - 1).wait_recv()
+                self.term(d, h - 1).wait()
+                i, r = (0 if d == 1 else 1), (d * (self.hops[d] - h + 1)) % self.n
+                total = self.slots[i, h - 2].astype(F32) + self.terms[r].astype(F32)
+                self.terms[r] = total.astype(BF)
+            self.copy(d, h).start()
+            if h < self.hops[d]:
+                self.term(d, h).start()
+        if h == 1:
+            self.own = pltpu.make_async_copy(self.source(0), self.terms.at[0], self.load.at[0])
+            self.own.start()
+
+    def finish(self):
+        while self.done < self.steps:
+            self.step()
+        self.own.wait()
+        total = self.terms[0].astype(F32)
+        for d in self.order:
+            i, h = (0 if d == 1 else 1), self.hops[d]
+            self.copy(d, h).wait_recv()
+            total = total + self.slots[i, h - 1].astype(F32)
+        self.out[...] = total
+        for d in self.order:
+            for h in range(1, self.hops[d] + 1):
+                self.copy(d, h).wait_send()
+
+
+def scatter_kernel(n, flips, *refs):
+    count = len(flips)
+    fulls, outs, rest = refs[:count], refs[count : 2 * count], refs[2 * count :]
+    terms, slots, (send, recv, load) = rest[:count], rest[count : 2 * count], rest[2 * count :]
+    where = greet(n)
+    rings = [
+        ScatterRing(
+            n, where, fulls[j], outs[j], terms[j], slots[j], send.at[j], recv.at[j], load.at[j], flips[j]
+        )
+        for j in range(count)
+    ]
+    for _ in range(n // 2):
+        for ring in rings:
+            ring.step()
+    for ring in rings:
+        ring.finish()
+
+
+def scatter_all(fulls, call_id, flip=0):
+    n = lax.axis_size("seq")
+    if not ring_size(n):
+        return [
+            lax.psum_scatter(g, "seq", scatter_dimension=0, tiled=True).astype(F32) for g in fulls
+        ]
+    count = len(fulls)
+    blocks = [(g.shape[0] // n, g.shape[1]) for g in fulls]
+    return pl.pallas_call(
+        partial(scatter_kernel, n, [(j + flip) % 2 == 1 for j in range(count)]),
+        in_specs=[ANY] * count,
+        out_specs=[pl.BlockSpec(memory_space=pltpu.VMEM)] * count,
+        out_shape=[jax.ShapeDtypeStruct(b, F32) for b in blocks],
+        scratch_shapes=[pltpu.VMEM((n,) + b, BF) for b in blocks]
+        + [pltpu.VMEM((2, n // 2) + b, BF) for b in blocks]
+        + [
+            pltpu.SemaphoreType.DMA((count, 2, n // 2)),
+            pltpu.SemaphoreType.DMA((count, 2, n // 2)),
+            pltpu.SemaphoreType.DMA((count, n)),
+        ],
+        compiler_params=pltpu.CompilerParams(
+            collective_id=call_id, has_side_effects=True, vmem_limit_bytes=56 * 1024 * 1024
+        ),
+    )(*fulls)
+
+
+def small_sum(x, axis):
+    size = lax.axis_size(axis)
+    if size > 8:
+        return lax.psum(x.astype(BF), axis).astype(F32)
+    sent = x.astype(BF)
+    routes = [[(i, (i + k) % size) for i in range(size)] for k in range(1, size)]
+    return x + sum(lax.ppermute(sent, axis, r).astype(F32) for r in routes)
 
 
 def dot(a, b, ca, cb):
@@ -242,7 +387,11 @@
 
 
 def head_total(partial_sum):
-    return lax.psum(partial_sum.astype(BF), "head").astype(F32)
+    return lax.psum(partial_sum, "head").astype(F32)
+
+
+def tie(xs, *others):
+    return list(lax.optimization_barrier((tuple(xs), tuple(others)))[0])
 
 
 def mlp_forward(resid, gain, weights):
@@ -251,25 +400,22 @@
     gate_val = dot(normed, gate_w, 1, 0)
     up_val = dot(normed, up_w, 1, 0)
     hidden = (gate_val * jax.nn.sigmoid(gate_val) * up_val).astype(BF)
-    result = resid + head_total(dot(hidden, down_t, 1, 1))
-    return result, (normed, gate_val, up_val, hidden)
-
-
-def mlp_backward(resid, grad_out, gain, saved, weights):
+    return dot(hidden, down_t, 1, 1).astype(BF), (normed, gate_val, up_val, hidden)
+
+
+def mlp_backward(grad_b, saved, weights):
     gate_w, up_w, down_t = weights
     normed, gate_val, up_val, hidden = saved
-    grad_b = grad_out.astype(BF)
-    down_grad = dot(grad_b, hidden, 0, 0).astype(BF)
     dh = dot(grad_b, down_t, 1, 0)
     sig = jax.nn.sigmoid(gate_val)
     silu = gate_val * sig
     d_gate = (dh * up_val * (sig * (1.0 + gate_val * (1.0 - sig)))).astype(BF)
     d_up = (dh * silu).astype(BF)
+    dn_part = (dot(d_gate, gate_w, 1, 1) + dot(d_up, up_w, 1, 1)).astype(BF)
     gate_grad = dot(normed, d_gate, 0, 0).astype(BF)
     up_grad = dot(normed, d_up, 0, 0).astype(BF)
-    dn = head_total(dot(d_gate, gate_w, 1, 1) + dot(d_up, up_w, 1, 1))
-    dx, gain_grad = rms_back(resid, gain, dn)
-    return grad_out + dx, gain_grad, (gate_grad, up_grad, down_grad)
+    down_grad = dot(grad_b, hidden, 0, 0).astype(BF)
+    return dn_part, (gate_grad, up_grad, down_grad)
 
 
 def shifted(block, before, shift):
@@ -305,7 +451,6 @@
     norm_gains,
 ):
     n = lax.axis_size("seq")
-    ring = Ring(n)
     micro, row_count, tok, width = activations.shape
     rows = micro * row_count
     count = rows * tok
@@ -317,38 +462,36 @@
     off = offsets.reshape(rows)
 
     qkv_s = jnp.concatenate([attn_query, attn_key, attn_value], axis=1)
-    groups = (
-        (qkv_s, attn_output.T),
-        (ffn1_gate, ffn1_up, ffn1_down.T),
-        (conv_input, conv_gate, conv_output.T),
-        (ffn2_gate, ffn2_up, ffn2_down.T),
-    )
-    gathered = []
-    ties = None
-    for group in groups:
-        blocks, ties = ring.gather(list(group), ties)
-        gathered.append([jnp.concatenate(b, axis=0) for b in blocks])
-    (qkv_w, out_t), ffn1, (inner_w, gate_w, conv_out_t), ffn2 = gathered
-
-    gains = ring.to_relative(norm_gains).astype(F32)
+    gains = norm_gains.astype(F32)
     kernel_f = conv_kernel.astype(F32)
-    inputs = ring.to_relative(activations.reshape(count, width)).astype(F32)
-    grad_four = ring.to_relative(cotangent.reshape(count, width)).astype(F32)
+    inputs = activations.reshape(count, width).astype(F32)
+    grad_four = cotangent.reshape(count, width)
+    qkv_w, out_t = gather_all([qkv_s, attn_output.T], 1)
 
     scal = jnp.concatenate([start[None].astype(jnp.int32), off])
-    place = (ring.owners()[:, None] * tok + jnp.arange(tok, dtype=jnp.int32)[None]).reshape(1, n * tok)
+    place = jnp.arange(n * tok, dtype=jnp.int32).reshape(1, n * tok)
     normed_a = rms_norm(inputs, gains[0]).astype(BF)
     qkv = dot(normed_a, qkv_w, 1, 0).astype(BF)
-    (qkv_blocks,), _ = ring.gather([qkv])
-    qkv_all = jnp.concatenate([b.reshape(rows, tok, -1) for b in qkv_blocks], axis=1)
+
+    def by_sequence(blocks):
+        return jnp.swapaxes(blocks.reshape(n, rows, tok, -1), 0, 1).reshape(rows, n * tok, -1)
+
+    qkv_all = by_sequence(gather_all([qkv], 2)[0])
     own = qkv.reshape(rows, tok, -1)
     q_own, k_own, v_own = own[..., :qw], own[..., qw : 2 * qw], own[..., 2 * qw :]
     q_all, k_all, v_all = qkv_all[..., :qw], qkv_all[..., qw : 2 * qw], qkv_all[..., 2 * qw :]
     (mixed,) = by_rows(attend_kernel, scal, place, (q_own, k_all, v_all), (vw,), (BF,))
     mixed = mixed.reshape(count, vw)
-    resid_one = inputs + head_total(dot(mixed, out_t, 1, 1))
-
-    resid_two, kept_one = mlp_forward(resid_one, gains[1], ffn1)
+    attn_part = dot(mixed, out_t, 1, 1).astype(BF)
+    attn_sum = head_total(attn_part)
+    ffn1 = gather_all(tie((ffn1_gate, ffn1_up, ffn1_down.T), attn_part), 3)
+    resid_one = inputs + attn_sum
+    part, kept_one = mlp_forward(resid_one, gains[1], ffn1)
+    ffn1_sum = head_total(part)
+    inner_w, gate_w, conv_out_t = gather_all(
+        tie((conv_input, conv_gate, conv_output.T), part), 4, 1
+    )
+    resid_two = resid_one + ffn1_sum
 
     normed_c = rms_norm(resid_two, gains[2]).astype(BF)
     inner = dot(normed_c, inner_w, 1, 0).reshape(rows, tok, cw)
@@ -366,14 +509,20 @@
     moved = [shifted(inner, edge, t) * valid(t, 0, tok) for t in range(taps)]
     conv = sum(kernel_f[t][None, None, :] * moved[t] for t in range(taps))
     product = (conv * gate_c).astype(BF).reshape(count, cw)
-    resid_three = resid_two + head_total(dot(product, conv_out_t, 1, 1))
-
-    resid_four, kept_two = mlp_forward(resid_three, gains[3], ffn2)
-    block_output = ring.from_relative(resid_four.astype(BF)).reshape(activations.shape)
-
-    grad_three, gain_four, grads_two = mlp_backward(resid_three, grad_four, gains[3], kept_two, ffn2)
-    sums_two = [ring.scatter(g, i % 2 == 1) for i, g in enumerate(grads_two)]
-
+    conv_part = dot(product, conv_out_t, 1, 1).astype(BF)
+    conv_sum = head_total(conv_part)
+    ffn2 = gather_all(tie((ffn2_gate, ffn2_up, ffn2_down.T), conv_part), 3)
+    resid_three = resid_two + conv_sum
+    out_part, kept_two = mlp_forward(resid_three, gains[3], ffn2)
+
+    dn_part, grads_two = mlp_backward(grad_four, kept_two, ffn2)
+    dn = head_total(dn_part)
+    sums_two = scatter_all(tie(grads_two, dn_part), 5)
+    (dn,) = tie((dn,), *sums_two)
+    out_sum = head_total(tie((out_part,), *sums_two)[0])
+    block_output = (resid_three + out_sum).astype(BF).reshape(activations.shape)
+    dx, gain_four = rms_back(resid_three, gains[3], dn)
+    grad_three = grad_four.astype(F32) + dx
     grad_b = grad_three.astype(BF)
     conv_out_grad = dot(grad_b, product, 0, 0).astype(BF)
     d_product = dot(grad_b, conv_out_t, 1, 0).reshape(rows, tok, cw)
@@ -388,15 +537,18 @@
     kernel_grad = jnp.stack([jnp.sum(d_conv * moved[t], axis=(0, 1)) for t in range(taps)])
     conv_in_grad = dot(normed_c, d_inner, 0, 0).astype(BF)
     conv_gate_grad = dot(normed_c, d_gate_c, 0, 0).astype(BF)
-    dn = head_total(dot(d_inner, inner_w, 1, 1) + dot(d_gate_c, gate_w, 1, 1))
+    dn_part = (dot(d_inner, inner_w, 1, 1) + dot(d_gate_c, gate_w, 1, 1)).astype(BF)
+    dn = head_total(dn_part)
+    sums_conv = scatter_all(tie((conv_in_grad, conv_gate_grad, conv_out_grad), dn_part), 6, 1)
+    (dn,) = tie((dn,), *sums_conv)
     dx, gain_three = rms_back(resid_two, gains[2], dn)
     grad_two = grad_three + dx
-    sums_conv = [
-        ring.scatter(g, i % 2 == 0) for i, g in enumerate((conv_in_grad, conv_gate_grad, conv_out_grad))
-    ]
-
-    grad_one, gain_two, grads_one = mlp_backward(resid_one, grad_two, gains[1], kept_one, ffn1)
-    sums_one = [ring.scatter(g, i % 2 == 1) for i, g in enumerate(grads_one)]
+    dn_part, grads_one = mlp_backward(grad_two.astype(BF), kept_one, ffn1)
+    dn = head_total(dn_part)
+    sums_one = scatter_all(tie(grads_one, dn_part), 5)
+    (dn,) = tie((dn,), *sums_one)
+    dx, gain_two = rms_back(resid_one, gains[1], dn)
+    grad_one = grad_two + dx
 
     grad_b = grad_one.astype(BF)
     output_grad = dot(grad_b, mixed, 0, 0).astype(BF)
@@ -405,8 +557,7 @@
         query_back_kernel, scal, place, (q_own, k_all, v_all, da), (qw, vw, qw), (BF, BF, BF)
     )
     back = jnp.concatenate([dan, extra], axis=-1).reshape(count, vw + qw)
-    (back_blocks,), _ = ring.gather([back])
-    back_all = jnp.concatenate([b.reshape(rows, tok, -1) for b in back_blocks], axis=1)
+    back_all = by_sequence(gather_all([back], 7, 1)[0])
     dk, dv = by_rows(
         key_back_kernel,
         scal,
@@ -417,14 +568,18 @@
     )
     d_qkv = jnp.concatenate([dq, dk, dv], axis=-1).reshape(count, 2 * qw + vw)
     qkv_grad = dot(normed_a, d_qkv, 0, 0).astype(BF)
-    dn = head_total(dot(d_qkv, qkv_w, 1, 1))
-    dx, gain_one = rms_back(inputs, gains[0], dn)
-    input_grad = ring.from_relative(grad_one + dx).reshape(activations.shape)
-    sums_attn = [ring.scatter(g, i % 2 == 0) for i, g in enumerate((qkv_grad, output_grad))]
-
-    gains_grad = ring.from_relative(jnp.stack([gain_one, gain_two, gain_three, gain_four]))
-    gains_grad = lax.psum(gains_grad.astype(BF), "seq").astype(F32)
-    kernel_grad = lax.psum(kernel_grad.astype(BF), "seq").astype(F32)
+    dn_part = dot(d_qkv, qkv_w, 1, 1).astype(BF)
+    dn = head_total(dn_part)
+    sums_attn = scatter_all(tie((qkv_grad, output_grad), dn_part), 8)
+    (dn,) = tie((dn,), *sums_attn)
+    unit = inputs * rms_scale(inputs)
+    gain_one = jnp.sum(dn_part.astype(F32) * unit, axis=0)
+    gain_one = small_sum(gain_one, "head")
+    dx, _ = rms_back(inputs, gains[0], dn)
+    input_grad = (grad_one + dx).reshape(activations.shape)
+
+    gains_grad = small_sum(jnp.stack([gain_one, gain_two, gain_three, gain_four]), "seq")
+    kernel_grad = small_sum(kernel_grad, "seq")
     return (
         block_output,
         input_grad,

time: 1250 us -> 1120 us (0.90)
  Pallas kernels: 38 us -> 820 us
  waiting for transfers between devices: 470 us -> 22.5 us
  starting transfers between devices: 195 us -> 26.3 us
  local copies, waits for them, and re-layouts: 232 us -> 70.7 us
  other arithmetic: 122 us -> 48.3 us
  blocking collectives: 37.1 us -> 0 us
    pallas_call x0 -> x10, Pallas kernels: none -> 782 us  [the longest x6 450 us: gather_all(): pl.pallas_call(partial(gather_kernel, n, [(j + flip) % 2 == 1 for j in ra...]
    ppermute x168 -> x17, waiting for transfers between devices: 378 us -> 10.6 us  [small_sum(): return x + sum((lax.ppermute(sent, axis, r).astype(F32) for r in routes))]
    ppermute x168 -> x17, starting transfers between devices: 190 us -> 20.9 us  [small_sum(): return x + sum((lax.ppermute(sent, axis, r).astype(F32) for r in routes))]
    unnamed x304 -> x214, local copies, waits for them, and re-layouts: 127 us -> 45.3 us
    psum x7, waiting for transfers between devices: 91.2 us -> 10.4 us  [head_total(): return lax.psum(partial_sum, 'head').astype(F32)]
    concatenate x19 -> x0, local copies, waits for them, and re-layouts: 42.8 us -> none  [the longest x11 22.4 us: per_device(): gathered.append([jnp.concatenate(b, axis=0) for b in blocks])]
    psum x1 -> x0, blocking collectives: 37.1 us -> none  [per_device(): kernel_grad = lax.psum(kernel_grad.astype(BF), 'seq').astype(F32)]
    slice x24 -> x1, local copies, waits for them, and re-layouts: 30.7 us -> 0.07 us  [per_device(): out_part, kept_two = mlp_forward(resid_three, gains[3], ffn2)]
  transfers between devices with their start and end apart: 177 -> 26, of which waited for: 70 -> 11; matrix products, arithmetic and copies ran while one was open for 31% -> 3% of each run, Pallas kernels for 3% -> 56%
where the time goes in v2:
time: 1120 us
  Pallas kernels  820 us (73%)
  matrix products  111 us (10%)
  local copies, waits for them, and re-layouts  70.7 us (6%)
  other arithmetic  48.3 us (4%)
  starting transfers between devices  26.3 us (2%)
  waiting for transfers between devices  22.5 us (2%)
  between operations  15.7 us (1%)
    pallas_call x6, Pallas kernels, gather_all(): pl.pallas_call(partial(gather_kernel, n, [(j + flip) % 2 == 1 for j in ra...  450 us
    pallas_call x4, Pallas kernels, scatter_all(): pl.pallas_call(partial(scatter_kernel, n, [(j + flip) % 2 == 1 for j in r...  332 us
    dot_general x33, matrix products, dot(): lax.dot_general(a, b, (((ca,), (cb,)), ((), ())), preferred_element_type=...  111 us
    unnamed x214, local copies, waits for them, and re-layouts  45.3 us
    pallas_call x3, Pallas kernels, by_rows(): pl.pallas_call(kernel, grid=(rows,), in_specs=specs, out_specs=[pl.BlockS...  38.1 us
  transfers between devices with their start and end apart: 26, of which 11 were waited for; matrix products, arithmetic and copies ran while one was open for 3% of the time, Pallas kernels for 56%

profile of v2, /device:TPU:0, one launch (start us, length us, event | category | flops | bytes accessed | tf_op | source)
XLA Modules:
  0.0 1115.4 jit_solution(11263003021731061658)
XLA Ops:
  7.2 2.1 fusion.11
  16.3 45.5 %shard_map.305 = (bf16[1792,576]{1,0:T(8,128)(2,1)}, bf16[1792,448]{1,0:T(8,128)(2,1)}) custom-call(bf16[224,576]{1,0:T(8,128)(2,1)} %pad_maximum_fusion.6.refs_0_, bf16[224,448]{1,0:T(8,128)(2,1)} %bitcast.224), custom_call_target="tpu_custom_call" | custom-call | tf_op jit(solution)/shard_map/pallas_call | solution.py:123
  61.7 4.6 convolution_convert_fusion.16.refs_0_
  66.4 58.8 %shard_map.306 = bf16[4096,576]{1,0:T(8,128)(2,1)} custom-call(bf16[512,576]{1,0:T(8,128)(2,1)} %convolution_convert_fusion.16.refs_0_), custom_call_target="tpu_custom_call" | custom-call | tf_op jit(solution)/shard_map/pallas_call | solution.py:123
  125.1 2.9 copy.58
  128.6 2.4 slice.144.v_ref
  132.3 2.2 copy-done
  134.5 7.0 shard_map.307
  142.3 2.4 convolution_convert_fusion.14
  145.8 121.3 %shard_map.308 = (bf16[1792,1152]{1,0:T(8,128)(2,1)}, bf16[1792,1152]{1,0:T(8,128)(2,1)}, bf16[1792,1152]{1,0:T(8,128)(2,1)}) custom-call(bf16[224,1152]{1,0:T(8,128)(2,1)} %refs_0_, bf16[224,1152]{1,0:T(8,128)(2,1)} %refs_1_, bf16[224,1152]{1,0:T(8,128)(2,1)} %bitcast.228), custom_call_target="tpu_custom_call" | custom-call | tf_op jit(solution)/shard_map/pallas_call | solution.py:123
  267.2 2.9 multiply_reduce_fusion.8
  271.0 2.1 copy-done.83
  273.1 2.5 fusion.39
  275.7 4.0 multiply_convert_fusion.8
  280.8 3.8 convolution_convert_fusion.13
  285.0 54.5 %shard_map.309 = (bf16[1792,448]{1,0:T(8,128)(2,1)}, bf16[1792,448]{1,0:T(8,128)(2,1)}, bf16[1792,448]{1,0:T(8,128)(2,1)}) custom-call(bf16[224,448]{1,0:T(8,128)(2,1)} %refs_0_.1, bf16[224,448]{1,0:T(8,128)(2,1)} %refs_1_.1, bf16[224,448]{1,0:T(8,128)(2,1)} %bitcast.225), custom_call_target="tpu_custom_call" | custom-call | tf_op jit(solution)/shard_map/pallas_call | solution.py:123
  339.5 3.5 multiply_reduce_fusion.7
  346.1 2.0 fusion.40
  352.6 2.5 collective-permute-start
  362.0 2.0 multiply_convert_fusion.10
  364.8 2.4 convolution_convert_fusion.12
  367.7 119.6 %shard_map.310 = (bf16[1792,1152]{1,0:T(8,128)(2,1)}, bf16[1792,1152]{1,0:T(8,128)(2,1)}, bf16[1792,1152]{1,0:T(8,128)(2,1)}) custom-call(bf16[224,1152]{1,0:T(8,128)(2,1)} %refs_0_.2, bf16[224,1152]{1,0:T(8,128)(2,1)} %refs_1_.2, bf16[224,1152]{1,0:T(8,128)(2,1)} %bitcast.229), custom_call_target="tpu_custom_call" | custom-call | tf_op jit(solution)/shard_map/pallas_call | solution.py:123
  487.4 3.2 multiply_reduce_fusion.6
  494.0 2.5 fusion.41
  496.6 2.5 fusion.42
  499.3 4.1 multiply_convert_fusion.5
  503.4 2.6 fusion.43
  506.0 4.6 convolution_convert_fusion.5.refs_0_
  510.5 4.8 convolution_convert_fusion.4.refs_1_
  515.4 3.8 add_convert_fusion.3
  519.2 6.4 fusion.refs_2_
  525.6 119.9 %shard_map.311 = (f32[224,1152]{1,0:T(8,128)}, f32[224,1152]{1,0:T(8,128)}, f32[224,1152]{1,0:T(8,128)}) custom-call(bf16[1792,1152]{1,0:T(8,128)(2,1)} %convolution_convert_fusion.5.refs_0_, bf16[1792,1152]{1,0:T(8,128)(2,1)} %convolution_convert_fusion.4.refs_1_, bf16[1792,1152]{1,0:T(8,128)(2,1)} %fusion.refs_2_), custom_call_target="tpu_custom_call" | custom-call | tf_op jit(solution)/shard_map/pallas_call | solution.py:231
  653.1 2.5 convolution_convert_fusion.8.refs_2_
  655.6 2.0 multiply_reduce_fusion.11
  660.9 4.0 convolution_convert_fusion.9.refs_1_
  670.4 2.1 pad_maximum_fusion.3
  674.0 2.4 convolution_convert_fusion.10.refs_0_
  678.1 2.4 add_convert_fusion.1
  681.0 54.1 %shard_map.312 = (f32[224,448]{1,0:T(8,128)}, f32[224,448]{1,0:T(8,128)}, f32[224,448]{1,0:T(8,128)}) custom-call(bf16[1792,448]{1,0:T(8,128)(2,1)} %convolution_convert_fusion.10.refs_0_, bf16[1792,448]{1,0:T(8,128)(2,1)} %convolution_convert_fusion.9.refs_1_, bf16[1792,448]{1,0:T(8,128)(2,1)} %convolution_convert_fusion.8.refs_2_), custom_call_target="tpu_custom_call" | custom-call | tf_op jit(solution)/shard_map/pallas_call | solution.py:231
  740.6 2.3 copy-done.86
  744.0 4.8 multiply_convert_fusion.3
  748.9 2.6 fusion.45
  751.5 4.7 convolution_convert_fusion.2.refs_0_
  756.1 4.8 convolution_convert_fusion.refs_2_
  760.9 4.5 convolution_convert_fusion.1.refs_1_
  765.5 3.9 add_convert_fusion
  769.5 6.3 convolution_convert_fusion.11
  775.8 122.5 %shard_map.313 = (f32[224,1152]{1,0:T(8,128)}, f32[224,1152]{1,0:T(8,128)}, f32[224,1152]{1,0:T(8,128)}) custom-call(bf16[1792,1152]{1,0:T(8,128)(2,1)} %convolution_convert_fusion.2.refs_0_, bf16[1792,1152]{1,0:T(8,128)(2,1)} %convolution_convert_fusion.1.refs_1_, bf16[1792,1152]{1,0:T(8,128)(2,1)} %convolution_convert_fusion.refs_2_), custom_call_target="tpu_custom_call" | custom-call | tf_op jit(solution)/shard_map/pallas_call | solution.py:231
  906.4 15.6 %shard_map.314 = (bf16[4,128,64]{2,1,0:T(8,128)(2,1)S(1)}, bf16[4,128,448]{2,1,0:T(8,128)(2,1)S(1)}, bf16[4,128,64]{2,1,0:T(8,128)(2,1)S(1)}) custom-call(s32[5]{0:T(128)S(1)} %copy-done.6, s32[1,1024]{1,0:T(1,128)S(1)} %iota.15.place_ref, bf16[4,128,64]{2,1,0:T(8,128)(2,1)S(1)} %copy-done.4, bf16[4,1024,64]{2,1,0:T(8,128)(2,1)S(1)} %get-tuple-element.180.k_ref, ...), custom_call_target="tpu_custom_call" | custom-call | tf_op jit(solution)/shard_map/pallas_call | solution.py:362
  922.9 50.8 %shard_map.315 = bf16[4096,512]{1,0:T(8,128)(2,1)} custom-call(bf16[512,512]{1,0:T(8,128)(2,1)} %bitcast.217), custom_call_target="tpu_custom_call" | custom-call | tf_op jit(solution)/shard_map/pallas_call | solution.py:123
  973.8 2.6 copy.72
  978.4 15.5 %shard_map.316 = (bf16[4,128,64]{2,1,0:T(8,128)(2,1)S(1)}, bf16[4,128,448]{2,1,0:T(8,128)(2,1)S(1)}) custom-call(s32[5]{0:T(128)S(1)} %copy-done.6, s32[1,1024]{1,0:T(1,128)S(1)} %iota.16.place_ref, bf16[4,128,64]{2,1,0:T(8,128)(2,1)S(1)} %get-tuple-element.187.k_ref, bf16[4,128,448]{2,1,0:T(8,128)(2,1)S(1)} %slice.163.v_ref, ...), custom_call_target="tpu_custom_call" | custom-call | tf_op jit(solution)/shard_map/pallas_call | solution.py:362
  994.1 2.9 convolution_convert_fusion.15
  998.7 2.3 collective-permute-start.7
  1001.1 2.6 collective-permute-start.5
  1013.6 4.7 convolution_convert_fusion.6.refs_0_
  1018.3 2.4 convolution_convert_fusion.7.refs_1_
  1020.7 35.4 %shard_map.317 = (f32[224,576]{1,0:T(8,128)}, f32[224,448]{1,0:T(8,128)}) custom-call(bf16[1792,576]{1,0:T(8,128)(2,1)} %convolution_convert_fusion.6.refs_0_, bf16[1792,448]{1,0:T(8,128)(2,1)} %convolution_convert_fusion.7.refs_1_), custom_call_target="tpu_custom_call" | custom-call | tf_op jit(solution)/shard_map/pallas_call | solution.py:231
  1062.4 10.3 all-reduce.21.cloned.1.call-done
  1078.0 2.3 collective-permute-done.10
  1081.0 4.3 collective-permute-start.18
  1085.9 2.9 fusion.9
  1088.7 2.9 collective-permute-start.15
  1091.7 2.0 collective-permute-start.13
  (337 shorter events, 108.7 us)
Async XLA Ops:
  7.2 6.6 copy-start.7
  7.2 259.9 %all-reduce.9.cloned.1.call-start = ((), (), s32[]{:S(2)}) async-start(), calls=%async_computation | async-start | bytes 3670016 | tf_op jit(solution)/shard_map/psum | solution.py:390
  9.3 6.1 copy-start.67
  9.3 6.9 copy-start.72
  10.2 6.1 copy-start.68
  10.2 259.9 %copy-start.70 = (f32[1792]{0:T(1024)}, f32[1792]{0:T(1024)S(1)}, u32[]{:S(2)}) copy-start(f32[1792]{0:T(1024)S(1)} %get-tuple-element.168) | copy-start | bytes 21508
  132.2 9.3 copy-start.3
  132.3 9.2 copy-start.5
  134.5 7.9 copy-start.91
  144.7 194.8 %all-reduce.11.cloned.1.call-start = ((), (), s32[]{:S(2)}) async-start(), calls=%async_computation.1 | async-start | bytes 3670016 | tf_op jit(solution)/shard_map/psum | solution.py:390
  267.2 3.1 copy-start.19
  271.0 4.7 copy-start.50
  275.7 4.0 copy-start.96
  275.7 5.1 copy-start.85
  284.6 202.7 %all-reduce.13.cloned.1.call-start = ((), (), s32[]{:S(2)}) async-start(), calls=%async_computation.2 | async-start | bytes 3670016 | tf_op jit(solution)/shard_map/psum | solution.py:390
  343.1 3.1 copy-start.54
  348.1 7.0 copy-start.80
  352.6 3.9 collective-permute-start
  360.9 3.1 copy-start.29
  367.2 278.4 %all-reduce.15.cloned.1.call-start = ((), (), s32[]{:S(2)}) async-start(), calls=%async_computation.3 | async-start | bytes 3670016 | tf_op jit(solution)/shard_map/psum | solution.py:390
  490.5 3.5 copy-start.89
  525.6 209.6 %all-reduce.17.cloned.1.call-start = ((), (), s32[]{:S(2)}) async-start(), calls=%async_computation.4 | async-start | bytes 3670016 | tf_op jit(solution)/shard_map/psum | solution.py:390
  659.4 8.4 collective-permute-start.1
  667.8 4.7 copy-start.41
  680.5 217.9 %all-reduce.19.cloned.1.call-start = ((), (), s32[]{:S(2)}) async-start(), calls=%async_computation.5 | async-start | bytes 3670016 | tf_op jit(solution)/shard_map/psum | solution.py:390
  739.8 3.2 copy-start.86
  739.8 4.2 copy-start.97
  740.6 15.5 %copy-start.25 = (f32[512,1792]{1,0:T(8,128)}, f32[512,1792]{1,0:T(8,128)S(1)}, u32[]{:S(2)}) copy-start(f32[512,1792]{1,0:T(8,128)S(1)} %multiply_add_fusion.1) | copy-start | bytes 11010052
  744.0 4.8 copy-start.84
  751.4 4.7 copy-start.95
  760.9 4.5 copy-start.82
  765.5 4.0 copy-start.44
  769.4 303.4 %all-reduce.21.cloned.1.call-start = ((), (), s32[]{:S(2)}) async-start(), calls=%async_computation.6 | async-start | bytes 7340032 | tf_op jit(solution)/shard_map/psum | solution.py:390
  978.4 15.7 %copy-start.90 = (bf16[1792,576]{1,0:T(8,128)(2,1)S(1)}, bf16[1792,576]{1,0:T(8,128)(2,1)}, u32[]{:S(2)}) copy-start(bf16[1792,576]{1,0:T(8,128)(2,1)} %get-tuple-element.69) | copy-start | bytes 6193156
  997.0 9.5 copy-start.10
  997.0 9.5 copy-start.69
  997.0 9.5 copy-start.73
  997.1 15.6 %copy-start.65 = (f32[224,448]{1,0:T(8,128)S(1)}, f32[224,448]{1,0:T(8,128)}, u32[]{:S(2)}) copy-start(f32[224,448]{1,0:T(8,128)} %get-tuple-element.102) | copy-start | bytes 1204228
  997.1 16.5 %copy-start.74 = (f32[1792]{0:T(1024)S(1)}, f32[1792]{0:T(1024)}, u32[]{:S(2)}) copy-start(f32[1792]{0:T(1024)} %get-tuple-element.155) | copy-start | bytes 21508
  997.7 7.0 collective-permute-start.8
  998.7 6.7 collective-permute-start.7
  1001.1 7.2 collective-permute-start.6
  1001.1 7.2 collective-permute-start.5
  1003.7 5.4 collective-permute-start.4
  1004.7 5.4 collective-permute-start.3
  1005.5 6.5 collective-permute-start.2
  1013.6 4.7 copy-start.2
  1013.6 4.7 copy-start.22
  1075.4 10.5 copy-start.23
  1076.5 1.5 collective-permute-start.11
  1076.7 3.6 collective-permute-start.10
  1077.9 3.0 collective-permute-start.9
  1081.0 13.6 %copy-start.47 = (bf16[512,1792]{1,0:T(8,128)(2,1)S(1)}, bf16[512,1792]{1,0:T(8,128)(2,1)}, u32[]{:S(2)}) copy-start(bf16[512,1792]{1,0:T(8,128)(2,1)} %get-tuple-element.170) | copy-start | bytes 5505028
  1081.0 10.7 collective-permute-start.18
  1085.3 8.4 collective-permute-start.17
  1085.9 8.8 copy-start.14
  1088.7 7.5 collective-permute-start.16
  1088.7 7.5 collective-permute-start.15
  1091.7 5.5 collective-permute-start.14
  1091.7 6.6 collective-permute-start.13
  1093.7 6.4 collective-permute-start.12
  1094.6 6.1 copy-start.62
  1096.2 5.5 copy-start.61
  1096.2 6.4 copy-start.60
  (60 other events, 124.4 us)
Sparse Core Ops, SparseCore 0:
  144.8 46.1 all-reduce.8
  284.8 46.4 all-reduce.10
  367.4 47.8 all-reduce.12
  525.7 47.2 all-reduce.14
  680.6 49.2 all-reduce.16
  769.5 45.5 all-reduce.18
  997.2 75.5 all-reduce.20

commit v3 on v2

--- a/solution.py
+++ b/solution.py
@@ -42,35 +42,29 @@
 
 
 class GatherRing:
-    def __init__(self, n, where, src, out, send, recv, flip):
-        self.n, self.src, self.out, self.send, self.recv = n, src, out, send, recv
+    def __init__(self, n, where, src, out, place, send, recv, local, flip):
+        self.n, self.src, self.out, self.place = n, src, out, place
+        self.send, self.recv, self.local = send, recv, local
         self.pos, self.right, self.left = where
-        self.height = src.shape[0]
-        self.started = []
         self.flip = flip
         self.steps = n // 2
         self.done = 0
 
-    def rows(self, r):
-        owner = ring_device(lax.rem(self.pos + (r % self.n), self.n))
-        return pl.ds(pl.multiple_of(owner * self.height, 32), self.height)
+    def block(self, r):
+        return self.place(self.out, ring_device(lax.rem(self.pos + (r % self.n), self.n)))
 
     def copy(self, k, d):
-        rows = self.rows(-d * (k - 1))
+        block = self.block(-d * (k - 1))
         i = 0 if d == 1 else 1
         return pltpu.make_async_remote_copy(
-            src_ref=self.src if k == 1 else self.out.at[rows],
-            dst_ref=self.out.at[rows],
+            src_ref=self.src if k == 1 else block,
+            dst_ref=block,
             send_sem=self.send.at[i, k - 1],
             recv_sem=self.recv.at[i, k - 1],
             device_id={"seq": self.right if d == 1 else self.left},
             device_id_type=MESH,
         )
 
-    def begin(self, local):
-        self.own = pltpu.make_async_copy(self.src, self.out.at[self.rows(0)], local)
-        self.own.start()
-
     def ways(self, k):
         if k <= (self.n - 1) // 2:
             return (1, -1)
@@ -79,6 +73,8 @@
     def step(self):
         if self.done == self.steps:
             return
+        if self.done == 0:
+            pltpu.make_async_copy(self.src, self.block(0), self.local).start()
         self.done += 1
         k = self.done
         for d in self.ways(k):
@@ -89,7 +85,7 @@
     def finish(self):
         while self.done < self.steps:
             self.step()
-        self.own.wait()
+        pltpu.make_async_copy(self.src, self.block(0), self.local).wait()
         last = {d: max(k for k in range(1, self.steps + 1) if d in self.ways(k)) for d in (1, -1)}
         for d in (1, -1):
             self.copy(last[d], d).wait_recv()
@@ -98,67 +94,162 @@
                 self.copy(k, d).wait_send()
 
 
-def gather_kernel(n, flips, *refs):
-    count = len(flips)
-    srcs, outs, sems = refs[:count], refs[count : 2 * count], refs[2 * count :]
-    send, recv, local = sems
-    where = greet(n)
-    rings = [
-        GatherRing(n, where, srcs[j], outs[j], send.at[j], recv.at[j], flips[j]) for j in range(count)
-    ]
-    for j, ring in enumerate(rings):
-        ring.begin(local.at[j])
-    for _ in range(n // 2):
-        for ring in rings:
-            ring.step()
-    for ring in rings:
-        ring.finish()
+def by_block(height):
+    return lambda ref, owner: ref.at[pl.ds(pl.multiple_of(owner * height, min(height, 32)), height)]
+
+
+def by_position(tok):
+    return lambda ref, owner: ref.at[:, pl.ds(pl.multiple_of(owner * tok, 16), tok)]
+
+
+VMEM = pltpu.VMEM
+MIB = 1024 * 1024
+
+
+class Call:
+    def __init__(self, call_id):
+        self.n = lax.axis_size("seq")
+        self.call_id = call_id
+        self.ins, self.outs, self.scratch = {}, {}, {}
+        self.gathers, self.scatters = {}, {}
+
+    def take(self, name, array, space=VMEM):
+        self.ins[name] = (array, pl.BlockSpec(memory_space=space))
+        return name
+
+    def give(self, name, shape, kind, space=VMEM):
+        self.outs[name] = (jax.ShapeDtypeStruct(shape, kind), pl.BlockSpec(memory_space=space))
+        return name
+
+    def hold(self, name, shape, kind):
+        self.scratch[name] = VMEM(shape, kind)
+        return name
+
+    def sems(self, name, *shape):
+        self.scratch[name] = pltpu.SemaphoreType.DMA(shape)
+
+    def gather(self, name, src, out, place, flip=False):
+        half = self.n // 2
+        self.sems(name + ".send", 2, half)
+        self.sems(name + ".recv", 2, half)
+        self.sems(name + ".local", 1)
+        self.gathers[name] = (src, out, place, flip)
+
+    def left(self, name, array):
+        self.take(name, array)
+        rows, width = array.shape
+        self.hold(name + ".blocked", (self.n, rows, width // self.n), BF)
+
+    def scatter(self, name, left, right, flip=False):
+        n = self.n
+        height = self.ins[left][0].shape[1] // n
+        block = (height, right.shape[1])
+        self.take(name + ".right", right)
+        self.give(name, block, F32)
+        self.hold(name + ".sums", (2, n // 2) + block, BF)
+        self.hold(name + ".slots", (2, n // 2) + block, BF)
+        self.sems(name + ".send", 2, n // 2)
+        self.sems(name + ".recv", 2, n // 2)
+        self.scatters[name] = (left, flip)
+
+    def kernel(self, body, *refs):
+        names = list(self.ins) + list(self.outs) + list(self.scratch)
+        at = dict(zip(names, refs))
+        where = greet(self.n)
+        rings = {}
+        for name, (src, out, place, flip) in self.gathers.items():
+            rings[name] = GatherRing(
+                self.n,
+                where,
+                at[src],
+                at[out],
+                place,
+                at[name + ".send"],
+                at[name + ".recv"],
+                at[name + ".local"].at[0],
+                flip,
+            )
+        ready = set()
+        for name, (left, flip) in self.scatters.items():
+            blocked = at[left + ".blocked"]
+            if left not in ready:
+                ready.add(left)
+                width = blocked.shape[2]
+                for b in range(self.n):
+                    blocked[b] = at[left][:, b * width : (b + 1) * width]
+            rings[name] = ScatterRing(
+                self.n,
+                where,
+                blocked,
+                at[name + ".right"],
+                at[name],
+                at[name + ".sums"],
+                at[name + ".slots"],
+                at[name + ".send"],
+                at[name + ".recv"],
+                flip,
+            )
+            rings[name].step()
+        body(at, rings)
+        for ring in rings.values():
+            ring.finish()
+
+    def run(self, body):
+        outs = pl.pallas_call(
+            partial(self.kernel, body),
+            in_specs=[spec for _, spec in self.ins.values()],
+            out_specs=[spec for _, spec in self.outs.values()],
+            out_shape=[shape for shape, _ in self.outs.values()],
+            scratch_shapes=list(self.scratch.values()),
+            compiler_params=pltpu.CompilerParams(
+                collective_id=self.call_id, has_side_effects=True, vmem_limit_bytes=58 * MIB
+            ),
+        )(*[array for array, _ in self.ins.values()])
+        return dict(zip(self.outs, outs))
+
+
+def in_turn(n):
+    def body(at, rings):
+        for _ in range(n // 2):
+            for ring in rings.values():
+                ring.step()
+
+    return body
 
 
 def gather_all(arrays, call_id, flip=0):
     n = lax.axis_size("seq")
     if not ring_size(n):
         return [lax.all_gather(a, "seq", axis=0, tiled=True) for a in arrays]
-    count = len(arrays)
-    return pl.pallas_call(
-        partial(gather_kernel, n, [(j + flip) % 2 == 1 for j in range(count)]),
-        in_specs=[ANY] * count,
-        out_specs=[ANY] * count,
-        out_shape=[jax.ShapeDtypeStruct((n * a.shape[0], a.shape[1]), a.dtype) for a in arrays],
-        scratch_shapes=[
-            pltpu.SemaphoreType.DMA((count, 2, n // 2)),
-            pltpu.SemaphoreType.DMA((count, 2, n // 2)),
-            pltpu.SemaphoreType.DMA((count,)),
-        ],
-        compiler_params=pltpu.CompilerParams(collective_id=call_id, has_side_effects=True),
-    )(*arrays)
+    call = Call(call_id)
+    names = [str(j) for j in range(len(arrays))]
+    for j, (name, a) in enumerate(zip(names, arrays)):
+        call.take(name + ".src", a, pl.ANY)
+        call.give(name, (n * a.shape[0],) + a.shape[1:], a.dtype, pl.ANY)
+        call.gather(name, name + ".src", name, by_block(a.shape[0]), (j + flip) % 2 == 1)
+    out = call.run(in_turn(n))
+    return [out[name] for name in names]
 
 
 class ScatterRing:
-    def __init__(self, n, where, full, out, terms, slots, send, recv, load, flip):
-        self.n, self.full, self.out, self.terms, self.slots = n, full, out, terms, slots
-        self.send, self.recv, self.load = send, recv, load
+    def __init__(self, n, where, left, right, out, sums, slots, send, recv, flip):
+        self.n, self.left_ref, self.right_ref, self.out = n, left, right, out
+        self.sums, self.slots, self.send, self.recv = sums, slots, send, recv
         self.pos, self.right, self.left = where
-        self.height = out.shape[0]
         d = -1 if flip else 1
         self.hops = {d: n // 2, -d: (n - 1) // 2}
         self.order = (d, -d)
         self.done = 0
         self.steps = n // 2
 
-    def source(self, r):
+    def term(self, r):
         owner = ring_device(lax.rem(self.pos + (r % self.n), self.n))
-        return self.full.at[pl.ds(pl.multiple_of(owner * self.height, 32), self.height)]
-
-    def term(self, d, h):
-        r = d * (self.hops[d] - h)
-        return pltpu.make_async_copy(self.source(r), self.terms.at[r % self.n], self.load.at[r % self.n])
+        return dot(self.left_ref[owner], self.right_ref[...], 0, 0)
 
     def copy(self, d, h):
         i = 0 if d == 1 else 1
-        r = d * (self.hops[d] - h + 1)
         return pltpu.make_async_remote_copy(
-            src_ref=self.source(r) if h == 1 else self.terms.at[r % self.n],
+            src_ref=self.sums.at[i, h - 1],
             dst_ref=self.slots.at[i, h - 1],
             send_sem=self.send.at[i, h - 1],
             recv_sem=self.recv.at[i, h - 1],
@@ -174,24 +265,18 @@
         for d in self.order:
             if h > self.hops[d]:
                 continue
+            i = 0 if d == 1 else 1
+            total = self.term(d * (self.hops[d] - h + 1))
             if h > 1:
                 self.copy(d, h - 1).wait_recv()
-                self.term(d, h - 1).wait()
-                i, r = (0 if d == 1 else 1), (d * (self.hops[d] - h + 1)) % self.n
-                total = self.slots[i, h - 2].astype(F32) + self.terms[r].astype(F32)
-                self.terms[r] = total.astype(BF)
+                total = total + self.slots[i, h - 2].astype(F32)
+            self.sums[i, h - 1] = total.astype(BF)
             self.copy(d, h).start()
-            if h < self.hops[d]:
-                self.term(d, h).start()
-        if h == 1:
-            self.own = pltpu.make_async_copy(self.source(0), self.terms.at[0], self.load.at[0])
-            self.own.start()
 
     def finish(self):
         while self.done < self.steps:
             self.step()
-        self.own.wait()
-        total = self.terms[0].astype(F32)
+        total = self.term(0)
         for d in self.order:
             i, h = (0 if d == 1 else 1), self.hops[d]
             self.copy(d, h).wait_recv()
@@ -202,48 +287,40 @@
                 self.copy(d, h).wait_send()
 
 
-def scatter_kernel(n, flips, *refs):
-    count = len(flips)
-    fulls, outs, rest = refs[:count], refs[count : 2 * count], refs[2 * count :]
-    terms, slots, (send, recv, load) = rest[:count], rest[count : 2 * count], rest[2 * count :]
-    where = greet(n)
-    rings = [
-        ScatterRing(
-            n, where, fulls[j], outs[j], terms[j], slots[j], send.at[j], recv.at[j], load.at[j], flips[j]
-        )
-        for j in range(count)
-    ]
-    for _ in range(n // 2):
-        for ring in rings:
-            ring.step()
-    for ring in rings:
-        ring.finish()
-
-
-def scatter_all(fulls, call_id, flip=0):
+def scatter_all(lefts, pairs, call_id, flip=0, small=None):
     n = lax.axis_size("seq")
     if not ring_size(n):
-        return [
-            lax.psum_scatter(g, "seq", scatter_dimension=0, tiled=True).astype(F32) for g in fulls
+        sums = [
+            lax.psum_scatter(
+                dot(lefts[i], right, 0, 0).astype(BF), "seq", scatter_dimension=0, tiled=True
+            ).astype(F32)
+            for i, right in pairs
         ]
-    count = len(fulls)
-    blocks = [(g.shape[0] // n, g.shape[1]) for g in fulls]
-    return pl.pallas_call(
-        partial(scatter_kernel, n, [(j + flip) % 2 == 1 for j in range(count)]),
-        in_specs=[ANY] * count,
-        out_specs=[pl.BlockSpec(memory_space=pltpu.VMEM)] * count,
-        out_shape=[jax.ShapeDtypeStruct(b, F32) for b in blocks],
-        scratch_shapes=[pltpu.VMEM((n,) + b, BF) for b in blocks]
-        + [pltpu.VMEM((2, n // 2) + b, BF) for b in blocks]
-        + [
-            pltpu.SemaphoreType.DMA((count, 2, n // 2)),
-            pltpu.SemaphoreType.DMA((count, 2, n // 2)),
-            pltpu.SemaphoreType.DMA((count, n)),
-        ],
-        compiler_params=pltpu.CompilerParams(
-            collective_id=call_id, has_side_effects=True, vmem_limit_bytes=56 * 1024 * 1024
-        ),
-    )(*fulls)
+        return sums if small is None else sums + [lax.psum(small.astype(BF), "seq").astype(F32)]
+    call = Call(call_id)
+    names = [str(j) for j in range(len(pairs))]
+    if small is not None:
+        call.take("small.src", small)
+        call.hold("small.all", (n * small.shape[0], small.shape[1]), F32)
+        call.gather("small", "small.src", "small.all", by_block(small.shape[0]))
+    for i, a in enumerate(lefts):
+        call.left(f"left{i}", a)
+    for j, (i, right) in enumerate(pairs):
+        call.scatter(names[j], f"left{i}", right, (j + flip) % 2 == 1)
+    if small is not None:
+        names.append(call.give("small.sum", small.shape, F32))
+
+    def body(at, rings):
+        in_turn(n)(at, rings)
+        if small is not None:
+            rings["small"].finish()
+            rows = small.shape[0]
+            blocks = [at["small.all"][b * rows : (b + 1) * rows] for b in range(n)]
+            at["small.sum"][...] = sum(blocks[1:], blocks[0])
+            del rings["small"]
+
+    out = call.run(body)
+    return [out[name] for name in names]
 
 
 def small_sum(x, axis):
@@ -272,16 +349,16 @@
     ]
 
 
-def query_mask(scal_ref, place_ref, tok):
-    offset = scal_ref[1 + pl.program_id(0)]
+def query_mask(scal_ref, place_ref, tok, row):
+    offset = scal_ref[1 + row]
     pos = scal_ref[0] + lax.broadcasted_iota(jnp.int32, (tok, 1), 0)
     low = jnp.where(pos >= offset, offset, 0)
     other = place_ref[...]
     return (other >= low) & (other <= pos)
 
 
-def key_mask(scal_ref, place_ref, tok):
-    offset = scal_ref[1 + pl.program_id(0)]
+def key_mask(scal_ref, place_ref, tok, row):
+    offset = scal_ref[1 + row]
     pos = scal_ref[0] + lax.broadcasted_iota(jnp.int32, (tok, 1), 0)
     high = jnp.where(pos >= offset, jnp.int32(1 << 30), offset)
     other = place_ref[...]
@@ -290,7 +367,7 @@
 
 def attend_kernel(scal_ref, place_ref, q_ref, k_ref, v_ref, out_ref):
     q, k, v = q_ref[0], k_ref[0], v_ref[0]
-    mask = query_mask(scal_ref, place_ref, q.shape[0])
+    mask = query_mask(scal_ref, place_ref, q.shape[0], pl.program_id(0))
     total = jnp.zeros((q.shape[0], v.shape[1]), F32)
     for in_q, in_v in head_masks(q.shape[1], v.shape[1]):
         s = dot(jnp.where(in_q, q, jnp.zeros_like(q)), k, 1, 1) * (QK**-0.5)
@@ -304,7 +381,7 @@
     q, k, v = q_ref[0], k_ref[0], v_ref[0]
     da = da_ref[0]
     tok = q.shape[0]
-    mask = query_mask(scal_ref, place_ref, tok)
+    mask = query_mask(scal_ref, place_ref, tok, pl.program_id(0))
     lane = lax.broadcasted_iota(jnp.int32, (1, q.shape[1]), 1)
     heads = q.shape[1] // QK
     dq = jnp.zeros(q.shape, F32)
@@ -334,7 +411,7 @@
     k, v = k_ref[0], v_ref[0]
     q, dan, extra = q_ref[0], dan_ref[0], extra_ref[0]
     tok = k.shape[0]
-    mask = key_mask(scal_ref, place_ref, tok)
+    mask = key_mask(scal_ref, place_ref, tok, pl.program_id(0))
     lane = lax.broadcasted_iota(jnp.int32, (tok, k.shape[1]), 1)
     heads = k.shape[1] // QK
     dk = jnp.zeros(k.shape, F32)
@@ -349,6 +426,95 @@
         dk = dk + jnp.where(in_q, dot(ds, q, 1, 0) * (QK**-0.5), 0.0)
     dk_ref[0] = dk.astype(BF)
     dv_ref[0] = dv.astype(BF)
+
+
+def attend_back(scal, place, q, k, v, qkv_all, da, scatters, call_id):
+    n = lax.axis_size("seq")
+    rows, tok, vw = v.shape
+    qkw = q.shape[-1]
+    call = Call(call_id)
+    call.take("scal", scal, pltpu.SMEM)
+    for name, a in (("place", place), ("q", q), ("k", k), ("v", v), ("all", qkv_all), ("da", da)):
+        call.take(name, a)
+    lefts, pairs = scatters
+    for i, a in enumerate(lefts):
+        call.left(f"left{i}", a)
+    for j, (i, right) in enumerate(pairs):
+        call.scatter(f"s{j}", f"left{i}", right, j % 2 == 1)
+    call.give("dqk", (rows, tok, qkw), BF)
+    call.give("dv", (rows, tok, vw), BF)
+    call.hold("dq", (rows, tok, qkw), F32)
+    call.hold("back", (rows, tok, qkw + vw), BF)
+    call.hold("back_all", (rows, n * tok, qkw + vw), BF)
+    call.gather("g", "back", "back_all", by_position(tok), True)
+    heads = qkw // 2 // QK
+
+    def body(at, rings):
+        lane = lax.broadcasted_iota(jnp.int32, (1, qkw), 1)
+        masks = head_masks(qkw // 2, vw)
+        far = [(lane >= qkw // 2 + h * QK) & (lane < qkw // 2 + (h + 1) * QK) for h in range(heads)]
+        near = [(lane >= h * QK) & (lane < (h + 1) * QK) for h in range(heads)]
+
+        def query_side(r, carry):
+            q, da = at["q"][r], at["da"][r]
+            qk, v = at["all"][r, :, :qkw], at["all"][r, :, qkw:]
+            mask = query_mask(at["scal"], at["place"], tok, r)
+            dq = jnp.zeros((tok, qkw), F32)
+            dan_all = jnp.zeros((tok, vw), F32)
+            extra = jnp.zeros((tok, qkw), F32)
+            for h in range(heads):
+                in_v = masks[h][1]
+                s = dot(jnp.where(far[h], q, jnp.zeros_like(q)), qk, 1, 1) * (QK**-0.5)
+                w = jnp.where(mask, 1.0 + s + 0.5 * s * s, 0.0)
+                den = jnp.sum(w, axis=1, keepdims=True)
+                att = dot(w.astype(BF), v, 1, 0) / den
+                dan = jnp.where(in_v, da / den, 0.0).astype(BF)
+                dan_f = dan.astype(F32)
+                delta = jnp.sum(dan_f * att, axis=1, keepdims=True)
+                ds = jnp.where(mask, (dot(dan, v, 1, 1) - delta) * (1.0 + s), 0.0).astype(BF)
+                dq = dq + jnp.where(far[h], dot(ds, qk, 1, 0) * (QK**-0.5), 0.0)
+                dan_all = dan_all + dan_f
+                high = delta.astype(BF).astype(F32)
+                extra = extra + jnp.where(lane == h, high, 0.0)
+                extra = extra + jnp.where(lane == heads + h, delta - high, 0.0)
+            at["dq"][r] = dq
+            at["back"][r, :, :qkw] = extra.astype(BF)
+            at["back"][r, :, qkw:] = dan_all.astype(BF)
+            return carry
+
+        def key_side(r, carry):
+            k, v = at["k"][r], at["v"][r]
+            qk = at["all"][r, :, :qkw]
+            extra, dan = at["back_all"][r, :, :qkw], at["back_all"][r, :, qkw:]
+            mask = key_mask(at["scal"], at["place"], tok, r)
+            wide = lax.broadcasted_iota(jnp.int32, (tok, qkw), 1)
+            dqk = at["dq"][r]
+            dv = jnp.zeros((tok, vw), F32)
+            for h in range(heads):
+                in_v = masks[h][1]
+                s = dot(jnp.where(near[h], k, jnp.zeros_like(k)), qk, 1, 1) * (QK**-0.5)
+                w = jnp.where(mask, 1.0 + s + 0.5 * s * s, 0.0).astype(BF)
+                dv = dv + jnp.where(in_v, dot(w, dan, 1, 0), 0.0)
+                pick = jnp.where((wide == h) | (wide == heads + h), 1.0, 0.0).astype(BF)
+                d_kernel = dot(jnp.where(in_v, v, jnp.zeros_like(v)), dan, 1, 1) - dot(pick, extra, 1, 1)
+                ds = jnp.where(mask, d_kernel * (1.0 + s), 0.0).astype(BF)
+                dqk = dqk + jnp.where(near[h], dot(ds, qk, 1, 0) * (QK**-0.5), 0.0)
+            at["dqk"][r] = dqk.astype(BF)
+            at["dv"][r] = dv.astype(BF)
+            return carry
+
+        lax.fori_loop(0, rows, query_side, 0)
+        others = [ring for name, ring in rings.items() if name != "g"]
+        for _ in range(n // 2):
+            rings["g"].step()
+            for ring in others:
+                ring.step()
+        rings["g"].finish()
+        del rings["g"]
+        lax.fori_loop(0, rows, key_side, 0)
+
+    out = call.run(body)
+    return out["dqk"], out["dv"], [out[f"s{j}"] for j in range(len(pairs))]
 
 
 def by_rows(kernel, scal, place, operands, widths, kinds):
@@ -403,6 +569,12 @@
     return dot(hidden, down_t, 1, 1).astype(BF), (normed, gate_val, up_val, hidden)
 
 
+def mlp_scatter(kept, call_id, *others):
+    (normed, grad_b), d_gate, d_up, hidden = kept
+    normed, grad_b = tie((normed, grad_b), *others)
+    return scatter_all((normed, grad_b), ((0, d_gate), (0, d_up), (1, hidden)), call_id)
+
+
 def mlp_backward(grad_b, saved, weights):
     gate_w, up_w, down_t = weights
     normed, gate_val, up_val, hidden = saved
@@ -412,10 +584,7 @@
     d_gate = (dh * up_val * (sig * (1.0 + gate_val * (1.0 - sig)))).astype(BF)
     d_up = (dh * silu).astype(BF)
     dn_part = (dot(d_gate, gate_w, 1, 1) + dot(d_up, up_w, 1, 1)).astype(BF)
-    gate_grad = dot(normed, d_gate, 0, 0).astype(BF)
-    up_grad = dot(normed, d_up, 0, 0).astype(BF)
-    down_grad = dot(grad_b, hidden, 0, 0).astype(BF)
-    return dn_part, (gate_grad, up_grad, down_grad)
+    return dn_part, ((normed, grad_b), d_gate, d_up, hidden)
 
 
 def shifted(block, before, shift):
@@ -517,14 +686,13 @@
 
     dn_part, grads_two = mlp_backward(grad_four, kept_two, ffn2)
     dn = head_total(dn_part)
-    sums_two = scatter_all(tie(grads_two, dn_part), 5)
+    sums_two = mlp_scatter(grads_two, 5, dn_part)
     (dn,) = tie((dn,), *sums_two)
     out_sum = head_total(tie((out_part,), *sums_two)[0])
     block_output = (resid_three + out_sum).astype(BF).reshape(activations.shape)
     dx, gain_four = rms_back(resid_three, gains[3], dn)
     grad_three = grad_four.astype(F32) + dx
     grad_b = grad_three.astype(BF)
-    conv_out_grad = dot(grad_b, product, 0, 0).astype(BF)
     d_product = dot(grad_b, conv_out_t, 1, 0).reshape(rows, tok, cw)
     d_gate_c = (d_product * conv).astype(BF).reshape(count, cw)
     d_conv = d_product * gate_c
@@ -535,58 +703,86 @@
     )
     d_inner = d_inner.astype(BF).reshape(count, cw)
     kernel_grad = jnp.stack([jnp.sum(d_conv * moved[t], axis=(0, 1)) for t in range(taps)])
-    conv_in_grad = dot(normed_c, d_inner, 0, 0).astype(BF)
-    conv_gate_grad = dot(normed_c, d_gate_c, 0, 0).astype(BF)
     dn_part = (dot(d_inner, inner_w, 1, 1) + dot(d_gate_c, gate_w, 1, 1)).astype(BF)
     dn = head_total(dn_part)
-    sums_conv = scatter_all(tie((conv_in_grad, conv_gate_grad, conv_out_grad), dn_part), 6, 1)
+    sums_conv = scatter_all(
+        tie((normed_c, grad_b), dn_part), ((0, d_inner), (0, d_gate_c), (1, product)), 6, 1
+    )
     (dn,) = tie((dn,), *sums_conv)
     dx, gain_three = rms_back(resid_two, gains[2], dn)
     grad_two = grad_three + dx
     dn_part, grads_one = mlp_backward(grad_two.astype(BF), kept_one, ffn1)
     dn = head_total(dn_part)
-    sums_one = scatter_all(tie(grads_one, dn_part), 5)
-    (dn,) = tie((dn,), *sums_one)
+    (normed_1, grad_b1), d_gate_1, d_up_1, hidden_1 = grads_one
+    if ring_size(n):
+        sums_one = scatter_all(tie((normed_1,), dn_part), ((0, d_gate_1),), 9)
+        (dn,) = tie((dn,), *sums_one)
     dx, gain_two = rms_back(resid_one, gains[1], dn)
     grad_one = grad_two + dx
 
     grad_b = grad_one.astype(BF)
-    output_grad = dot(grad_b, mixed, 0, 0).astype(BF)
     da = dot(grad_b, out_t, 1, 0).reshape(rows, tok, vw)
-    dq, dan, extra = by_rows(
-        query_back_kernel, scal, place, (q_own, k_all, v_all, da), (qw, vw, qw), (BF, BF, BF)
+    later = ((normed_1, grad_b1), ((0, d_up_1), (1, hidden_1)))
+    if ring_size(n):
+        blank = jnp.zeros_like(q_own)
+        d_kq, d_v, more = attend_back(
+            scal,
+            place,
+            jnp.concatenate([blank, q_own], axis=-1),
+            jnp.concatenate([k_own, blank], axis=-1),
+            v_own,
+            qkv_all,
+            da,
+            later,
+            7,
+        )
+        sums_one = sums_one + more
+        d_kq = d_kq.reshape(count, 2 * qw)
+    else:
+        dq, dan, extra = by_rows(
+            query_back_kernel, scal, place, (q_own, k_all, v_all, da), (qw, vw, qw), (BF, BF, BF)
+        )
+        back = jnp.concatenate([dan, extra], axis=-1).reshape(count, vw + qw)
+        back_all = by_sequence(gather_all([back], 7, 1)[0])
+        dk, d_v = by_rows(
+            key_back_kernel,
+            scal,
+            place,
+            (k_own, v_own, q_all, back_all[..., :vw], back_all[..., vw:]),
+            (qw, vw),
+            (BF, BF),
+        )
+        sums_one = scatter_all((normed_1,), ((0, d_gate_1),), 9) + scatter_all(*later, 10)
+        d_kq = jnp.concatenate([dk, dq], axis=-1).reshape(count, 2 * qw)
+    d_v = d_v.reshape(count, vw)
+    d_all = jnp.concatenate([d_kq, d_v], axis=-1)
+    kqv_w = jnp.concatenate([qkv_w[:, qw : 2 * qw], qkv_w[:, :qw], qkv_w[:, 2 * qw :]], axis=1)
+    dn_part = dot(d_all, kqv_w, 1, 1).astype(BF)
+    dn = head_total(dn_part)
+    unit = inputs * rms_scale(inputs)
+    gain_one = small_sum(jnp.sum(dn_part.astype(F32) * unit, axis=0), "head")
+    small = jnp.concatenate(
+        [
+            jnp.stack([gain_one, gain_two, gain_three, gain_four]),
+            jnp.pad(kernel_grad, ((0, 0), (0, width - cw))),
+            jnp.zeros((8 - 4 - taps, width), F32),
+        ]
     )
-    back = jnp.concatenate([dan, extra], axis=-1).reshape(count, vw + qw)
-    back_all = by_sequence(gather_all([back], 7, 1)[0])
-    dk, dv = by_rows(
-        key_back_kernel,
-        scal,
-        place,
-        (k_own, v_own, q_all, back_all[..., :vw], back_all[..., vw:]),
-        (qw, vw),
-        (BF, BF),
+    sums_attn = scatter_all(
+        tie((normed_a, grad_b), dn_part), ((0, d_kq), (0, d_v), (1, mixed)), 8, 0, small
     )
-    d_qkv = jnp.concatenate([dq, dk, dv], axis=-1).reshape(count, 2 * qw + vw)
-    qkv_grad = dot(normed_a, d_qkv, 0, 0).astype(BF)
-    dn_part = dot(d_qkv, qkv_w, 1, 1).astype(BF)
-    dn = head_total(dn_part)
-    sums_attn = scatter_all(tie((qkv_grad, output_grad), dn_part), 8)
+    gains_grad, kernel_grad = sums_attn[3][:4], sums_attn[3][4 : 4 + taps, :cw]
     (dn,) = tie((dn,), *sums_attn)
-    unit = inputs * rms_scale(inputs)
-    gain_one = jnp.sum(dn_part.astype(F32) * unit, axis=0)
-    gain_one = small_sum(gain_one, "head")
     dx, _ = rms_back(inputs, gains[0], dn)
     input_grad = (grad_one + dx).reshape(activations.shape)
 
-    gains_grad = small_sum(jnp.stack([gain_one, gain_two, gain_three, gain_four]), "seq")
-    kernel_grad = small_sum(kernel_grad, "seq")
     return (
         block_output,
         input_grad,
+        sums_attn[0][:, qw:],
         sums_attn[0][:, :qw],
-        sums_attn[0][:, qw : 2 * qw],
-        sums_attn[0][:, 2 * qw :],
-        sums_attn[1].T,
+        sums_attn[1],
+        sums_attn[2].T,
         sums_one[0],
         sums_one[1],
         sums_one[2].T,

time: 1120 us -> 1060 us (0.946)
  matrix products: 111 us -> 65.6 us
  Pallas kernels: 820 us -> 840 us
  starting transfers between devices: 26.3 us -> 7.69 us
    pallas_call x10, Pallas kernels: 782 us -> 833 us  [run(): pl.pallas_call(partial(self.kernel, body), in_specs=[spec for _, spec in...]
    dot_general x33 -> x22, matrix products: 111 us -> 65.6 us  [dot(): lax.dot_general(a, b, (((ca,), (cb,)), ((), ())), preferred_element_type=...]
    pallas_call x3 -> x1, Pallas kernels: 38.1 us -> 7.33 us  [by_rows(): pl.pallas_call(kernel, grid=(rows,), in_specs=specs, out_specs=[pl.BlockS...]
    ppermute x17 -> x3, starting transfers between devices: 20.9 us -> 2.26 us  [small_sum(): return x + sum((lax.ppermute(sent, axis, r).astype(F32) for r in routes))]
    unnamed x214 -> x253, local copies, waits for them, and re-layouts: 45.3 us -> 43.8 us
  transfers between devices with their start and end apart: 26 -> 12, of which waited for: 11 -> 4; matrix products, arithmetic and copies ran while one was open for 3% -> 2% of each run, Pallas kernels for 56% -> 55%
where the time goes in v3:
time: 1060 us; the launch traced here: 1050 us
  Pallas kernels  840 us (79%)
  matrix products  65.6 us (6%)
  local copies, waits for them, and re-layouts  65.2 us (6%)
  other arithmetic  42.4 us (4%)
  waiting for transfers between devices  16.2 us (2%)
  between operations  16.2 us (2%)
    pallas_call x10, Pallas kernels, run(): pl.pallas_call(partial(self.kernel, body), in_specs=[spec for _, spec in...  833 us
    dot_general x22, matrix products, dot(): lax.dot_general(a, b, (((ca,), (cb,)), ((), ())), preferred_element_type=...  65.6 us
    unnamed x253, local copies, waits for them, and re-layouts  43.8 us
  transfers between devices with their start and end apart: 12, of which 4 were waited for; matrix products, arithmetic and copies ran while one was open for 2% of the time, Pallas kernels for 55%

profile of v3, /device:TPU:0, one launch (start us, length us, event | category | flops | bytes accessed | tf_op | source)
XLA Modules:
  0.0 1053.6 jit_solution(791376230937011532)
XLA Ops:
  8.8 1.9 fusion.10
  12.5 1.8 copy.37
  15.7 45.5 %shard_map.305 = (bf16[1792,576]{1,0:T(8,128)(2,1)}, bf16[1792,448]{1,0:T(8,128)(2,1)}) custom-call(bf16[224,576]{1,0:T(8,128)(2,1)} %pad_maximum_fusion.4.refs_0_, bf16[224,448]{1,0:T(8,128)(2,1)} %bitcast.185), custom_call_target="tpu_custom_call" | custom-call | tf_op jit(solution)/shard_map/pallas_call | solution.py:198
  61.1 4.1 convolution_convert_fusion.5.refs_0_
  65.2 58.8 %shard_map.306 = bf16[4096,576]{1,0:T(8,128)(2,1)} custom-call(bf16[512,576]{1,0:T(8,128)(2,1)} %convolution_convert_fusion.5.refs_0_), custom_call_target="tpu_custom_call" | custom-call | tf_op jit(solution)/shard_map/pallas_call | solution.py:198
  124.1 2.9 copy.39
  127.0 2.7 slice.148.v_ref
  131.1 1.7 fusion.34
  133.0 2.2 copy-done
  135.2 7.3 shard_map.307
  142.6 2.4 convolution_convert_fusion.3
  146.1 121.3 %shard_map.308 = (bf16[1792,1152]{1,0:T(8,128)(2,1)}, bf16[1792,1152]{1,0:T(8,128)(2,1)}, bf16[1792,1152]{1,0:T(8,128)(2,1)}) custom-call(bf16[224,1152]{1,0:T(8,128)(2,1)} %refs_0_, bf16[224,1152]{1,0:T(8,128)(2,1)} %refs_1_, bf16[224,1152]{1,0:T(8,128)(2,1)} %bitcast.189), custom_call_target="tpu_custom_call" | custom-call | tf_op jit(solution)/shard_map/pallas_call | solution.py:198
  267.4 2.3 multiply_reduce_fusion.8
  270.5 2.1 copy-done.103
  272.5 2.6 fusion.37
  275.2 4.1 multiply_convert_fusion.8
  280.3 3.8 convolution_convert_fusion.2
  285.1 54.5 %shard_map.309 = (bf16[1792,448]{1,0:T(8,128)(2,1)}, bf16[1792,448]{1,0:T(8,128)(2,1)}, bf16[1792,448]{1,0:T(8,128)(2,1)}) custom-call(bf16[224,448]{1,0:T(8,128)(2,1)} %refs_0_.1, bf16[224,448]{1,0:T(8,128)(2,1)} %refs_1_.1, bf16[224,448]{1,0:T(8,128)(2,1)} %bitcast.186), custom_call_target="tpu_custom_call" | custom-call | tf_op jit(solution)/shard_map/pallas_call | solution.py:198
  339.6 3.0 multiply_reduce_fusion.7
  343.0 2.4 copy-done.47
  346.6 2.6 collective-permute-start
  349.3 1.4 collective-permute-done
  351.1 2.6 multiply_convert_fusion.10
  354.5 2.4 convolution_convert_fusion.1
  357.3 119.6 %shard_map.310 = (bf16[1792,1152]{1,0:T(8,128)(2,1)}, bf16[1792,1152]{1,0:T(8,128)(2,1)}, bf16[1792,1152]{1,0:T(8,128)(2,1)}) custom-call(bf16[224,1152]{1,0:T(8,128)(2,1)} %refs_0_.2, bf16[224,1152]{1,0:T(8,128)(2,1)} %refs_1_.2, bf16[224,1152]{1,0:T(8,128)(2,1)} %bitcast.190), custom_call_target="tpu_custom_call" | custom-call | tf_op jit(solution)/shard_map/pallas_call | solution.py:198
  477.0 3.3 multiply_reduce_fusion.6
  481.8 2.3 copy-done.108
  484.0 2.5 fusion.40
  486.6 2.5 fusion.39
  489.3 4.2 multiply_convert_fusion.5
  493.5 2.6 fusion.41
  496.1 3.8 add_convert_fusion.3
  500.2 124.1 %shard_map.311 = (f32[224,1152]{1,0:T(8,128)}, f32[224,1152]{1,0:T(8,128)}, f32[224,1152]{1,0:T(8,128)}) custom-call(bf16[512,1792]{1,0:T(8,128)(2,1)} %copy-done.34, bf16[512,1792]{1,0:T(8,128)(2,1)} %bitcast.176, bf16[512,1152]{1,0:T(8,128)(2,1)} %copy-done.54, bf16[512,1152]{1,0:T(8,128)(2,1)} %copy-done.53, bf16[512,1152]{1,0:T(8,128)(2,1)} %get-tuple-element.152.refs_4_), custom_call_target="tpu_custom_call" | custom-call | tf_op jit(solution)/shard_map/pallas_call | solution.py:198
  624.3 1.9 convert_element_type.172
  628.2 1.6 multiply_reduce_fusion
  629.9 1.3 fusion.30.refs_1_
  635.3 1.3 collective-permute-start.1
  637.0 4.2 collective-permute-done.1
  644.3 2.4 add_convert_fusion.1
  647.9 2.9 slice.140
  652.2 54.5 %shard_map.312 = (f32[224,448]{1,0:T(8,128)}, f32[224,448]{1,0:T(8,128)}, f32[224,448]{1,0:T(8,128)}) custom-call(bf16[512,1792]{1,0:T(8,128)(2,1)} %copy-done.23, bf16[512,1792]{1,0:T(8,128)(2,1)} %copy-done.32, bf16[512,448]{1,0:T(8,128)(2,1)} %copy-done.39, bf16[512,448]{1,0:T(8,128)(2,1)} %copy-done.40, bf16[512,448]{1,0:T(8,128)(2,1)} %copy-done.45), custom_call_target="tpu_custom_call" | custom-call | tf_op jit(solution)/shard_map/pallas_call | solution.py:198
  706.8 1.9 convert_element_type.177
  712.6 4.6 fusion.32
  717.2 3.1 multiply_convert_fusion.3
  720.4 2.6 fusion.44
  723.4 4.0 add_convert_fusion
  727.6 2.3 fusion.33
  729.9 6.0 convolution_convert_fusion
  735.9 47.6 %shard_map.313 = f32[224,1152]{1,0:T(8,128)} custom-call(bf16[512,1792]{1,0:T(8,128)(2,1)} %copy-done.27, bf16[512,1152]{1,0:T(8,128)(2,1)} %copy-done.55), custom_call_target="tpu_custom_call" | custom-call | tf_op jit(solution)/shard_map/pallas_call | solution.py:198
  783.5 1.9 convert_element_type.182
  787.4 1.5 copy-done.21
  788.9 1.2 fusion.31.refs_2_
  791.4 2.1 fusion.45
  794.1 152.3 %shard_map.314 = (f32[224,1152]{1,0:T(8,128)}, f32[224,1152]{1,0:T(8,128)}, bf16[4,128,128]{2,1,0:T(8,128)(2,1)}, bf16[4,128,448]{2,1,0:T(8,128)(2,1)}) custom-call(s32[5]{0:T(128)} %copy-done.2, s32[1,1024]{1,0:T(1,128)} %iota.13.refs_1_, bf16[4,128,128]{2,1,0:T(8,128)(2,1)} %concatenate.51.refs_2_, bf16[4,128,128]{2,1,0:T(8,128)(2,1)} %concatenate.52.refs_3_, ...), custom_call_target="tpu_custom_call" | custom-call | tf_op jit(solution)/shard_map/pallas_call | solution.py:198
  946.5 4.6 fusion.5
  952.1 1.4 collective-permute-start.4
  955.7 54.8 %shard_map.315 = (f32[224,128]{1,0:T(8,128)}, f32[224,448]{1,0:T(8,128)}, f32[224,448]{1,0:T(8,128)}, f32[8,1792]{1,0:T(8,128)}) custom-call(f32[8,1792]{1,0:T(8,128)} %concatenate.55.refs_0_, bf16[512,1792]{1,0:T(8,128)(2,1)} %copy-done.35, bf16[512,1792]{1,0:T(8,128)(2,1)} %copy-done.33, bf16[512,128]{1,0:T(8,128)(2,1)} %bitcast.194, ...), custom_call_target="tpu_custom_call" | custom-call | tf_op jit(solution)/shard_map/pallas_call | solution.py:198
  1010.5 1.4 slice.144
  1012.0 1.3 slice.143
  1013.3 2.0 copy.53
  1017.8 9.9 all-reduce.24.cloned.1.call-done
  1027.7 1.9 convert_element_type.185
  1032.4 4.0 fusion.9
  1036.4 1.8 add_convert_fusion.2
  (327 shorter events, 52.0 us)
Async XLA Ops:
  7.2 7.0 copy-start.8
  7.2 7.5 copy-start.69
  7.2 260.2 %all-reduce.12.cloned.1.call-start = ((), (), s32[]{:S(2)}) async-start(), calls=%async_computation | async-start | bytes 3670016 | tf_op jit(solution)/shard_map/psum | solution.py:556
  8.8 56.5 %copy-start.72 = (f32[1792]{0:T(1024)}, f32[1792]{0:T(1024)S(1)}, u32[]{:S(2)}) copy-start(f32[1792]{0:T(1024)S(1)} %get-tuple-element.138) | copy-start | bytes 21508
  10.7 54.5 %copy-start.76 = (f32[2,2,128]{2,1,0:T(2,128)}, f32[2,2,128]{2,1,0:T(2,128)S(1)}, u32[]{:S(2)}) copy-start(f32[2,2,128]{2,1,0:T(2,128)S(1)} %add_rsqrt_fusion.3) | copy-start | bytes 6148
  14.7 50.5 %copy-start.35 = (bf16[512,1792]{1,0:T(8,128)(2,1)}, bf16[512,1792]{1,0:T(8,128)(2,1)S(1)}, u32[]{:S(2)}) copy-start(bf16[512,1792]{1,0:T(8,128)(2,1)S(1)} %fusion.4.refs_1_) | copy-start | bytes 5505028
  127.0 3.7 copy-start.20
  127.0 5.8 copy-start.114
  133.0 12.0 %copy-start.2 = (s32[5]{0:T(128)}, s32[5]{0:T(128)S(1)}, u32[]{:S(2)}) copy-start(s32[5]{0:T(128)S(1)} %pad_add_fusion.scal_ref.refs_0_) | copy-start | bytes 64
  135.2 7.4 copy-start.110
  145.0 194.6 %all-reduce.14.cloned.1.call-start = ((), (), s32[]{:S(2)}) async-start(), calls=%async_computation.1 | async-start | bytes 3670016 | tf_op jit(solution)/shard_map/psum | solution.py:556
  270.5 4.7 copy-start.27
  275.1 4.1 copy-start.115
  275.2 5.1 copy-start.105
  284.1 192.8 %all-reduce.16.cloned.1.call-start = ((), (), s32[]{:S(2)}) async-start(), calls=%async_computation.2 | async-start | bytes 3670016 | tf_op jit(solution)/shard_map/psum | solution.py:556
  285.1 65.9 %copy-start.79 = (f32[512]{0:T(512)}, f32[512]{0:T(512)S(1)}, u32[]{:S(2)}) copy-start(f32[512]{0:T(512)S(1)} %get-tuple-element.167) | copy-start | bytes 6148
  285.1 66.0 %copy-start.89 = (f32[512]{0:T(512)}, f32[512]{0:T(512)S(1)}, u32[]{:S(2)}) copy-start(f32[512]{0:T(512)S(1)} %get-tuple-element.164) | copy-start | bytes 6148
  285.1 66.0 %copy-start.91 = (f32[512]{0:T(512)}, f32[512]{0:T(512)S(1)}, u32[]{:S(2)}) copy-start(f32[512]{0:T(512)S(1)} %get-tuple-element.165) | copy-start | bytes 6148
  342.6 4.0 copy-start.3
  342.6 4.0 copy-start.81
  343.0 8.0 copy-start.23
  343.0 6.3 copy-start.95
  346.6 4.5 copy-start.36
  346.6 4.1 collective-permute-start
  349.3 4.3 copy-start.83
  349.3 4.3 copy-start.85
  349.3 4.3 copy-start.87
  356.9 123.4 %copy-start.70 = (f32[1792]{0:T(1024)S(1)}, f32[1792]{0:T(1024)}, u32[]{:S(2)}) copy-start(f32[1792]{0:T(1024)} %get-tuple-element.136) | copy-start | bytes 21508
  356.9 267.4 %all-reduce.18.cloned.1.call-start = ((), (), s32[]{:S(2)}) async-start(), calls=%async_computation.3 | async-start | bytes 3670016 | tf_op jit(solution)/shard_map/psum | solution.py:556
  476.9 3.7 copy-start.4
  477.0 4.2 copy-start.12
  481.8 4.8 copy-start.34
  500.0 206.8 %all-reduce.20.cloned.1.call-start = ((), (), s32[]{:S(2)}) async-start(), calls=%async_computation.4 | async-start | bytes 3670016 | tf_op jit(solution)/shard_map/psum | solution.py:556
  624.3 3.7 copy-start.13
  631.4 3.9 copy-start.32
  635.3 8.5 copy-start.40
  635.3 5.8 collective-permute-start.1
  636.8 4.6 copy-start.84
  636.8 4.6 copy-start.86
  636.8 4.6 copy-start.88
  636.8 4.6 copy-start.96
  636.8 4.6 copy-start.97
  646.7 4.8 copy-start.61
  646.8 136.8 %all-reduce.22.cloned.1.call-start = ((), (), s32[]{:S(2)}) async-start(), calls=%async_computation.5 | async-start | bytes 3670016 | tf_op jit(solution)/shard_map/psum | solution.py:556
  712.6 4.7 copy-start.106
  712.6 4.7 copy-start.116
  712.6 4.7 copy-start.117
  727.4 300.4 %all-reduce.24.cloned.1.call-start = ((), (), s32[]{:S(2)}) async-start(), calls=%async_computation.6 | async-start | bytes 7340032 | tf_op jit(solution)/shard_map/psum | solution.py:556
  794.1 152.3 %copy-start.46 = (bf16[1792,448]{1,0:T(8,128)(2,1)S(1)}, bf16[1792,448]{1,0:T(8,128)(2,1)}, u32[]{:S(2)}) copy-start(bf16[1792,448]{1,0:T(8,128)(2,1)} %slice.140) | copy-start | bytes 4816900
  794.1 152.3 %copy-start.62 = (bf16[1792,64]{1,0:T(8,128)(2,1)S(1)}, bf16[1792,64]{1,0:T(8,128)(2,1)}, u32[]{:S(2)}) copy-start(bf16[1792,64]{1,0:T(8,128)(2,1)} %get-tuple-element.153) | copy-start | bytes 688132
  794.1 152.3 %copy-start.63 = (bf16[1792,64]{1,0:T(8,128)(2,1)S(1)}, bf16[1792,64]{1,0:T(8,128)(2,1)}, u32[]{:S(2)}) copy-start(bf16[1792,64]{1,0:T(8,128)(2,1)} %get-tuple-element.154) | copy-start | bytes 688132
  794.1 152.4 %copy-start.77 = (f32[2,2,128]{2,1,0:T(2,128)S(1)}, f32[2,2,128]{2,1,0:T(2,128)}, u32[]{:S(2)}) copy-start(f32[2,2,128]{2,1,0:T(2,128)} %copy-done.76) | copy-start | bytes 6148
  951.2 3.3 collective-permute-start.2
  951.2 3.7 collective-permute-start.3
  952.1 2.8 collective-permute-start.4
  1010.5 19.1 %copy-start.73 = (f32[1792]{0:T(1024)S(1)}, f32[1792]{0:T(1024)}, u32[]{:S(2)}) copy-start(f32[1792]{0:T(1024)} %copy-done.72) | copy-start | bytes 21508
  1032.4 4.0 copy-start.7
  1032.4 4.0 copy-start.15
  1032.4 4.0 copy-start.49
  1038.2 3.7 copy-start.65
  1039.0 3.7 copy-start.64
  1039.0 4.4 copy-start.58
  1040.0 4.4 copy-start.57
  1040.9 4.4 copy-start.56
  (66 other events, 160.0 us)
Sparse Core Ops, SparseCore 0:
  145.1 46.1 all-reduce.11
  284.2 46.4 all-reduce.13
  357.0 47.8 all-reduce.15
  500.1 47.2 all-reduce.17
  646.9 47.9 all-reduce.19
  727.5 47.1 all-reduce.21
  951.3 76.3 all-reduce.23

commit v4 on v3

--- a/solution.py
+++ b/solution.py
@@ -30,14 +30,16 @@
     return n == 8
 
 
-def greet(n):
-    pos = ring_position(lax.axis_index("seq"))
+def greet(n, everyone=False):
+    me = lax.axis_index("seq")
+    pos = ring_position(me)
     right = ring_device(lax.rem(pos + 1, n))
     left = ring_device(lax.rem(pos + n - 1, n))
     barrier = pltpu.get_barrier_semaphore()
-    for neighbour in (left, right):
-        pl.semaphore_signal(barrier, inc=1, device_id={"seq": neighbour}, device_id_type=MESH)
-    pl.semaphore_wait(barrier, 2)
+    partners = [lax.rem(me + k, n) for k in range(1, n)] if everyone else [left, right]
+    for partner in partners:
+        pl.semaphore_signal(barrier, inc=1, device_id={"seq": partner}, device_id_type=MESH)
+    pl.semaphore_wait(barrier, len(partners))
     return pos, right, left
 
 
@@ -112,6 +114,12 @@
         self.call_id = call_id
         self.ins, self.outs, self.scratch = {}, {}, {}
         self.gathers, self.scatters = {}, {}
+        self.exchanges = []
+
+    def exchange(self, name):
+        self.sems(name + ".send", self.n)
+        self.sems(name + ".recv", self.n)
+        self.exchanges.append(name)
 
     def take(self, name, array, space=VMEM):
         self.ins[name] = (array, pl.BlockSpec(memory_space=space))
@@ -140,23 +148,25 @@
         rows, width = array.shape
         self.hold(name + ".blocked", (self.n, rows, width // self.n), BF)
 
-    def scatter(self, name, left, right, flip=False):
+    def scatter(self, name, left, right, flip=False, axis=0):
         n = self.n
         height = self.ins[left][0].shape[1] // n
-        block = (height, right.shape[1])
+        block = (height, right.shape[1 - axis])
         self.take(name + ".right", right)
         self.give(name, block, F32)
         self.hold(name + ".sums", (2, n // 2) + block, BF)
         self.hold(name + ".slots", (2, n // 2) + block, BF)
         self.sems(name + ".send", 2, n // 2)
         self.sems(name + ".recv", 2, n // 2)
-        self.scatters[name] = (left, flip)
+        self.scatters[name] = (left, flip, axis)
 
     def kernel(self, body, *refs):
         names = list(self.ins) + list(self.outs) + list(self.scratch)
         at = dict(zip(names, refs))
-        where = greet(self.n)
+        where = greet(self.n, bool(self.exchanges))
         rings = {}
+        if self.early is not None:
+            self.early(at)
         for name, (src, out, place, flip) in self.gathers.items():
             rings[name] = GatherRing(
                 self.n,
@@ -170,7 +180,7 @@
                 flip,
             )
         ready = set()
-        for name, (left, flip) in self.scatters.items():
+        for name, (left, flip, axis) in self.scatters.items():
             blocked = at[left + ".blocked"]
             if left not in ready:
                 ready.add(left)
@@ -188,13 +198,17 @@
                 at[name + ".send"],
                 at[name + ".recv"],
                 flip,
+                axis,
             )
             rings[name].step()
         body(at, rings)
         for ring in rings.values():
             ring.finish()
 
-    def run(self, body):
+    early = None
+
+    def run(self, body, early=None):
+        self.early = early
         outs = pl.pallas_call(
             partial(self.kernel, body),
             in_specs=[spec for _, spec in self.ins.values()],
@@ -232,7 +246,8 @@
 
 
 class ScatterRing:
-    def __init__(self, n, where, left, right, out, sums, slots, send, recv, flip):
+    def __init__(self, n, where, left, right, out, sums, slots, send, recv, flip, axis):
+        self.axis = axis
         self.n, self.left_ref, self.right_ref, self.out = n, left, right, out
         self.sums, self.slots, self.send, self.recv = sums, slots, send, recv
         self.pos, self.right, self.left = where
@@ -244,7 +259,7 @@
 
     def term(self, r):
         owner = ring_device(lax.rem(self.pos + (r % self.n), self.n))
-        return dot(self.left_ref[owner], self.right_ref[...], 0, 0)
+        return dot(self.left_ref[owner], self.right_ref[...], 0, self.axis)
 
     def copy(self, d, h):
         i = 0 if d == 1 else 1
@@ -289,12 +304,13 @@
 
 def scatter_all(lefts, pairs, call_id, flip=0, small=None):
     n = lax.axis_size("seq")
+    pairs = [p if len(p) == 3 else p + (0,) for p in pairs]
     if not ring_size(n):
         sums = [
             lax.psum_scatter(
-                dot(lefts[i], right, 0, 0).astype(BF), "seq", scatter_dimension=0, tiled=True
+                dot(lefts[i], right, 0, axis).astype(BF), "seq", scatter_dimension=0, tiled=True
             ).astype(F32)
-            for i, right in pairs
+            for i, right, axis in pairs
         ]
         return sums if small is None else sums + [lax.psum(small.astype(BF), "seq").astype(F32)]
     call = Call(call_id)
@@ -305,8 +321,8 @@
         call.gather("small", "small.src", "small.all", by_block(small.shape[0]))
     for i, a in enumerate(lefts):
         call.left(f"left{i}", a)
-    for j, (i, right) in enumerate(pairs):
-        call.scatter(names[j], f"left{i}", right, (j + flip) % 2 == 1)
+    for j, (i, right, axis) in enumerate(pairs):
+        call.scatter(names[j], f"left{i}", right, (j + flip) % 2 == 1, axis)
     if small is not None:
         names.append(call.give("small.sum", small.shape, F32))
 
@@ -428,93 +444,196 @@
     dv_ref[0] = dv.astype(BF)
 
 
-def attend_back(scal, place, q, k, v, qkv_all, da, scatters, call_id):
+class Exchange:
+    def __init__(self, n, at, name, block, place):
+        self.n, self.block, self.place = n, block, place
+        self.send, self.recv = at[name + ".send"], at[name + ".recv"]
+        self.me = lax.axis_index("seq")
+
+    def copy(self, k):
+        partner = lax.rem(self.me + k, self.n)
+        return pltpu.make_async_remote_copy(
+            src_ref=self.block(partner),
+            dst_ref=self.place(self.me),
+            send_sem=self.send.at[k],
+            recv_sem=self.recv.at[k],
+            device_id={"seq": partner},
+            device_id_type=MESH,
+        )
+
+    def own(self):
+        return pltpu.make_async_copy(self.block(self.me), self.place(self.me), self.send.at[0])
+
+    def start(self):
+        for k in range(1, self.n):
+            self.copy(k).start()
+        self.own().start()
+
+    def wait(self):
+        self.own().wait()
+        for k in range(1, self.n):
+            self.copy(k).wait_recv()
+
+    def wait_sent(self):
+        for k in range(1, self.n):
+            self.copy(k).wait_send()
+
+
+def to_pair(ref, features, tok):
+    def block(partner):
+        rows = pl.ds(pl.multiple_of(lax.rem(partner, 2) * features, 16), features)
+        return ref.at[rows, pl.ds(pl.multiple_of((partner // 2) * tok, 128), tok)]
+
+    return block
+
+
+def at_positions(ref, tok):
+    return lambda device: ref.at[:, pl.ds(pl.multiple_of(device * tok, 128), tok)]
+
+
+def causal(offset, i, tok):
+    shape = ((i + 1) * tok, tok)
+    earlier = lax.broadcasted_iota(jnp.int32, shape, 0)
+    pos = i * tok + lax.broadcasted_iota(jnp.int32, shape, 1)
+    return (earlier <= pos) & ((earlier >= offset) | (pos < offset))
+
+
+def attend_pairs(off, qkv, carried, call_id):
     n = lax.axis_size("seq")
-    rows, tok, vw = v.shape
-    qkw = q.shape[-1]
+    tok = qkv.shape[1] * 2 // n
+    features = qkv.shape[0] // 2
+    vf = features - 4 * QK
     call = Call(call_id)
-    call.take("scal", scal, pltpu.SMEM)
-    for name, a in (("place", place), ("q", q), ("k", k), ("v", v), ("all", qkv_all), ("da", da)):
-        call.take(name, a)
+    call.take("off", off, pltpu.SMEM)
+    call.take("qkv", qkv)
+    for j, a in enumerate(carried):
+        call.take(f"c{j}.src", a, pl.ANY)
+        call.give(f"c{j}", (n * a.shape[0], a.shape[1]), a.dtype, pl.ANY)
+        call.gather(f"c{j}", f"c{j}.src", f"c{j}", by_block(a.shape[0]), j % 2 == 1)
+    call.give("mixed", (2 * vf, qkv.shape[1]), BF)
+    call.give("all", (features, n * tok), BF)
+    call.give("att", (vf, n * tok), F32)
+    call.give("den", (8, n * tok), F32)
+    call.hold("own", (vf, n * tok), BF)
+    call.exchange("in")
+    call.exchange("out")
+
+    def incoming(at):
+        return Exchange(n, at, "in", to_pair(at["qkv"], features, tok), at_positions(at["all"], tok))
+
+    def body(at, rings):
+        def turn():
+            for ring in rings.values():
+                ring.step()
+
+        turn()
+        arriving = incoming(at)
+        arriving.wait()
+        turn()
+        me = lax.axis_index("seq")
+        offset = at["off"][me // 2]
+        whole = at["all"]
+        at["den"][...] = jnp.ones_like(at["den"])
+        for h in range(2):
+            lines = slice(h * vf // 2, (h + 1) * vf // 2)
+            for i in range(n):
+                here, upto = slice(i * tok, (i + 1) * tok), slice(0, (i + 1) * tok)
+                q = whole[h * QK : (h + 1) * QK, here]
+                k = whole[(2 + h) * QK : (3 + h) * QK, upto]
+                v = whole[4 * QK + h * vf // 2 : 4 * QK + (h + 1) * vf // 2, upto]
+                s = dot(k, q, 0, 0) * (QK**-0.5)
+                w = jnp.where(causal(offset, i, tok), 1.0 + s + 0.5 * s * s, 0.0)
+                den = jnp.sum(w, axis=0, keepdims=True)
+                att = dot(v, w.astype(BF), 1, 0) / den
+                at["att"][lines, here] = att
+                at["den"][h : h + 1, here] = den
+                at["own"][lines, here] = att.astype(BF)
+        leaving = Exchange(
+            n, at, "out", at_positions(at["own"], tok), lambda me: to_pair(at["mixed"], vf, tok)(me)
+        )
+        leaving.start()
+        turn()
+        leaving.wait()
+        arriving.wait_sent()
+        leaving.wait_sent()
+
+    out = call.run(body, lambda at: incoming(at).start())
+    return out, [out[f"c{j}"] for j in range(len(carried))]
+
+
+def attend_pairs_back(off, da, kept, scatters, call_id):
+    n = lax.axis_size("seq")
+    whole = kept["all"]
+    features, tok = whole.shape[0], whole.shape[1] // n
+    vf = features - 4 * QK
+    call = Call(call_id)
+    call.take("off", off, pltpu.SMEM)
+    call.take("da", da)
+    for name in ("all", "att", "den"):
+        call.take(name, kept[name])
     lefts, pairs = scatters
     for i, a in enumerate(lefts):
         call.left(f"left{i}", a)
     for j, (i, right) in enumerate(pairs):
         call.scatter(f"s{j}", f"left{i}", right, j % 2 == 1)
-    call.give("dqk", (rows, tok, qkw), BF)
-    call.give("dv", (rows, tok, vw), BF)
-    call.hold("dq", (rows, tok, qkw), F32)
-    call.hold("back", (rows, tok, qkw + vw), BF)
-    call.hold("back_all", (rows, n * tok, qkw + vw), BF)
-    call.gather("g", "back", "back_all", by_position(tok), True)
-    heads = qkw // 2 // QK
+    call.give("d", (2 * features, da.shape[1]), BF)
+    call.hold("da_all", (vf, n * tok), BF)
+    call.hold("sum", (2 * QK + vf, n * tok), F32)
+    call.hold("own", (features, n * tok), BF)
+    call.exchange("in")
+    call.exchange("out")
+
+    def incoming(at):
+        return Exchange(n, at, "in", to_pair(at["da"], vf, tok), at_positions(at["da_all"], tok))
 
     def body(at, rings):
-        lane = lax.broadcasted_iota(jnp.int32, (1, qkw), 1)
-        masks = head_masks(qkw // 2, vw)
-        far = [(lane >= qkw // 2 + h * QK) & (lane < qkw // 2 + (h + 1) * QK) for h in range(heads)]
-        near = [(lane >= h * QK) & (lane < (h + 1) * QK) for h in range(heads)]
-
-        def query_side(r, carry):
-            q, da = at["q"][r], at["da"][r]
-            qk, v = at["all"][r, :, :qkw], at["all"][r, :, qkw:]
-            mask = query_mask(at["scal"], at["place"], tok, r)
-            dq = jnp.zeros((tok, qkw), F32)
-            dan_all = jnp.zeros((tok, vw), F32)
-            extra = jnp.zeros((tok, qkw), F32)
-            for h in range(heads):
-                in_v = masks[h][1]
-                s = dot(jnp.where(far[h], q, jnp.zeros_like(q)), qk, 1, 1) * (QK**-0.5)
-                w = jnp.where(mask, 1.0 + s + 0.5 * s * s, 0.0)
-                den = jnp.sum(w, axis=1, keepdims=True)
-                att = dot(w.astype(BF), v, 1, 0) / den
-                dan = jnp.where(in_v, da / den, 0.0).astype(BF)
-                dan_f = dan.astype(F32)
-                delta = jnp.sum(dan_f * att, axis=1, keepdims=True)
-                ds = jnp.where(mask, (dot(dan, v, 1, 1) - delta) * (1.0 + s), 0.0).astype(BF)
-                dq = dq + jnp.where(far[h], dot(ds, qk, 1, 0) * (QK**-0.5), 0.0)
-                dan_all = dan_all + dan_f
-                high = delta.astype(BF).astype(F32)
-                extra = extra + jnp.where(lane == h, high, 0.0)
-                extra = extra + jnp.where(lane == heads + h, delta - high, 0.0)
-            at["dq"][r] = dq
-            at["back"][r, :, :qkw] = extra.astype(BF)
-            at["back"][r, :, qkw:] = dan_all.astype(BF)
-            return carry
-
-        def key_side(r, carry):
-            k, v = at["k"][r], at["v"][r]
-            qk = at["all"][r, :, :qkw]
-            extra, dan = at["back_all"][r, :, :qkw], at["back_all"][r, :, qkw:]
-            mask = key_mask(at["scal"], at["place"], tok, r)
-            wide = lax.broadcasted_iota(jnp.int32, (tok, qkw), 1)
-            dqk = at["dq"][r]
-            dv = jnp.zeros((tok, vw), F32)
-            for h in range(heads):
-                in_v = masks[h][1]
-                s = dot(jnp.where(near[h], k, jnp.zeros_like(k)), qk, 1, 1) * (QK**-0.5)
+        arriving = incoming(at)
+        arriving.wait()
+        me = lax.axis_index("seq")
+        offset = at["off"][me // 2]
+        whole = at["all"]
+        total = at["sum"]
+        for h in range(2):
+            lines = slice(h * vf // 2, (h + 1) * vf // 2)
+            k_lines = slice(h * QK, (h + 1) * QK)
+            v_lines = slice(2 * QK + h * vf // 2, 2 * QK + (h + 1) * vf // 2)
+            for i in range(n - 1, -1, -1):
+                here, upto = slice(i * tok, (i + 1) * tok), slice(0, (i + 1) * tok)
+                q = whole[h * QK : (h + 1) * QK, here]
+                k = whole[(2 + h) * QK : (3 + h) * QK, upto]
+                v = whole[4 * QK + h * vf // 2 : 4 * QK + (h + 1) * vf // 2, upto]
+                mask = causal(offset, i, tok)
+                s = dot(k, q, 0, 0) * (QK**-0.5)
                 w = jnp.where(mask, 1.0 + s + 0.5 * s * s, 0.0).astype(BF)
-                dv = dv + jnp.where(in_v, dot(w, dan, 1, 0), 0.0)
-                pick = jnp.where((wide == h) | (wide == heads + h), 1.0, 0.0).astype(BF)
-                d_kernel = dot(jnp.where(in_v, v, jnp.zeros_like(v)), dan, 1, 1) - dot(pick, extra, 1, 1)
-                ds = jnp.where(mask, d_kernel * (1.0 + s), 0.0).astype(BF)
-                dqk = dqk + jnp.where(near[h], dot(ds, qk, 1, 0) * (QK**-0.5), 0.0)
-            at["dqk"][r] = dqk.astype(BF)
-            at["dv"][r] = dv.astype(BF)
-            return carry
-
-        lax.fori_loop(0, rows, query_side, 0)
-        others = [ring for name, ring in rings.items() if name != "g"]
-        for _ in range(n // 2):
-            rings["g"].step()
-            for ring in others:
-                ring.step()
-        rings["g"].finish()
-        del rings["g"]
-        lax.fori_loop(0, rows, key_side, 0)
-
-    out = call.run(body)
-    return out["dqk"], out["dv"], [out[f"s{j}"] for j in range(len(pairs))]
+                dan = (at["da_all"][lines, here].astype(F32) / at["den"][h : h + 1, here]).astype(BF)
+                delta = jnp.sum(dan.astype(F32) * at["att"][lines, here], axis=0, keepdims=True)
+                ds = jnp.where(mask, (dot(v, dan, 0, 0) - delta) * (1.0 + s), 0.0).astype(BF)
+                dq = dot(k, ds, 1, 0) * (QK**-0.5)
+                at["own"][h * QK : (h + 1) * QK, here] = dq.astype(BF)
+                dk = dot(q, ds, 1, 1) * (QK**-0.5)
+                dv = dot(dan, w, 1, 1)
+                if i == n - 1:
+                    total[k_lines, upto] = dk
+                    total[v_lines, upto] = dv
+                else:
+                    total[k_lines, upto] += dk
+                    total[v_lines, upto] += dv
+            if h == 0:
+                for ring in rings.values():
+                    ring.step()
+        at["own"][2 * QK :, :] = total[...].astype(BF)
+        leaving = Exchange(
+            n, at, "out", at_positions(at["own"], tok), lambda me: to_pair(at["d"], features, tok)(me)
+        )
+        leaving.start()
+        for ring in rings.values():
+            ring.step()
+        leaving.wait()
+        arriving.wait_sent()
+        leaving.wait_sent()
+
+    out = call.run(body, lambda at: incoming(at).start())
+    return out["d"], [out[f"s{j}"] for j in range(len(pairs))]
 
 
 def by_rows(kernel, scal, place, operands, widths, kinds):
@@ -630,36 +749,51 @@
     start = here * tok
     off = offsets.reshape(rows)
 
-    qkv_s = jnp.concatenate([attn_query, attn_key, attn_value], axis=1)
+    paired = ring_size(n) and 2 * rows == n and qw == 4 * QK
+    if paired:
+        halves = [
+            a[:, g * a.shape[1] // 2 : (g + 1) * a.shape[1] // 2]
+            for g in range(2)
+            for a in (attn_query, attn_key, attn_value)
+        ]
+        qkv_s = jnp.concatenate(halves, axis=1)
+    else:
+        qkv_s = jnp.concatenate([attn_query, attn_key, attn_value], axis=1)
     gains = norm_gains.astype(F32)
     kernel_f = conv_kernel.astype(F32)
     inputs = activations.reshape(count, width).astype(F32)
     grad_four = cotangent.reshape(count, width)
-    qkv_w, out_t = gather_all([qkv_s, attn_output.T], 1)
+    outs_s = jnp.concatenate([attn_output.T, conv_output.T], axis=1)
+    (qkv_w,) = gather_all([qkv_s], 1)
 
     scal = jnp.concatenate([start[None].astype(jnp.int32), off])
     place = jnp.arange(n * tok, dtype=jnp.int32).reshape(1, n * tok)
     normed_a = rms_norm(inputs, gains[0]).astype(BF)
-    qkv = dot(normed_a, qkv_w, 1, 0).astype(BF)
 
     def by_sequence(blocks):
         return jnp.swapaxes(blocks.reshape(n, rows, tok, -1), 0, 1).reshape(rows, n * tok, -1)
 
-    qkv_all = by_sequence(gather_all([qkv], 2)[0])
-    own = qkv.reshape(rows, tok, -1)
-    q_own, k_own, v_own = own[..., :qw], own[..., qw : 2 * qw], own[..., 2 * qw :]
-    q_all, k_all, v_all = qkv_all[..., :qw], qkv_all[..., qw : 2 * qw], qkv_all[..., 2 * qw :]
-    (mixed,) = by_rows(attend_kernel, scal, place, (q_own, k_all, v_all), (vw,), (BF,))
-    mixed = mixed.reshape(count, vw)
-    attn_part = dot(mixed, out_t, 1, 1).astype(BF)
+    if paired:
+        qkv = dot(qkv_w, normed_a, 0, 1).astype(BF)
+        attention, (outs_t, gate_1) = attend_pairs(off, qkv, (outs_s, ffn1_gate), 2)
+        mixed, mixed_axis = attention["mixed"], 1
+    else:
+        qkv = dot(normed_a, qkv_w, 1, 0).astype(BF)
+        qkv_all = by_sequence(gather_all([qkv], 2)[0])
+        own = qkv.reshape(rows, tok, -1)
+        q_own, k_own, v_own = own[..., :qw], own[..., qw : 2 * qw], own[..., 2 * qw :]
+        q_all, k_all, v_all = qkv_all[..., :qw], qkv_all[..., qw : 2 * qw], qkv_all[..., 2 * qw :]
+        (mixed,) = by_rows(attend_kernel, scal, place, (q_own, k_all, v_all), (vw,), (BF,))
+        mixed, mixed_axis = mixed.reshape(count, vw), 0
+        outs_t, gate_1 = gather_all((outs_s, ffn1_gate), 11)
+    out_t, conv_out_t = outs_t[:, :vw], outs_t[:, vw:]
+    attn_part = dot(mixed, out_t, 1 - mixed_axis, 1).astype(BF)
     attn_sum = head_total(attn_part)
-    ffn1 = gather_all(tie((ffn1_gate, ffn1_up, ffn1_down.T), attn_part), 3)
+    ffn1 = [gate_1] + gather_all(tie((ffn1_up, ffn1_down.T), attn_part), 12)
     resid_one = inputs + attn_sum
     part, kept_one = mlp_forward(resid_one, gains[1], ffn1)
     ffn1_sum = head_total(part)
-    inner_w, gate_w, conv_out_t = gather_all(
-        tie((conv_input, conv_gate, conv_output.T), part), 4, 1
-    )
+    inner_w, gate_w = gather_all(tie((conv_input, conv_gate), part), 4)
     resid_two = resid_one + ffn1_sum
 
     normed_c = rms_norm(resid_two, gains[2]).astype(BF)
@@ -721,30 +855,19 @@
     grad_one = grad_two + dx
 
     grad_b = grad_one.astype(BF)
-    da = dot(grad_b, out_t, 1, 0).reshape(rows, tok, vw)
     later = ((normed_1, grad_b1), ((0, d_up_1), (1, hidden_1)))
-    if ring_size(n):
-        blank = jnp.zeros_like(q_own)
-        d_kq, d_v, more = attend_back(
-            scal,
-            place,
-            jnp.concatenate([blank, q_own], axis=-1),
-            jnp.concatenate([k_own, blank], axis=-1),
-            v_own,
-            qkv_all,
-            da,
-            later,
-            7,
-        )
+    if paired:
+        da = dot(out_t, grad_b, 0, 1).astype(BF)
+        d_qkv, more = attend_pairs_back(off, da, attention, later, 7)
         sums_one = sums_one + more
-        d_kq = d_kq.reshape(count, 2 * qw)
     else:
+        da = dot(grad_b, out_t, 1, 0).reshape(rows, tok, vw)
         dq, dan, extra = by_rows(
             query_back_kernel, scal, place, (q_own, k_all, v_all, da), (qw, vw, qw), (BF, BF, BF)
         )
         back = jnp.concatenate([dan, extra], axis=-1).reshape(count, vw + qw)
         back_all = by_sequence(gather_all([back], 7, 1)[0])
-        dk, d_v = by_rows(
+        dk, dv = by_rows(
             key_back_kernel,
             scal,
             place,
@@ -753,11 +876,8 @@
             (BF, BF),
         )
         sums_one = scatter_all((normed_1,), ((0, d_gate_1),), 9) + scatter_all(*later, 10)
-        d_kq = jnp.concatenate([dk, dq], axis=-1).reshape(count, 2 * qw)
-    d_v = d_v.reshape(count, vw)
-    d_all = jnp.concatenate([d_kq, d_v], axis=-1)
-    kqv_w = jnp.concatenate([qkv_w[:, qw : 2 * qw], qkv_w[:, :qw], qkv_w[:, 2 * qw :]], axis=1)
-    dn_part = dot(d_all, kqv_w, 1, 1).astype(BF)
+        d_qkv = jnp.concatenate([dq, dk, dv], axis=-1).reshape(count, 2 * qw + vw)
+    dn_part = dot(d_qkv, qkv_w, 1 - mixed_axis, 1).astype(BF)
     dn = head_total(dn_part)
     unit = inputs * rms_scale(inputs)
     gain_one = small_sum(jnp.sum(dn_part.astype(F32) * unit, axis=0), "head")
@@ -769,9 +889,20 @@
         ]
     )
     sums_attn = scatter_all(
-        tie((normed_a, grad_b), dn_part), ((0, d_kq), (0, d_v), (1, mixed)), 8, 0, small
+        tie((normed_a, grad_b), dn_part), ((0, d_qkv, mixed_axis), (1, mixed, mixed_axis)), 8, 0, small
     )
-    gains_grad, kernel_grad = sums_attn[3][:4], sums_attn[3][4 : 4 + taps, :cw]
+    gains_grad, kernel_grad = sums_attn[2][:4], sums_attn[2][4 : 4 + taps, :cw]
+    qkv_sum = sums_attn[0]
+    if paired:
+        edges = (0, qw // 2, qw, qw + vw // 2)
+        step = qw + vw // 2
+        query_sum, key_sum, value_sum = (
+            jnp.concatenate([qkv_sum[:, g * step + a : g * step + b] for g in range(2)], axis=1)
+            for a, b in zip(edges[:-1], edges[1:])
+        )
+    else:
+        query_sum, key_sum = qkv_sum[:, :qw], qkv_sum[:, qw : 2 * qw]
+        value_sum = qkv_sum[:, 2 * qw :]
     (dn,) = tie((dn,), *sums_attn)
     dx, _ = rms_back(inputs, gains[0], dn)
     input_grad = (grad_one + dx).reshape(activations.shape)
@@ -779,10 +910,10 @@
     return (
         block_output,
         input_grad,
-        sums_attn[0][:, qw:],
-        sums_attn[0][:, :qw],
-        sums_attn[1],
-        sums_attn[2].T,
+        query_sum,
+        key_sum,
+        value_sum,
+        sums_attn[1].T,
         sums_one[0],
         sums_one[1],
         sums_one[2].T,

time: 1060 us -> 998 us (0.942)
  Pallas kernels: 840 us -> 788 us
  local copies, waits for them, and re-layouts: 65.2 us -> 48.4 us
    pallas_call x10, Pallas kernels: 833 us -> 788 us  [run(): pl.pallas_call(partial(self.kernel, body), in_specs=[spec for _, spec in...]
    unnamed x253 -> x178, local copies, waits for them, and re-layouts: 43.8 us -> 37.9 us
  transfers between devices with their start and end apart: 12 -> 12, of which waited for: 4 -> 5; matrix products, arithmetic and copies ran while one was open for 2% -> 2% of each run, Pallas kernels for 55% -> 55%
where the time goes in v4:
time: 998 us; the launch traced here: 991 us
  Pallas kernels  788 us (79%)
  matrix products  65.6 us (7%)
  local copies, waits for them, and re-layouts  48.4 us (5%)
  other arithmetic  41.7 us (4%)
  waiting for transfers between devices  23 us (2%)
  between operations  15.8 us (2%)
    pallas_call x10, Pallas kernels, run(): pl.pallas_call(partial(self.kernel, body), in_specs=[spec for _, spec in...  788 us
    dot_general x22, matrix products, dot(): lax.dot_general(a, b, (((ca,), (cb,)), ((), ())), preferred_element_type=...  65.6 us
    unnamed x178, local copies, waits for them, and re-layouts  37.9 us
  transfers between devices with their start and end apart: 12, of which 5 were waited for; matrix products, arithmetic and copies ran while one was open for 2% of the time, Pallas kernels for 55%

profile of v4, /device:TPU:0, one launch (start us, length us, event | category | flops | bytes accessed | tf_op | source)
XLA Modules:
  0.0 991.0 jit_solution(14899008069205024849)
XLA Ops:
  8.2 1.9 fusion.10
  14.2 32.7 %shard_map.305 = bf16[1792,576]{1,0:T(8,128)(2,1)} custom-call(bf16[224,576]{1,0:T(8,128)(2,1)} %concatenate.38.refs_0_), custom_call_target="tpu_custom_call" | custom-call | tf_op jit(solution)/shard_map/pallas_call | solution.py:212
  48.3 1.1 copy-done.40
  49.5 2.4 convolution_convert_fusion.5.refs_1_
  52.7 102.7 %shard_map.306 = (bf16[1792,896]{1,0:T(8,128)(2,1)}, bf16[1792,1152]{1,0:T(8,128)(2,1)}, bf16[448,512]{1,0:T(8,128)(2,1)}, bf16[288,1024]{1,0:T(8,128)(2,1)}, f32[224,1024]{1,0:T(8,128)}, /*index=5*/f32[8,1024]{1,0:T(8,128)}) custom-call(s32[4]{0:T(128)} %reshape.177.refs_0_, bf16[576,512]{1,0:T(8,128)(2,1)} %convolution_convert_fusion.5.refs_1_, ...), custom_call_target="tpu_custom_call" | custom-call | tf_op jit(solution)/shard_map/pallas_call | solution.py:212
  155.4 4.1 convolution_convert_fusion.3
  159.8 81.7 %shard_map.307 = (bf16[1792,1152]{1,0:T(8,128)(2,1)}, bf16[1792,1152]{1,0:T(8,128)(2,1)}) custom-call(bf16[224,1152]{1,0:T(8,128)(2,1)} %refs_0_, bf16[224,1152]{1,0:T(8,128)(2,1)} %bitcast.167), custom_call_target="tpu_custom_call" | custom-call | tf_op jit(solution)/shard_map/pallas_call | solution.py:212
  241.5 2.3 multiply_reduce_fusion.8
  244.6 2.1 copy-done.64
  246.6 2.5 fusion.39
  249.2 4.0 multiply_convert_fusion.8
  254.2 3.8 convolution_convert_fusion.2
  258.4 39.3 %shard_map.308 = (bf16[1792,448]{1,0:T(8,128)(2,1)}, bf16[1792,448]{1,0:T(8,128)(2,1)}) custom-call(bf16[224,448]{1,0:T(8,128)(2,1)} %refs_0_.1, bf16[224,448]{1,0:T(8,128)(2,1)} %refs_1_), custom_call_target="tpu_custom_call" | custom-call | tf_op jit(solution)/shard_map/pallas_call | solution.py:212
  297.8 7.8 all-reduce.12.cloned.1.call-done
  305.6 3.0 multiply_reduce_fusion.7
  309.0 2.4 copy-done.43
  312.5 3.5 collective-permute-start
  316.1 1.4 collective-permute-done
  317.8 2.6 multiply_convert_fusion.10
  321.3 2.5 convolution_convert_fusion.1
  324.2 125.5 %shard_map.309 = (bf16[1792,1152]{1,0:T(8,128)(2,1)}, bf16[1792,1152]{1,0:T(8,128)(2,1)}, bf16[1792,1152]{1,0:T(8,128)(2,1)}) custom-call(bf16[224,1152]{1,0:T(8,128)(2,1)} %refs_0_.2, bf16[224,1152]{1,0:T(8,128)(2,1)} %refs_1_.1, bf16[224,1152]{1,0:T(8,128)(2,1)} %bitcast.166), custom_call_target="tpu_custom_call" | custom-call | tf_op jit(solution)/shard_map/pallas_call | solution.py:212
  449.7 3.3 multiply_reduce_fusion.6
  454.6 2.3 copy-done.71
  456.8 2.6 fusion.42
  459.4 2.6 fusion.41
  462.1 4.3 multiply_convert_fusion.5
  466.4 2.6 fusion.43
  469.0 3.8 add_convert_fusion.3
  473.1 129.9 %shard_map.310 = (f32[224,1152]{1,0:T(8,128)}, f32[224,1152]{1,0:T(8,128)}, f32[224,1152]{1,0:T(8,128)}) custom-call(bf16[512,1792]{1,0:T(8,128)(2,1)} %copy-done.31, bf16[512,1792]{1,0:T(8,128)(2,1)} %bitcast.158, bf16[512,1152]{1,0:T(8,128)(2,1)} %copy-done.48, bf16[512,1152]{1,0:T(8,128)(2,1)} %copy-done.47, bf16[512,1152]{1,0:T(8,128)(2,1)} %get-tuple-element.148.refs_4_), custom_call_target="tpu_custom_call" | custom-call | tf_op jit(solution)/shard_map/pallas_call | solution.py:212
  603.0 1.9 convert_element_type.175
  605.6 1.2 copy-done.10
  608.4 1.3 fusion.30.refs_1_
  610.4 1.2 fusion.14
  613.7 1.3 collective-permute-start.1
  615.3 4.0 collective-permute-done.1
  620.9 1.2 fusion.44
  622.5 2.4 add_convert_fusion.1
  625.3 58.6 %shard_map.311 = (f32[224,448]{1,0:T(8,128)}, f32[224,448]{1,0:T(8,128)}, f32[224,448]{1,0:T(8,128)}) custom-call(bf16[512,1792]{1,0:T(8,128)(2,1)} %copy-done.19, bf16[512,1792]{1,0:T(8,128)(2,1)} %copy-done.29, bf16[512,448]{1,0:T(8,128)(2,1)} %copy-done.35, bf16[512,448]{1,0:T(8,128)(2,1)} %copy-done.36, bf16[512,448]{1,0:T(8,128)(2,1)} %copy-done.42), custom_call_target="tpu_custom_call" | custom-call | tf_op jit(solution)/shard_map/pallas_call | solution.py:212
  683.9 1.9 convert_element_type.180
  689.6 4.6 fusion.32
  694.2 3.1 multiply_convert_fusion.3
  697.3 2.6 fusion.45
  700.4 3.8 add_convert_fusion
  704.4 6.0 convolution_convert_fusion
  710.4 54.8 %shard_map.312 = f32[224,1152]{1,0:T(8,128)} custom-call(bf16[512,1792]{1,0:T(8,128)(2,1)} %copy-done.23, bf16[512,1152]{1,0:T(8,128)(2,1)} %copy-done.51), custom_call_target="tpu_custom_call" | custom-call | tf_op jit(solution)/shard_map/pallas_call | solution.py:212
  765.3 1.9 convert_element_type.185
  767.3 1.2 multiply_reduce_fusion.2
  769.2 1.5 copy-done.17
  770.7 1.2 fusion.31.refs_2_
  771.9 1.2 copy-done.28
  773.1 2.1 fusion.20.refs_1_
  775.2 108.3 %shard_map.313 = (f32[224,1152]{1,0:T(8,128)}, f32[224,1152]{1,0:T(8,128)}, bf16[576,512]{1,0:T(8,128)(2,1)}) custom-call(s32[4]{0:T(128)} %reshape.177.refs_0_, bf16[448,512]{1,0:T(8,128)(2,1)} %fusion.20.refs_1_, bf16[288,1024]{1,0:T(8,128)(2,1)} %get-tuple-element.93.refs_2_, f32[224,1024]{1,0:T(8,128)} %get-tuple-element.94.refs_3_, ...), custom_call_target="tpu_custom_call" | custom-call | tf_op jit(solution)/shard_map/pallas_call | solution.py:212
  883.6 4.5 fusion.5
  888.8 1.4 collective-permute-start.4
  892.5 54.5 %shard_map.314 = (f32[224,576]{1,0:T(8,128)}, f32[224,448]{1,0:T(8,128)}, f32[8,1792]{1,0:T(8,128)}) custom-call(f32[8,1792]{1,0:T(8,128)} %concatenate.48.refs_0_, bf16[512,1792]{1,0:T(8,128)(2,1)} %copy-done.30, bf16[512,1792]{1,0:T(8,128)(2,1)} %copy-done.28, bf16[576,512]{1,0:T(8,128)(2,1)} %get-tuple-element.96.refs_3_, ...), custom_call_target="tpu_custom_call" | custom-call | tf_op jit(solution)/shard_map/pallas_call | solution.py:212
  947.1 1.4 slice.160
  948.5 1.3 slice.159
  949.8 1.2 fusion.34
  952.7 2.0 copy.52
  954.7 1.3 fusion.33
  956.9 9.0 all-reduce.22.cloned.1.call-done
  965.9 1.9 convert_element_type.189
  970.5 4.0 fusion.9
  974.5 1.8 add_convert_fusion.2
  (247 shorter events, 43.1 us)
Async XLA Ops:
  7.2 40.6 %copy-start.5 = (bf16[2,2,128,1792]{3,2,1,0:T(8,128)(2,1)S(1)}, bf16[2,2,128,1792]{3,2,1,0:T(8,128)(2,1)}, u32[]{:S(2)}) copy-start(bf16[2,2,128,1792]{3,2,1,0:T(8,128)(2,1)} %param.18) | copy-start | bytes 5505028
  7.2 39.7 %copy-start.76 = (s32[2,2]{1,0:T(2,128)S(1)}, s32[2,2]{1,0:T(2,128)}, u32[]{:S(2)}) copy-start(s32[2,2]{1,0:T(2,128)} %param.19) | copy-start | bytes 52
  7.2 40.3 %copy-start.60 = (bf16[448,224]{1,0:T(8,128)(2,1)S(1)}, bf16[448,224]{1,0:T(8,128)(2,1)}, u32[]{:S(2)}) copy-start(bf16[448,224]{1,0:T(8,128)(2,1)} %param.24) | copy-start | bytes 602116
  7.2 40.4 %copy-start.61 = (bf16[448,224]{1,0:T(8,128)(2,1)S(1)}, bf16[448,224]{1,0:T(8,128)(2,1)}, u32[]{:S(2)}) copy-start(bf16[448,224]{1,0:T(8,128)(2,1)} %param.30) | copy-start | bytes 602116
  7.2 234.2 %all-reduce.10.cloned.1.call-start = ((), (), s32[]{:S(2)}) async-start(), calls=%async_computation | async-start | bytes 3670016 | tf_op jit(solution)/shard_map/psum | solution.py:675
  159.5 146.1 %all-reduce.12.cloned.1.call-start = ((), (), s32[]{:S(2)}) async-start(), calls=%async_computation.1 | async-start | bytes 3670016 | tf_op jit(solution)/shard_map/psum | solution.py:675
  243.8 2.8 copy-start.64
  244.5 4.6 copy-start.23
  249.2 4.0 copy-start.77
  249.2 5.0 copy-start.68
  254.2 3.9 copy-start.63
  258.1 191.6 %all-reduce.14.cloned.1.call-start = ((), (), s32[]{:S(2)}) async-start(), calls=%async_computation.2 | async-start | bytes 3670016 | tf_op jit(solution)/shard_map/psum | solution.py:675
  308.5 4.0 copy-start
  308.5 2.9 copy-start.43
  309.0 8.8 copy-start.19
  309.0 7.1 copy-start.62
  312.5 5.3 copy-start.32
  312.5 4.9 collective-permute-start
  317.8 2.7 copy-start.24
  317.8 2.7 copy-start.26
  317.8 3.4 copy-start.73
  323.8 279.2 %all-reduce.16.cloned.1.call-start = ((), (), s32[]{:S(2)}) async-start(), calls=%async_computation.3 | async-start | bytes 3670016 | tf_op jit(solution)/shard_map/psum | solution.py:675
  449.7 3.7 copy-start.1
  449.7 4.2 copy-start.9
  454.0 2.8 copy-start.71
  454.5 4.8 copy-start.31
  456.8 2.6 copy-start.72
  459.4 2.6 copy-start.20
  459.4 2.7 copy-start.70
  472.9 211.0 %all-reduce.18.cloned.1.call-start = ((), (), s32[]{:S(2)}) async-start(), calls=%async_computation.4 | async-start | bytes 3670016 | tf_op jit(solution)/shard_map/psum | solution.py:675
  603.0 3.7 copy-start.10
  604.9 3.1 copy-start.15
  610.3 3.3 copy-start.29
  610.4 2.8 copy-start.38
  613.7 8.3 copy-start.36
  613.7 5.6 collective-permute-start.1
  625.0 140.3 %all-reduce.20.cloned.1.call-start = ((), (), s32[]{:S(2)}) async-start(), calls=%async_computation.5 | async-start | bytes 3670016 | tf_op jit(solution)/shard_map/psum | solution.py:675
  686.4 3.1 copy-start.22
  689.6 4.6 copy-start.69
  689.6 4.6 copy-start.78
  689.6 4.6 copy-start.79
  694.2 3.1 copy-start.34
  694.2 3.1 copy-start.65
  697.3 2.6 copy-start.51
  697.3 2.6 copy-start.50
  697.3 3.0 copy-start.67
  700.4 4.1 copy-start.46
  704.2 261.7 %all-reduce.22.cloned.1.call-start = ((), (), s32[]{:S(2)}) async-start(), calls=%async_computation.6 | async-start | bytes 7340032 | tf_op jit(solution)/shard_map/psum | solution.py:675
  767.3 3.4 copy-start.17
  775.2 108.3 %copy-start.41 = (bf16[1792,576]{1,0:T(8,128)(2,1)S(1)}, bf16[1792,576]{1,0:T(8,128)(2,1)}, u32[]{:S(2)}) copy-start(bf16[1792,576]{1,0:T(8,128)(2,1)} %shard_map.305) | copy-start | bytes 6193156
  888.1 3.1 collective-permute-start.2
  888.1 3.7 collective-permute-start.3
  888.8 3.0 collective-permute-start.4
  965.9 2.7 copy-start.18
  967.8 2.7 copy-start.14
  970.5 4.0 copy-start.4
  970.5 4.0 copy-start.12
  970.5 4.0 copy-start.45
  974.5 2.8 copy-start.56
  976.3 2.9 copy-start.58
  976.3 3.7 copy-start.57
  976.3 4.4 copy-start.54
  977.3 4.4 copy-start.53
  978.3 4.4 copy-start.52
  (28 other events, 54.8 us)
Sparse Core Ops, SparseCore 0:
  159.6 49.7 all-reduce.9
  258.2 47.3 all-reduce.11
  323.9 47.9 all-reduce.13
  473.0 46.3 all-reduce.15
  625.1 46.4 all-reduce.17
  704.3 46.5 all-reduce.19
  888.2 77.6 all-reduce.21

commit v5 on v4

--- a/solution.py
+++ b/solution.py
@@ -96,8 +96,10 @@
                 self.copy(k, d).wait_send()
 
 
-def by_block(height):
-    return lambda ref, owner: ref.at[pl.ds(pl.multiple_of(owner * height, min(height, 32)), height)]
+def by_block(height, first=0, rows=None):
+    rows = height if rows is None else rows
+    unit = 8 if height % 16 else 16
+    return lambda ref, owner: ref.at[pl.ds(pl.multiple_of(owner * height + first, unit), rows)]
 
 
 def by_position(tok):
@@ -136,12 +138,27 @@
     def sems(self, name, *shape):
         self.scratch[name] = pltpu.SemaphoreType.DMA(shape)
 
-    def gather(self, name, src, out, place, flip=False):
+    def gather_blocks(self, name, array, flip=False):
+        height = array.shape[0]
+        self.take(name + ".src", array, pl.ANY)
+        self.give(name, (self.n * height,) + array.shape[1:], array.dtype, pl.ANY)
+        half = height // 2
+        for p in range(2):
+            self.gather(
+                f"{name}.{p}",
+                name + ".src",
+                name,
+                by_block(height, p * half, half),
+                bool(p) != flip,
+                (p * half, half),
+            )
+
+    def gather(self, name, src, out, place, flip=False, rows=None):
         half = self.n // 2
         self.sems(name + ".send", 2, half)
         self.sems(name + ".recv", 2, half)
         self.sems(name + ".local", 1)
-        self.gathers[name] = (src, out, place, flip)
+        self.gathers[name] = (src, out, place, flip, rows)
 
     def left(self, name, array):
         self.take(name, array)
@@ -151,14 +168,18 @@
     def scatter(self, name, left, right, flip=False, axis=0):
         n = self.n
         height = self.ins[left][0].shape[1] // n
-        block = (height, right.shape[1 - axis])
+        width = right.shape[1 - axis]
         self.take(name + ".right", right)
-        self.give(name, block, F32)
-        self.hold(name + ".sums", (2, n // 2) + block, BF)
-        self.hold(name + ".slots", (2, n // 2) + block, BF)
-        self.sems(name + ".send", 2, n // 2)
-        self.sems(name + ".recv", 2, n // 2)
-        self.scatters[name] = (left, flip, axis)
+        self.give(name, (height, width), F32)
+        cut = -(-width // 256) * 128
+        for p, span in enumerate(((0, cut), (cut, width))):
+            part = f"{name}.{p}"
+            block = (height, span[1] - span[0])
+            self.hold(part + ".sums", (2, n // 2) + block, BF)
+            self.hold(part + ".slots", (2, n // 2) + block, BF)
+            self.sems(part + ".send", 2, n // 2)
+            self.sems(part + ".recv", 2, n // 2)
+            self.scatters[part] = (name, left, bool(p) != flip, axis, span)
 
     def kernel(self, body, *refs):
         names = list(self.ins) + list(self.outs) + list(self.scratch)
@@ -167,11 +188,11 @@
         rings = {}
         if self.early is not None:
             self.early(at)
-        for name, (src, out, place, flip) in self.gathers.items():
+        for name, (src, out, place, flip, rows) in self.gathers.items():
             rings[name] = GatherRing(
                 self.n,
                 where,
-                at[src],
+                at[src] if rows is None else at[src].at[pl.ds(*rows)],
                 at[out],
                 place,
                 at[name + ".send"],
@@ -180,7 +201,7 @@
                 flip,
             )
         ready = set()
-        for name, (left, flip, axis) in self.scatters.items():
+        for name, (whole, left, flip, axis, span) in self.scatters.items():
             blocked = at[left + ".blocked"]
             if left not in ready:
                 ready.add(left)
@@ -191,14 +212,15 @@
                 self.n,
                 where,
                 blocked,
-                at[name + ".right"],
-                at[name],
+                at[whole + ".right"],
+                at[whole],
                 at[name + ".sums"],
                 at[name + ".slots"],
                 at[name + ".send"],
                 at[name + ".recv"],
                 flip,
                 axis,
+                span,
             )
             rings[name].step()
         body(at, rings)
@@ -238,16 +260,14 @@
     call = Call(call_id)
     names = [str(j) for j in range(len(arrays))]
     for j, (name, a) in enumerate(zip(names, arrays)):
-        call.take(name + ".src", a, pl.ANY)
-        call.give(name, (n * a.shape[0],) + a.shape[1:], a.dtype, pl.ANY)
-        call.gather(name, name + ".src", name, by_block(a.shape[0]), (j + flip) % 2 == 1)
+        call.gather_blocks(name, a, (j + flip) % 2 == 1)
     out = call.run(in_turn(n))
     return [out[name] for name in names]
 
 
 class ScatterRing:
-    def __init__(self, n, where, left, right, out, sums, slots, send, recv, flip, axis):
-        self.axis = axis
+    def __init__(self, n, where, left, right, out, sums, slots, send, recv, flip, axis, span):
+        self.axis, self.span = axis, slice(*span)
         self.n, self.left_ref, self.right_ref, self.out = n, left, right, out
         self.sums, self.slots, self.send, self.recv = sums, slots, send, recv
         self.pos, self.right, self.left = where
@@ -259,7 +279,8 @@
 
     def term(self, r):
         owner = ring_device(lax.rem(self.pos + (r % self.n), self.n))
-        return dot(self.left_ref[owner], self.right_ref[...], 0, self.axis)
+        right = self.right_ref[:, self.span] if self.axis == 0 else self.right_ref[self.span]
+        return dot(self.left_ref[owner], right, 0, self.axis)
 
     def copy(self, d, h):
         i = 0 if d == 1 else 1
@@ -296,13 +317,13 @@
             i, h = (0 if d == 1 else 1), self.hops[d]
             self.copy(d, h).wait_recv()
             total = total + self.slots[i, h - 1].astype(F32)
-        self.out[...] = total
+        self.out[:, self.span] = total
         for d in self.order:
             for h in range(1, self.hops[d] + 1):
                 self.copy(d, h).wait_send()
 
 
-def scatter_all(lefts, pairs, call_id, flip=0, small=None):
+def scatter_all(lefts, pairs, call_id, flip=0, small=None, after=()):
     n = lax.axis_size("seq")
     pairs = [p if len(p) == 3 else p + (0,) for p in pairs]
     if not ring_size(n):
@@ -315,6 +336,8 @@
         return sums if small is None else sums + [lax.psum(small.astype(BF), "seq").astype(F32)]
     call = Call(call_id)
     names = [str(j) for j in range(len(pairs))]
+    for j, a in enumerate(after):
+        call.take(f"after{j}", a, pl.ANY)
     if small is not None:
         call.take("small.src", small)
         call.hold("small.all", (n * small.shape[0], small.shape[1]), F32)
@@ -507,9 +530,7 @@
     call.take("off", off, pltpu.SMEM)
     call.take("qkv", qkv)
     for j, a in enumerate(carried):
-        call.take(f"c{j}.src", a, pl.ANY)
-        call.give(f"c{j}", (n * a.shape[0], a.shape[1]), a.dtype, pl.ANY)
-        call.gather(f"c{j}", f"c{j}.src", f"c{j}", by_block(a.shape[0]), j % 2 == 1)
+        call.gather_blocks(f"c{j}", a, j % 2 == 1)
     call.give("mixed", (2 * vf, qkv.shape[1]), BF)
     call.give("all", (features, n * tok), BF)
     call.give("att", (vf, n * tok), F32)
@@ -552,9 +573,10 @@
             n, at, "out", at_positions(at["own"], tok), lambda me: to_pair(at["mixed"], vf, tok)(me)
         )
         leaving.start()
-        turn()
+        for _ in range(n // 2):
+            turn()
+        arriving.wait_sent()
         leaving.wait()
-        arriving.wait_sent()
         leaving.wait_sent()
 
     out = call.run(body, lambda at: incoming(at).start())
@@ -626,10 +648,11 @@
             n, at, "out", at_positions(at["own"], tok), lambda me: to_pair(at["d"], features, tok)(me)
         )
         leaving.start()
-        for ring in rings.values():
-            ring.step()
+        for _ in range(n // 2):
+            for ring in rings.values():
+                ring.step()
+        arriving.wait_sent()
         leaving.wait()
-        arriving.wait_sent()
         leaving.wait_sent()
 
     out = call.run(body, lambda at: incoming(at).start())
@@ -793,7 +816,7 @@
     resid_one = inputs + attn_sum
     part, kept_one = mlp_forward(resid_one, gains[1], ffn1)
     ffn1_sum = head_total(part)
-    inner_w, gate_w = gather_all(tie((conv_input, conv_gate), part), 4)
+    inner_w, gate_w, gate_2 = gather_all(tie((conv_input, conv_gate, ffn2_gate), part), 4)
     resid_two = resid_one + ffn1_sum
 
     normed_c = rms_norm(resid_two, gains[2]).astype(BF)
@@ -814,16 +837,16 @@
     product = (conv * gate_c).astype(BF).reshape(count, cw)
     conv_part = dot(product, conv_out_t, 1, 1).astype(BF)
     conv_sum = head_total(conv_part)
-    ffn2 = gather_all(tie((ffn2_gate, ffn2_up, ffn2_down.T), conv_part), 3)
+    ffn2 = [gate_2] + gather_all(tie((ffn2_up, ffn2_down.T), conv_part), 12)
     resid_three = resid_two + conv_sum
     out_part, kept_two = mlp_forward(resid_three, gains[3], ffn2)
 
     dn_part, grads_two = mlp_backward(grad_four, kept_two, ffn2)
-    dn = head_total(dn_part)
-    sums_two = mlp_scatter(grads_two, 5, dn_part)
+    both = lax.psum(jnp.concatenate([dn_part, out_part]), "head")
+    dn, out_sum = both[:count].astype(F32), both[count:]
+    sums_two = mlp_scatter(grads_two, 5, dn_part, out_part)
     (dn,) = tie((dn,), *sums_two)
-    out_sum = head_total(tie((out_part,), *sums_two)[0])
-    block_output = (resid_three + out_sum).astype(BF).reshape(activations.shape)
+    block_output = (resid_three + out_sum.astype(F32)).astype(BF).reshape(activations.shape)
     dx, gain_four = rms_back(resid_three, gains[3], dn)
     grad_three = grad_four.astype(F32) + dx
     grad_b = grad_three.astype(BF)
@@ -840,7 +863,10 @@
     dn_part = (dot(d_inner, inner_w, 1, 1) + dot(d_gate_c, gate_w, 1, 1)).astype(BF)
     dn = head_total(dn_part)
     sums_conv = scatter_all(
-        tie((normed_c, grad_b), dn_part), ((0, d_inner), (0, d_gate_c), (1, product)), 6, 1
+        tie((normed_c, grad_b), dn_part),
+        ((0, d_inner), (0, d_gate_c), (1, product)),
+        6,
+        1,
     )
     (dn,) = tie((dn,), *sums_conv)
     dx, gain_three = rms_back(resid_two, gains[2], dn)
@@ -888,8 +914,10 @@
             jnp.zeros((8 - 4 - taps, width), F32),
         ]
     )
+    if paired:
+        d_qkv, mixed = d_qkv.T, mixed.T
     sums_attn = scatter_all(
-        tie((normed_a, grad_b), dn_part), ((0, d_qkv, mixed_axis), (1, mixed, mixed_axis)), 8, 0, small
+        tie((normed_a, grad_b), dn_part), ((0, d_qkv), (1, mixed)), 8, 0, small
     )
     gains_grad, kernel_grad = sums_attn[2][:4], sums_attn[2][4 : 4 + taps, :cw]
     qkv_sum = sums_attn[0]

time: 998 us -> 937 us (0.939)
  Pallas kernels: 788 us -> 744 us
  waiting for transfers between devices: 23 us -> 9.57 us
    pallas_call x10, Pallas kernels: 788 us -> 744 us  [run(): pl.pallas_call(partial(self.kernel, body), in_specs=[spec for _, spec in...]
    psum x7 -> x6, waiting for transfers between devices: 16.9 us -> 3.98 us  [head_total(): return lax.psum(partial_sum, 'head').astype(F32)]
    unnamed x178 -> x180, local copies, waits for them, and re-layouts: 37.9 us -> 38 us
  transfers between devices with their start and end apart: 12 -> 12, of which waited for: 5 -> 3; matrix products, arithmetic and copies ran while one was open for 2% -> 2% of each run, Pallas kernels for 55% -> 56%
where the time goes in v5:
time: 937 us; the launch traced here: 930 us
  Pallas kernels  744 us (79%)
  matrix products  60 us (6%)
  local copies, waits for them, and re-layouts  50.6 us (5%)
  other arithmetic  43.7 us (5%)
  between operations  15.5 us (2%)
  waiting for transfers between devices  9.57 us (1%)
    pallas_call x10, Pallas kernels, run(): pl.pallas_call(partial(self.kernel, body), in_specs=[spec for _, spec in...  744 us
    dot_general x22, matrix products, dot(): lax.dot_general(a, b, (((ca,), (cb,)), ((), ())), preferred_element_type=...  60 us
    unnamed x180, local copies, waits for them, and re-layouts  38 us
  transfers between devices with their start and end apart: 12, of which 3 were waited for; matrix products, arithmetic and copies ran while one was open for 2% of the time, Pallas kernels for 56%

profile of v5, /device:TPU:0, one launch (start us, length us, event | category | flops | bytes accessed | tf_op | source)
XLA Modules:
  0.0 930.4 jit_solution(6425908064950240275)
XLA Ops:
  8.2 1.9 fusion.10
  14.2 29.1 %shard_map.305 = bf16[1792,576]{1,0:T(8,128)(2,1)} custom-call(bf16[224,576]{1,0:T(8,128)(2,1)} %concatenate.41.refs_0_), custom_call_target="tpu_custom_call" | custom-call | tf_op jit(solution)/shard_map/pallas_call | solution.py:234
  44.7 1.1 copy-done.38
  45.8 2.4 convolution_convert_fusion.5.refs_1_
  49.1 90.9 %shard_map.306 = (bf16[1792,896]{1,0:T(8,128)(2,1)}, bf16[1792,1152]{1,0:T(8,128)(2,1)}, bf16[448,512]{1,0:T(8,128)(2,1)}, bf16[288,1024]{1,0:T(8,128)(2,1)}, f32[224,1024]{1,0:T(8,128)}, /*index=5*/f32[8,1024]{1,0:T(8,128)}) custom-call(s32[4]{0:T(128)} %reshape.177.refs_0_, bf16[576,512]{1,0:T(8,128)(2,1)} %convolution_convert_fusion.5.refs_1_, ...), custom_call_target="tpu_custom_call" | custom-call | tf_op jit(solution)/shard_map/pallas_call | solution.py:234
  140.0 4.1 convolution_convert_fusion.3
  144.3 86.0 %shard_map.307 = (bf16[1792,1152]{1,0:T(8,128)(2,1)}, bf16[1792,1152]{1,0:T(8,128)(2,1)}) custom-call(bf16[224,1152]{1,0:T(8,128)(2,1)} %refs_0_, bf16[224,1152]{1,0:T(8,128)(2,1)} %bitcast.170), custom_call_target="tpu_custom_call" | custom-call | tf_op jit(solution)/shard_map/pallas_call | solution.py:234
  230.4 2.3 multiply_reduce_fusion.8
  233.4 2.1 copy-done.65
  235.5 2.5 fusion.39
  238.1 4.1 multiply_convert_fusion.8
  243.2 3.8 convolution_convert_fusion.2
  247.4 75.3 %shard_map.308 = (bf16[1792,448]{1,0:T(8,128)(2,1)}, bf16[1792,448]{1,0:T(8,128)(2,1)}, bf16[1792,1152]{1,0:T(8,128)(2,1)}) custom-call(bf16[224,448]{1,0:T(8,128)(2,1)} %refs_0_.1, bf16[224,448]{1,0:T(8,128)(2,1)} %refs_1_, bf16[224,1152]{1,0:T(8,128)(2,1)} %refs_2_), custom_call_target="tpu_custom_call" | custom-call | tf_op jit(solution)/shard_map/pallas_call | solution.py:234
  322.8 3.0 multiply_reduce_fusion.7
  326.1 2.4 copy-done.41
  328.6 1.1 fusion.40
  329.7 2.6 collective-permute-start
  332.3 1.4 collective-permute-done
  334.1 2.6 multiply_convert_fusion.10
  337.5 2.5 convolution_convert_fusion.1
  340.4 80.0 %shard_map.309 = (bf16[1792,1152]{1,0:T(8,128)(2,1)}, bf16[1792,1152]{1,0:T(8,128)(2,1)}) custom-call(bf16[224,1152]{1,0:T(8,128)(2,1)} %refs_0_.2, bf16[224,1152]{1,0:T(8,128)(2,1)} %bitcast.171), custom_call_target="tpu_custom_call" | custom-call | tf_op jit(solution)/shard_map/pallas_call | solution.py:234
  420.5 3.3 multiply_reduce_fusion.6
  425.3 2.3 copy-done.72
  427.5 2.5 fusion.41
  430.1 2.6 fusion.42
  432.8 3.2 multiply_convert_fusion.6
  436.1 2.6 fusion.43
  438.7 2.6 convolution_convert_fusion
  441.3 2.6 add_convert_fusion.3
  444.0 2.2 pad_maximum_fusion
  446.3 122.2 %shard_map.310 = (f32[224,1152]{1,0:T(8,128)}, f32[224,1152]{1,0:T(8,128)}, f32[224,1152]{1,0:T(8,128)}) custom-call(bf16[512,1792]{1,0:T(8,128)(2,1)} %copy-done.29, bf16[512,1792]{1,0:T(8,128)(2,1)} %bitcast.160, bf16[512,1152]{1,0:T(8,128)(2,1)} %copy-done.44, bf16[512,1152]{1,0:T(8,128)(2,1)} %copy-done.43, bf16[512,1152]{1,0:T(8,128)(2,1)} %copy-done.45), custom_call_target="tpu_custom_call" | custom-call | tf_op jit(solution)/shard_map/pallas_call | solution.py:234
  568.5 1.9 slice_convert_fusion
  571.1 1.2 copy-done.13
  573.8 1.3 fusion.30.refs_1_
  575.7 1.2 fusion.14
  579.0 1.3 collective-permute-start.1
  580.6 4.0 collective-permute-done.1
  586.2 1.2 fusion.44
  587.9 2.4 add_convert_fusion.1
  590.7 54.4 %shard_map.311 = (f32[224,448]{1,0:T(8,128)}, f32[224,448]{1,0:T(8,128)}, f32[224,448]{1,0:T(8,128)}) custom-call(bf16[512,1792]{1,0:T(8,128)(2,1)} %copy-done.20, bf16[512,1792]{1,0:T(8,128)(2,1)} %copy-done.26, bf16[512,448]{1,0:T(8,128)(2,1)} %copy-done.33, bf16[512,448]{1,0:T(8,128)(2,1)} %copy-done.34, bf16[512,448]{1,0:T(8,128)(2,1)} %copy-done.40), custom_call_target="tpu_custom_call" | custom-call | tf_op jit(solution)/shard_map/pallas_call | solution.py:234
  645.2 1.9 convert_element_type.180
  650.9 6.2 fusion.32
  657.2 3.1 multiply_convert_fusion.3
  660.3 2.6 fusion.45
  663.3 3.8 add_convert_fusion
  668.4 41.2 %shard_map.312 = f32[224,1152]{1,0:T(8,128)} custom-call(bf16[512,1792]{1,0:T(8,128)(2,1)} %copy-done.21, bf16[512,1152]{1,0:T(8,128)(2,1)} %copy-done.48), custom_call_target="tpu_custom_call" | custom-call | tf_op jit(solution)/shard_map/pallas_call | solution.py:234
  709.6 3.9 all-reduce.19.cloned.1.call-done
  713.5 1.9 convert_element_type.185
  715.6 1.2 multiply_reduce_fusion.2
  717.5 1.5 copy-done.15
  719.0 1.2 fusion.31.refs_2_
  720.2 1.3 copy-done.28
  721.5 2.1 fusion.20.refs_1_
  723.6 106.3 %shard_map.313 = (f32[224,1152]{1,0:T(8,128)}, f32[224,1152]{1,0:T(8,128)}, bf16[576,512]{1,0:T(8,128)(2,1)}) custom-call(s32[4]{0:T(128)} %reshape.177.refs_0_, bf16[448,512]{1,0:T(8,128)(2,1)} %fusion.20.refs_1_, bf16[288,1024]{1,0:T(8,128)(2,1)} %get-tuple-element.91.refs_2_, f32[224,1024]{1,0:T(8,128)} %get-tuple-element.92.refs_3_, ...), custom_call_target="tpu_custom_call" | custom-call | tf_op jit(solution)/shard_map/pallas_call | solution.py:234
  829.9 4.4 fusion.5
  835.1 1.4 collective-permute-start.4
  839.4 58.2 %shard_map.314 = (f32[224,576]{1,0:T(8,128)}, f32[224,448]{1,0:T(8,128)}, f32[8,1792]{1,0:T(8,128)}) custom-call(f32[8,1792]{1,0:T(8,128)} %concatenate.52.refs_0_, bf16[512,1792]{1,0:T(8,128)(2,1)} %copy-done.30, bf16[512,1792]{1,0:T(8,128)(2,1)} %copy-done.28, bf16[512,576]{1,0:T(8,128)(2,1)} %bitcast.163, bf16[512,448]{1,0:T(8,128)(2,1)} %bitcast.164), custom_call_target="tpu_custom_call" | custom-call | tf_op jit(solution)/shard_map/pallas_call | solution.py:234
  897.6 1.4 slice.168
  899.0 1.3 slice.167
  900.3 1.2 fusion.34
  903.2 2.0 copy.54
  905.2 1.3 fusion.33
  907.4 1.9 convert_element_type.189
  912.1 4.0 fusion.9
  (251 shorter events, 43.5 us)
Async XLA Ops:
  7.2 37.0 %copy-start.4 = (bf16[2,2,128,1792]{3,2,1,0:T(8,128)(2,1)S(1)}, bf16[2,2,128,1792]{3,2,1,0:T(8,128)(2,1)}, u32[]{:S(2)}) copy-start(bf16[2,2,128,1792]{3,2,1,0:T(8,128)(2,1)} %param.18) | copy-start | bytes 5505028
  7.2 36.1 %copy-start.77 = (s32[2,2]{1,0:T(2,128)S(1)}, s32[2,2]{1,0:T(2,128)}, u32[]{:S(2)}) copy-start(s32[2,2]{1,0:T(2,128)} %param.19) | copy-start | bytes 52
  7.2 36.6 %copy-start.59 = (bf16[448,224]{1,0:T(8,128)(2,1)S(1)}, bf16[448,224]{1,0:T(8,128)(2,1)}, u32[]{:S(2)}) copy-start(bf16[448,224]{1,0:T(8,128)(2,1)} %param.24) | copy-start | bytes 602116
  7.2 36.8 %copy-start.60 = (bf16[448,224]{1,0:T(8,128)(2,1)S(1)}, bf16[448,224]{1,0:T(8,128)(2,1)}, u32[]{:S(2)}) copy-start(bf16[448,224]{1,0:T(8,128)(2,1)} %param.30) | copy-start | bytes 602116
  7.2 223.1 %all-reduce.9.cloned.1.call-start = ((), (), s32[]{:S(2)}) async-start(), calls=%async_computation | async-start | bytes 3670016 | tf_op jit(solution)/shard_map/psum | solution.py:698
  8.2 36.4 %copy-start.61 = (f32[1792]{0:T(1024)}, f32[1792]{0:T(1024)S(1)}, u32[]{:S(2)}) copy-start(f32[1792]{0:T(1024)S(1)} %get-tuple-element.132) | copy-start | bytes 21508
  144.1 178.7 %all-reduce.11.cloned.1.call-start = ((), (), s32[]{:S(2)}) async-start(), calls=%async_computation.1 | async-start | bytes 3670016 | tf_op jit(solution)/shard_map/psum | solution.py:698
  232.7 2.8 copy-start.65
  233.4 4.6 copy-start.21
  238.0 4.1 copy-start.78
  238.1 5.1 copy-start.69
  243.2 3.9 copy-start.64
  247.0 173.4 %all-reduce.13.cloned.1.call-start = ((), (), s32[]{:S(2)}) async-start(), calls=%async_computation.2 | async-start | bytes 3670016 | tf_op jit(solution)/shard_map/psum | solution.py:698
  325.7 4.0 copy-start
  325.7 2.9 copy-start.41
  326.1 7.9 copy-start.20
  326.1 6.2 copy-start.63
  329.7 4.4 copy-start.31
  329.7 4.0 collective-permute-start
  334.0 2.7 copy-start.22
  334.0 2.7 copy-start.24
  334.1 3.4 copy-start.74
  336.7 83.7 %copy-start.40 = (bf16[512,448]{1,0:T(8,128)(2,1)}, bf16[512,448]{1,0:T(8,128)(2,1)S(1)}, u32[]{:S(2)}) copy-start(bf16[512,448]{1,0:T(8,128)(2,1)S(1)} %get-tuple-element.136.refs_4_) | copy-start | bytes 1376260
  340.0 228.5 %all-reduce.15.cloned.1.call-start = ((), (), s32[]{:S(2)}) async-start(), calls=%async_computation.3 | async-start | bytes 7340032 | tf_op jit(solution)/shard_map/psum | solution.py:845
  420.4 3.7 copy-start.1
  420.5 4.2 copy-start.12
  424.7 2.8 copy-start.72
  425.3 4.8 copy-start.29
  430.1 2.7 copy-start.73
  436.1 5.2 copy-start.43
  446.2 199.0 %all-reduce.17.cloned.1.call-start = ((), (), s32[]{:S(2)}) async-start(), calls=%async_computation.4 | async-start | bytes 3670016 | tf_op jit(solution)/shard_map/psum | solution.py:698
  568.5 3.8 copy-start.13
  570.4 2.9 copy-start.10
  575.7 3.3 copy-start.26
  575.7 2.8 copy-start.36
  579.0 8.3 copy-start.34
  579.0 5.6 collective-permute-start.1
  590.3 123.3 %all-reduce.19.cloned.1.call-start = ((), (), s32[]{:S(2)}) async-start(), calls=%async_computation.5 | async-start | bytes 3670016 | tf_op jit(solution)/shard_map/psum | solution.py:698
  647.8 3.2 copy-start.19
  650.9 6.2 copy-start.70
  650.9 6.2 copy-start.79
  650.9 6.2 copy-start.80
  657.1 3.1 copy-start.27
  657.2 3.1 copy-start.66
  660.3 3.0 copy-start.68
  663.3 4.1 copy-start.58
  667.1 240.3 %all-reduce.21.cloned.1.call-start = ((), (), s32[]{:S(2)}) async-start(), calls=%async_computation.6 | async-start | bytes 3670016 | tf_op jit(solution)/shard_map/psum | solution.py:698
  715.6 3.4 copy-start.15
  723.6 106.3 %copy-start.39 = (bf16[1792,576]{1,0:T(8,128)(2,1)S(1)}, bf16[1792,576]{1,0:T(8,128)(2,1)}, u32[]{:S(2)}) copy-start(bf16[1792,576]{1,0:T(8,128)(2,1)} %shard_map.305) | copy-start | bytes 6193156
  829.9 6.6 copy-start.57
  829.9 7.6 copy-start.54
  834.4 4.2 collective-permute-start.2
  834.4 4.2 collective-permute-start.3
  835.1 3.6 collective-permute-start.4
  905.2 4.1 copy-start.62
  907.4 2.8 copy-start.16
  909.3 2.7 copy-start.9
  912.0 4.0 copy-start.37
  912.1 5.0 copy-start.53
  916.0 2.9 copy-start.56
  916.0 3.7 copy-start.55
  916.1 4.4 copy-start.51
  917.0 4.4 copy-start.50
  918.0 4.4 copy-start.49
  (29 other events, 61.2 us)
Sparse Core Ops, SparseCore 0:
  144.2 51.8 all-reduce.8
  247.1 46.2 all-reduce.10
  340.1 47.9 all-reduce.12
  446.3 75.9 all-reduce.14
  590.4 46.1 all-reduce.16
  667.2 46.2 all-reduce.18
  838.7 50.7 all-reduce.20

commit v6 on v5

--- a/solution.py
+++ b/solution.py
@@ -186,8 +186,6 @@
         at = dict(zip(names, refs))
         where = greet(self.n, bool(self.exchanges))
         rings = {}
-        if self.early is not None:
-            self.early(at)
         for name, (src, out, place, flip, rows) in self.gathers.items():
             rings[name] = GatherRing(
                 self.n,
@@ -227,10 +225,7 @@
         for ring in rings.values():
             ring.finish()
 
-    early = None
-
-    def run(self, body, early=None):
-        self.early = early
+    def run(self, body):
         outs = pl.pallas_call(
             partial(self.kernel, body),
             in_specs=[spec for _, spec in self.ins.values()],
@@ -263,6 +258,30 @@
         call.gather_blocks(name, a, (j + flip) % 2 == 1)
     out = call.run(in_turn(n))
     return [out[name] for name in names]
+
+
+def gather_beside_norm(x, gain, array, call_id):
+    n = lax.axis_size("seq")
+    if not ring_size(n):
+        normed = rms_norm(x.astype(F32), gain[0]).astype(BF)
+        return normed, lax.all_gather(array, "seq", axis=0, tiled=True)
+    call = Call(call_id)
+    call.take("x", x)
+    call.take("gain", gain)
+    call.give("normed", x.shape, BF)
+    call.gather_blocks("w", array)
+    rows = x.shape[0] // n
+
+    def body(at, rings):
+        for k in range(n):
+            if k % 2 == 0:
+                for ring in rings.values():
+                    ring.step()
+            lines = slice(k * rows, (k + 1) * rows)
+            at["normed"][lines] = rms_norm(at["x"][lines].astype(F32), at["gain"][...]).astype(BF)
+
+    out = call.run(body)
+    return out["normed"], out["w"]
 
 
 class ScatterRing:
@@ -521,17 +540,21 @@
     return (earlier <= pos) & ((earlier >= offset) | (pos < offset))
 
 
-def attend_pairs(off, qkv, carried, call_id):
+def attend_pairs(off, weight, normed, carried, call_id):
     n = lax.axis_size("seq")
-    tok = qkv.shape[1] * 2 // n
-    features = qkv.shape[0] // 2
+    count = normed.shape[0]
+    tok = count * 2 // n
+    features = weight.shape[1] // 2
     vf = features - 4 * QK
     call = Call(call_id)
     call.take("off", off, pltpu.SMEM)
-    call.take("qkv", qkv)
+    call.take("weight", weight)
+    call.take("normed", normed)
+    call.hold("qkv", (2 * features, count), BF)
+    call.hold("mixed_t", (2 * vf, count), BF)
     for j, a in enumerate(carried):
         call.gather_blocks(f"c{j}", a, j % 2 == 1)
-    call.give("mixed", (2 * vf, qkv.shape[1]), BF)
+    call.give("mixed", (count, 2 * vf), BF)
     call.give("all", (features, n * tok), BF)
     call.give("att", (vf, n * tok), F32)
     call.give("den", (8, n * tok), F32)
@@ -548,7 +571,12 @@
                 ring.step()
 
         turn()
+        half = count // 2
+        for p in range(2):
+            part = dot(at["normed"][p * half : (p + 1) * half], at["weight"][...], 1, 0)
+            at["qkv"][:, p * half : (p + 1) * half] = part.T.astype(BF)
         arriving = incoming(at)
+        arriving.start()
         arriving.wait()
         turn()
         me = lax.axis_index("seq")
@@ -570,27 +598,32 @@
                 at["den"][h : h + 1, here] = den
                 at["own"][lines, here] = att.astype(BF)
         leaving = Exchange(
-            n, at, "out", at_positions(at["own"], tok), lambda me: to_pair(at["mixed"], vf, tok)(me)
+            n, at, "out", at_positions(at["own"], tok), lambda me: to_pair(at["mixed_t"], vf, tok)(me)
         )
         leaving.start()
         for _ in range(n // 2):
             turn()
         arriving.wait_sent()
         leaving.wait()
+        at["mixed"][...] = at["mixed_t"][...].astype(F32).T.astype(BF)
         leaving.wait_sent()
 
-    out = call.run(body, lambda at: incoming(at).start())
+    out = call.run(body)
     return out, [out[f"c{j}"] for j in range(len(carried))]
 
 
-def attend_pairs_back(off, da, kept, scatters, call_id):
+def attend_pairs_back(off, grad, out_t, weight, kept, scatters, call_id):
     n = lax.axis_size("seq")
     whole = kept["all"]
     features, tok = whole.shape[0], whole.shape[1] // n
     vf = features - 4 * QK
     call = Call(call_id)
     call.take("off", off, pltpu.SMEM)
-    call.take("da", da)
+    call.take("grad", grad)
+    call.take("out_t", out_t)
+    call.take("weight", weight)
+    count, width = grad.shape
+    call.hold("da", (2 * vf, count), BF)
     for name in ("all", "att", "den"):
         call.take(name, kept[name])
     lefts, pairs = scatters
@@ -598,7 +631,9 @@
         call.left(f"left{i}", a)
     for j, (i, right) in enumerate(pairs):
         call.scatter(f"s{j}", f"left{i}", right, j % 2 == 1)
-    call.give("d", (2 * features, da.shape[1]), BF)
+    call.give("d", (count, 2 * features), BF)
+    call.give("part", (count, width), BF)
+    call.hold("d_t", (2 * features, count), BF)
     call.hold("da_all", (vf, n * tok), BF)
     call.hold("sum", (2 * QK + vf, n * tok), F32)
     call.hold("own", (features, n * tok), BF)
@@ -609,8 +644,15 @@
         return Exchange(n, at, "in", to_pair(at["da"], vf, tok), at_positions(at["da_all"], tok))
 
     def body(at, rings):
+        half = count // 2
+        for p in range(2):
+            part = dot(at["grad"][p * half : (p + 1) * half], at["out_t"][:, : 2 * vf], 1, 0)
+            at["da"][:, p * half : (p + 1) * half] = part.T.astype(BF)
         arriving = incoming(at)
+        arriving.start()
         arriving.wait()
+        for ring in rings.values():
+            ring.step()
         me = lax.axis_index("seq")
         offset = at["off"][me // 2]
         whole = at["all"]
@@ -640,23 +682,26 @@
                 else:
                     total[k_lines, upto] += dk
                     total[v_lines, upto] += dv
-            if h == 0:
-                for ring in rings.values():
-                    ring.step()
         at["own"][2 * QK :, :] = total[...].astype(BF)
         leaving = Exchange(
-            n, at, "out", at_positions(at["own"], tok), lambda me: to_pair(at["d"], features, tok)(me)
+            n, at, "out", at_positions(at["own"], tok), lambda me: to_pair(at["d_t"], features, tok)(me)
         )
         leaving.start()
+        for ring in rings.values():
+            ring.step()
+        leaving.wait()
+        at["d"][...] = at["d_t"][...].astype(F32).T.astype(BF)
+        for j in range(width // 256):
+            lines = slice(j * 256, (j + 1) * 256)
+            at["part"][:, lines] = dot(at["d"][...], at["weight"][lines, :], 1, 1).astype(BF)
         for _ in range(n // 2):
             for ring in rings.values():
                 ring.step()
         arriving.wait_sent()
-        leaving.wait()
         leaving.wait_sent()
 
-    out = call.run(body, lambda at: incoming(at).start())
-    return out["d"], [out[f"s{j}"] for j in range(len(pairs))]
+    out = call.run(body)
+    return out["d"], out["part"], [out[f"s{j}"] for j in range(len(pairs))]
 
 
 def by_rows(kernel, scal, place, operands, widths, kinds):
@@ -692,6 +737,35 @@
     dg = dn * gain
     dx = scale * (dg - unit * jnp.mean(dg * unit, axis=-1, keepdims=True))
     return dx, gain_grad
+
+
+def closing_kernel(count, *refs):
+    x_ref, dn_ref, grad_ref, gain_ref = refs[:4]
+    srcs, out_ref, dsts = refs[4 : 4 + count], refs[4 + count], refs[5 + count :]
+    dx, _ = rms_back(x_ref[...].astype(F32), gain_ref[...], dn_ref[...].astype(F32))
+    out_ref[...] = grad_ref[...] + dx
+    for src, dst in zip(srcs, dsts):
+        dst[...] = src[...]
+
+
+def closing(x, dn, grad, gain, results):
+    steps = 4
+
+    def rows(a):
+        return pl.BlockSpec((a.shape[0] // steps, a.shape[1]), lambda i: (i, 0))
+
+    whole = pl.BlockSpec(gain.shape, lambda i: (0, 0))
+    shapes = [jax.ShapeDtypeStruct(x.shape, F32)]
+    shapes += [jax.ShapeDtypeStruct(r.shape, r.dtype) for r in results]
+    out = pl.pallas_call(
+        partial(closing_kernel, len(results)),
+        grid=(steps,),
+        in_specs=[rows(x), rows(dn), rows(grad), whole] + [rows(r) for r in results],
+        out_specs=[rows(a) for a in shapes],
+        out_shape=shapes,
+        compiler_params=pltpu.CompilerParams(vmem_limit_bytes=58 * MIB),
+    )(x, dn, grad, gain, *results)
+    return out[0], out[1:]
 
 
 def head_total(partial_sum):
@@ -784,22 +858,21 @@
         qkv_s = jnp.concatenate([attn_query, attn_key, attn_value], axis=1)
     gains = norm_gains.astype(F32)
     kernel_f = conv_kernel.astype(F32)
-    inputs = activations.reshape(count, width).astype(F32)
+    acts_flat = activations.reshape(count, width)
+    inputs = acts_flat.astype(F32)
     grad_four = cotangent.reshape(count, width)
     outs_s = jnp.concatenate([attn_output.T, conv_output.T], axis=1)
-    (qkv_w,) = gather_all([qkv_s], 1)
+    normed_a, qkv_w = gather_beside_norm(acts_flat, gains[:1], qkv_s, 1)
 
     scal = jnp.concatenate([start[None].astype(jnp.int32), off])
     place = jnp.arange(n * tok, dtype=jnp.int32).reshape(1, n * tok)
-    normed_a = rms_norm(inputs, gains[0]).astype(BF)
 
     def by_sequence(blocks):
         return jnp.swapaxes(blocks.reshape(n, rows, tok, -1), 0, 1).reshape(rows, n * tok, -1)
 
     if paired:
-        qkv = dot(qkv_w, normed_a, 0, 1).astype(BF)
-        attention, (outs_t, gate_1) = attend_pairs(off, qkv, (outs_s, ffn1_gate), 2)
-        mixed, mixed_axis = attention["mixed"], 1
+        attention, (outs_t, gate_1) = attend_pairs(off, qkv_w, normed_a, (outs_s, ffn1_gate), 2)
+        mixed = attention["mixed"]
     else:
         qkv = dot(normed_a, qkv_w, 1, 0).astype(BF)
         qkv_all = by_sequence(gather_all([qkv], 2)[0])
@@ -807,10 +880,10 @@
         q_own, k_own, v_own = own[..., :qw], own[..., qw : 2 * qw], own[..., 2 * qw :]
         q_all, k_all, v_all = qkv_all[..., :qw], qkv_all[..., qw : 2 * qw], qkv_all[..., 2 * qw :]
         (mixed,) = by_rows(attend_kernel, scal, place, (q_own, k_all, v_all), (vw,), (BF,))
-        mixed, mixed_axis = mixed.reshape(count, vw), 0
+        mixed = mixed.reshape(count, vw)
         outs_t, gate_1 = gather_all((outs_s, ffn1_gate), 11)
     out_t, conv_out_t = outs_t[:, :vw], outs_t[:, vw:]
-    attn_part = dot(mixed, out_t, 1 - mixed_axis, 1).astype(BF)
+    attn_part = dot(mixed, out_t, 1, 1).astype(BF)
     attn_sum = head_total(attn_part)
     ffn1 = [gate_1] + gather_all(tie((ffn1_up, ffn1_down.T), attn_part), 12)
     resid_one = inputs + attn_sum
@@ -883,8 +956,7 @@
     grad_b = grad_one.astype(BF)
     later = ((normed_1, grad_b1), ((0, d_up_1), (1, hidden_1)))
     if paired:
-        da = dot(out_t, grad_b, 0, 1).astype(BF)
-        d_qkv, more = attend_pairs_back(off, da, attention, later, 7)
+        d_qkv, dn_part, more = attend_pairs_back(off, grad_b, outs_t, qkv_w, attention, later, 7)
         sums_one = sums_one + more
     else:
         da = dot(grad_b, out_t, 1, 0).reshape(rows, tok, vw)
@@ -903,8 +975,8 @@
         )
         sums_one = scatter_all((normed_1,), ((0, d_gate_1),), 9) + scatter_all(*later, 10)
         d_qkv = jnp.concatenate([dq, dk, dv], axis=-1).reshape(count, 2 * qw + vw)
-    dn_part = dot(d_qkv, qkv_w, 1 - mixed_axis, 1).astype(BF)
-    dn = head_total(dn_part)
+        dn_part = dot(d_qkv, qkv_w, 1, 1).astype(BF)
+    dn = lax.psum(dn_part, "head")
     unit = inputs * rms_scale(inputs)
     gain_one = small_sum(jnp.sum(dn_part.astype(F32) * unit, axis=0), "head")
     small = jnp.concatenate(
@@ -914,8 +986,6 @@
             jnp.zeros((8 - 4 - taps, width), F32),
         ]
     )
-    if paired:
-        d_qkv, mixed = d_qkv.T, mixed.T
     sums_attn = scatter_all(
         tie((normed_a, grad_b), dn_part), ((0, d_qkv), (1, mixed)), 8, 0, small
     )
@@ -931,10 +1001,12 @@
     else:
         query_sum, key_sum = qkv_sum[:, :qw], qkv_sum[:, qw : 2 * qw]
         value_sum = qkv_sum[:, 2 * qw :]
-    (dn,) = tie((dn,), *sums_attn)
-    dx, _ = rms_back(inputs, gains[0], dn)
-    input_grad = (grad_one + dx).reshape(activations.shape)
-
+    straight = (sums_one[0], sums_one[1], sums_conv[0], sums_conv[1], sums_two[0], sums_two[1])
+    if ring_size(n):
+        input_grad, straight = closing(acts_flat, dn, grad_one, gains[:1], straight)
+    else:
+        input_grad = grad_one + rms_back(inputs, gains[0], dn.astype(F32))[0]
+    input_grad = input_grad.reshape(activations.shape)
     return (
         block_output,
         input_grad,
@@ -942,15 +1014,15 @@
         key_sum,
         value_sum,
         sums_attn[1].T,
-        sums_one[0],
-        sums_one[1],
+        straight[0],
+        straight[1],
         sums_one[2].T,
-        sums_conv[0],
-        sums_conv[1],
+        straight[2],
+        straight[3],
         sums_conv[2].T,
         kernel_grad,
-        sums_two[0],
-        sums_two[1],
+        straight[4],
+        straight[5],
         sums_two[2].T,
         gains_grad,
     )

time: 937 us -> 924 us (0.986)
  local copies, waits for them, and re-layouts: 50.6 us -> 40.8 us
    unnamed x180 -> x132, local copies, waits for them, and re-layouts: 38 us -> 28.3 us
    dot_general x22 -> x19, matrix products: 60 us -> 51.1 us  [dot(): lax.dot_general(a, b, (((ca,), (cb,)), ((), ())), preferred_element_type=...]
  transfers between devices with their start and end apart: 12 -> 12, of which waited for: 3 -> 4; matrix products, arithmetic and copies ran while one was open for 2% -> 1% of each run, Pallas kernels for 56% -> 55%
where the time goes in v6:
time: 924 us; the launch traced here: 917 us
  Pallas kernels  753 us (81%)
  matrix products  51.1 us (6%)
  local copies, waits for them, and re-layouts  40.8 us (4%)
  other arithmetic  39.7 us (4%)
  between operations  15.4 us (2%)
    pallas_call x10, Pallas kernels, run(): pl.pallas_call(partial(self.kernel, body), in_specs=[spec for _, spec in...  745 us
    dot_general x19, matrix products, dot(): lax.dot_general(a, b, (((ca,), (cb,)), ((), ())), preferred_element_type=...  51.1 us
    unnamed x132, local copies, waits for them, and re-layouts  28.3 us
  transfers between devices with their start and end apart: 12, of which 4 were waited for; matrix products, arithmetic and copies ran while one was open for 1% of the time, Pallas kernels for 55%

profile of v6, /device:TPU:0, one launch (start us, length us, event | category | flops | bytes accessed | tf_op | source)
XLA Modules:
  0.0 917.0 jit_solution(12476669257798786002)
XLA Ops:
  7.2 1.1 fusion.21
  10.3 1.3 slice.169.refs_1_.refs_3_
  11.6 1.3 reshape.174.refs_0_
  12.9 1.1 copy.39
  13.9 1.1 copy.40
  16.8 31.8 %shard_map.305 = (bf16[512,1792]{1,0:T(8,128)(2,1)}, bf16[1792,576]{1,0:T(8,128)(2,1)}) custom-call(bf16[512,1792]{1,0:T(8,128)(2,1)} %bitcast.115, f32[1,1792]{1,0:T(1,128)} %slice.169.refs_1_.refs_3_, bf16[224,576]{1,0:T(8,128)(2,1)} %concatenate.41.refs_2_), custom_call_target="tpu_custom_call" | custom-call | tf_op jit(solution)/shard_map/pallas_call | solution.py:229
  48.7 93.6 %shard_map.306 = (bf16[1792,896]{1,0:T(8,128)(2,1)}, bf16[1792,1152]{1,0:T(8,128)(2,1)}, bf16[512,448]{1,0:T(8,128)(2,1)}, bf16[288,1024]{1,0:T(8,128)(2,1)}, f32[224,1024]{1,0:T(8,128)}, /*index=5*/f32[8,1024]{1,0:T(8,128)}) custom-call(s32[4]{0:T(128)} %reshape.174.refs_0_, bf16[1792,576]{1,0:T(8,128)(2,1)} %get-tuple-element.69.refs_1_.refs_3_, ...), custom_call_target="tpu_custom_call" | custom-call | tf_op jit(solution)/shard_map/pallas_call | solution.py:229
  142.3 4.2 convolution_convert_fusion.3
  146.8 82.6 %shard_map.307 = (bf16[1792,1152]{1,0:T(8,128)(2,1)}, bf16[1792,1152]{1,0:T(8,128)(2,1)}) custom-call(bf16[224,1152]{1,0:T(8,128)(2,1)} %refs_0_, bf16[224,1152]{1,0:T(8,128)(2,1)} %bitcast.130), custom_call_target="tpu_custom_call" | custom-call | tf_op jit(solution)/shard_map/pallas_call | solution.py:229
  229.6 2.3 multiply_reduce_fusion.9
  232.9 1.7 copy-done.48
  234.6 2.5 fusion.25
  237.2 4.1 multiply_convert_fusion.8
  242.3 3.8 convolution_convert_fusion.2
  246.5 73.4 %shard_map.308 = (bf16[1792,448]{1,0:T(8,128)(2,1)}, bf16[1792,448]{1,0:T(8,128)(2,1)}, bf16[1792,1152]{1,0:T(8,128)(2,1)}) custom-call(bf16[224,448]{1,0:T(8,128)(2,1)} %refs_0_.1, bf16[224,448]{1,0:T(8,128)(2,1)} %refs_1_, bf16[224,1152]{1,0:T(8,128)(2,1)} %refs_2_), custom_call_target="tpu_custom_call" | custom-call | tf_op jit(solution)/shard_map/pallas_call | solution.py:229
  320.0 3.0 multiply_reduce_fusion.8
  323.4 2.4 copy-done.34
  325.8 1.1 fusion.26
  326.9 2.8 collective-permute-start
  329.8 1.4 collective-permute-done
  331.5 2.6 multiply_convert_fusion.10
  334.9 2.5 convolution_convert_fusion.1
  338.0 77.8 %shard_map.309 = (bf16[1792,1152]{1,0:T(8,128)(2,1)}, bf16[1792,1152]{1,0:T(8,128)(2,1)}) custom-call(bf16[224,1152]{1,0:T(8,128)(2,1)} %refs_0_.2, bf16[224,1152]{1,0:T(8,128)(2,1)} %bitcast.131), custom_call_target="tpu_custom_call" | custom-call | tf_op jit(solution)/shard_map/pallas_call | solution.py:229
  415.8 3.3 multiply_reduce_fusion.7
  420.7 2.3 copy-done.55
  422.9 2.5 fusion.27
  425.5 2.5 fusion.28
  428.2 3.2 multiply_convert_fusion.6
  431.5 2.6 fusion.29
  434.1 2.6 convolution_convert_fusion
  436.7 2.6 add_convert_fusion.3
  439.3 2.2 pad_maximum_fusion
  441.6 120.3 %shard_map.310 = (f32[224,1152]{1,0:T(8,128)}, f32[224,1152]{1,0:T(8,128)}, f32[224,1152]{1,0:T(8,128)}) custom-call(bf16[512,1792]{1,0:T(8,128)(2,1)} %copy-done.24, bf16[512,1792]{1,0:T(8,128)(2,1)} %bitcast.123, bf16[512,1152]{1,0:T(8,128)(2,1)} %copy-done.39, bf16[512,1152]{1,0:T(8,128)(2,1)} %copy-done.38, bf16[512,1152]{1,0:T(8,128)(2,1)} %copy-done.40), custom_call_target="tpu_custom_call" | custom-call | tf_op jit(solution)/shard_map/pallas_call | solution.py:229
  561.9 1.9 slice_convert_fusion
  564.5 1.2 copy-done.10
  565.7 1.1 multiply_reduce_fusion
  567.2 1.3 fusion.16.refs_1_
  569.1 1.2 fusion.6
  572.5 1.3 collective-permute-start.1
  574.1 4.0 collective-permute-done.1
  579.6 1.2 fusion.30
  581.3 2.4 add_convert_fusion.1
  584.2 52.5 %shard_map.311 = (f32[224,448]{1,0:T(8,128)}, f32[224,448]{1,0:T(8,128)}, f32[224,448]{1,0:T(8,128)}) custom-call(bf16[512,1792]{1,0:T(8,128)(2,1)} %copy-done.15, bf16[512,1792]{1,0:T(8,128)(2,1)} %copy-done.23, bf16[512,448]{1,0:T(8,128)(2,1)} %copy-done.27, bf16[512,448]{1,0:T(8,128)(2,1)} %copy-done.28, bf16[512,448]{1,0:T(8,128)(2,1)} %copy-done.33), custom_call_target="tpu_custom_call" | custom-call | tf_op jit(solution)/shard_map/pallas_call | solution.py:229
  636.7 1.9 convert_element_type.158
  640.3 1.1 copy-done.6
  642.5 6.2 fusion.18
  648.7 3.1 multiply_convert_fusion.3
  651.8 2.6 fusion.31
  654.8 3.8 add_convert_fusion
  659.1 43.1 %shard_map.312.refs_4_ = f32[224,1152]{1,0:T(8,128)} custom-call(bf16[512,1792]{1,0:T(8,128)(2,1)} %copy-done.16, bf16[512,1152]{1,0:T(8,128)(2,1)} %copy-done.41), custom_call_target="tpu_custom_call" | custom-call | tf_op jit(solution)/shard_map/pallas_call | solution.py:229
  702.2 2.9 all-reduce.19.cloned.1.call-done
  705.0 1.9 convert_element_type.163
  707.1 1.4 multiply_reduce_fusion.2
  709.1 4.1 fusion.17
  713.2 112.3 %shard_map.313 = (f32[224,1152]{1,0:T(8,128)}, f32[224,1152]{1,0:T(8,128)}, bf16[512,576]{1,0:T(8,128)(2,1)}, bf16[512,1792]{1,0:T(8,128)(2,1)}) custom-call(s32[4]{0:T(128)} %reshape.174.refs_0_, bf16[512,1792]{1,0:T(8,128)(2,1)} %get-tuple-element.109.refs_1_.refs_2_, bf16[1792,896]{1,0:T(8,128)(2,1)} %get-tuple-element.72.refs_2_, ...), custom_call_target="tpu_custom_call" | custom-call | tf_op jit(solution)/shard_map/pallas_call | solution.py:229
  825.5 2.2 fusion.1
  828.8 1.4 collective-permute-start.4
  832.3 57.2 %shard_map.315 = (f32[224,576]{1,0:T(8,128)}, f32[224,448]{1,0:T(8,128)}, f32[8,1792]{1,0:T(8,128)}) custom-call(f32[8,1792]{1,0:T(8,128)} %concatenate.52.refs_0_, bf16[512,1792]{1,0:T(8,128)(2,1)} %get-tuple-element.108.refs_2_.refs_1_, bf16[512,1792]{1,0:T(8,128)(2,1)} %get-tuple-element.109.refs_1_.refs_2_, bf16[512,576]{1,0:T(8,128)(2,1)} %get-tuple-element.110.refs_3_, ...), custom_call_target="tpu_custom_call" | custom-call | tf_op jit(solution)/shard_map/pallas_call | solution.py:229
  889.5 1.4 slice.168
  890.9 1.3 slice.167
  892.3 1.2 fusion.20
  895.1 2.0 copy.52
  897.1 1.3 fusion.19
  899.3 8.7 shard_map.314
  (196 shorter events, 29.0 us)
Async XLA Ops:
  7.2 222.4 %all-reduce.9.cloned.1.call-start = ((), (), s32[]{:S(2)}) async-start(), calls=%async_computation | async-start | bytes 3670016 | tf_op jit(solution)/shard_map/psum | solution.py:772
  142.3 4.5 copy-start.45
  142.3 87.3 %copy-start.4 = (bf16[2,2,128,1792]{3,2,1,0:T(8,128)(2,1)S(1)}, bf16[2,2,128,1792]{3,2,1,0:T(8,128)(2,1)}, u32[]{:S(2)}) copy-start(bf16[2,2,128,1792]{3,2,1,0:T(8,128)(2,1)} %param.18) | copy-start | bytes 5505028
  146.5 173.5 %all-reduce.11.cloned.1.call-start = ((), (), s32[]{:S(2)}) async-start(), calls=%async_computation.1 | async-start | bytes 3670016 | tf_op jit(solution)/shard_map/psum | solution.py:772
  229.6 2.3 copy-start.7
  231.9 2.7 copy-start.48
  232.9 4.3 copy-start.16
  234.6 2.6 copy-start.50
  237.2 4.1 copy-start.57
  237.2 5.1 copy-start.52
  242.3 3.9 copy-start.47
  246.1 169.7 %all-reduce.13.cloned.1.call-start = ((), (), s32[]{:S(2)}) async-start(), calls=%async_computation.2 | async-start | bytes 3670016 | tf_op jit(solution)/shard_map/psum | solution.py:772
  322.9 4.0 copy-start
  322.9 2.9 copy-start.34
  323.3 8.2 copy-start.15
  323.4 6.4 copy-start.46
  326.9 4.6 copy-start.25
  326.9 4.2 collective-permute-start
  331.5 2.6 copy-start.18
  331.5 2.6 copy-start.20
  331.5 3.4 copy-start.31
  337.4 224.5 %all-reduce.15.cloned.1.call-start = ((), (), s32[]{:S(2)}) async-start(), calls=%async_computation.3 | async-start | bytes 7340032 | tf_op jit(solution)/shard_map/psum | solution.py:918
  415.8 3.7 copy-start.1
  415.8 4.2 copy-start.9
  420.1 2.8 copy-start.55
  420.7 4.8 copy-start.24
  422.9 2.6 copy-start.54
  425.5 2.6 copy-start.12
  425.5 2.7 copy-start.56
  431.5 2.6 copy-start.39
  431.5 2.6 copy-start.40
  431.5 5.2 copy-start.38
  441.5 195.1 %all-reduce.17.cloned.1.call-start = ((), (), s32[]{:S(2)}) async-start(), calls=%async_computation.4 | async-start | bytes 3670016 | tf_op jit(solution)/shard_map/psum | solution.py:772
  561.9 2.6 copy-start.2
  561.9 3.8 copy-start.10
  563.8 2.9 copy-start.5
  569.1 3.3 copy-start.23
  569.1 2.2 copy-start.21
  569.1 2.5 copy-start.29
  569.1 2.8 copy-start.30
  572.4 8.3 copy-start.28
  572.5 5.6 collective-permute-start.1
  583.7 121.3 %all-reduce.19.cloned.1.call-start = ((), (), s32[]{:S(2)}) async-start(), calls=%async_computation.5 | async-start | bytes 3670016 | tf_op jit(solution)/shard_map/psum | solution.py:772
  636.7 2.6 copy-start.3
  639.3 2.0 copy-start.6
  639.3 2.6 copy-start.11
  639.3 3.2 copy-start.14
  642.4 6.2 copy-start.53
  642.5 6.2 copy-start.58
  642.5 6.2 copy-start.59
  648.6 3.1 copy-start.22
  648.7 3.1 copy-start.49
  651.8 2.6 copy-start.41
  651.8 2.6 copy-start.37
  651.8 3.0 copy-start.51
  705.0 2.1 copy-start.8
  707.1 2.0 copy-start.17
  825.5 4.7 copy-start.44
  827.8 71.5 %all-reduce.21.cloned.1.call-start = ((), (), s32[]{:S(2)}) async-start(), calls=%async_computation.6 | async-start | bytes 3670016 | tf_op jit(solution)/shard_map/psum | solution.py:979
  827.8 3.5 collective-permute-start.2
  827.9 3.7 collective-permute-start.3
  828.8 2.7 collective-permute-start.4
  899.3 8.8 copy-start.43
  899.3 9.7 %copy-start.42 = (f32[224,1152]{1,0:T(8,128)S(1)}, f32[224,1152]{1,0:T(8,128)}, u32[]{:S(2)}) copy-start(f32[224,1152]{1,0:T(8,128)} %get-tuple-element.92) | copy-start | bytes 3096580
  (8 other events, 11.5 us)
Sparse Core Ops, SparseCore 0:
  146.6 50.5 all-reduce.8
  246.3 46.2 all-reduce.10
  337.6 47.9 all-reduce.12
  441.7 76.0 all-reduce.14
  583.8 46.1 all-reduce.16
  658.7 46.2 all-reduce.18
  831.4 50.1 all-reduce.20

commit v7 on v6

--- a/solution.py
+++ b/solution.py
@@ -260,28 +260,47 @@
     return [out[name] for name in names]
 
 
-def gather_beside_norm(x, gain, array, call_id):
+def first_gather(x, gain, parts, paired_outs, call_id):
     n = lax.axis_size("seq")
-    if not ring_size(n):
-        normed = rms_norm(x.astype(F32), gain[0]).astype(BF)
-        return normed, lax.all_gather(array, "seq", axis=0, tiled=True)
     call = Call(call_id)
     call.take("x", x)
     call.take("gain", gain)
+    height = parts[2].shape[0]
+    for name, a in zip("qkv", parts):
+        call.take(name, a)
+    for i, a in enumerate(paired_outs):
+        call.take(f"o{i}", a)
     call.give("normed", x.shape, BF)
-    call.gather_blocks("w", array)
+    call.give("outs", (height, sum(a.shape[0] for a in paired_outs)), BF)
+    width = parts[0].shape[0] + parts[1].shape[0] + parts[2].shape[1]
+    call.hold("src", (height, width), BF)
+    call.give("w", (n * height, width), BF, pl.ANY)
+    half = height // 2
+    for p in range(2):
+        call.gather(f"w.{p}", "src", "w", by_block(height, p * half, half), p == 1, (p * half, half))
     rows = x.shape[0] // n
 
     def body(at, rings):
+        first = at["gain"][:1].astype(F32)
+        kinds = [at["q"][...].astype(F32).T, at["k"][...].astype(F32).T, at["v"][...].astype(F32)]
+        pieces = []
+        for g in range(2):
+            for a in kinds:
+                size = a.shape[1] // 2
+                pieces.append(a[:, g * size : (g + 1) * size])
+        at["src"][...] = jnp.concatenate(pieces, axis=1).astype(BF)
         for k in range(n):
             if k % 2 == 0:
                 for ring in rings.values():
                     ring.step()
             lines = slice(k * rows, (k + 1) * rows)
-            at["normed"][lines] = rms_norm(at["x"][lines].astype(F32), at["gain"][...]).astype(BF)
+            at["normed"][lines] = rms_norm(at["x"][lines].astype(F32), first).astype(BF)
+            if k == 1:
+                both = [at[f"o{i}"][...].astype(F32) for i in range(len(paired_outs))]
+                at["outs"][...] = jnp.concatenate(both, axis=0).T.astype(BF)
 
     out = call.run(body)
-    return out["normed"], out["w"]
+    return out["normed"], out["w"], out["outs"]
 
 
 class ScatterRing:
@@ -740,32 +759,60 @@
 
 
 def closing_kernel(count, *refs):
-    x_ref, dn_ref, grad_ref, gain_ref = refs[:4]
-    srcs, out_ref, dsts = refs[4 : 4 + count], refs[4 + count], refs[5 + count :]
-    dx, _ = rms_back(x_ref[...].astype(F32), gain_ref[...], dn_ref[...].astype(F32))
+    x_ref, dn_ref, grad_ref, gain_ref, qkv_ref, small_ref = refs[:6]
+    srcs, turned, refs = refs[6 : 6 + count], refs[6 + count : 8 + count], refs[8 + count :]
+    out_ref, (q_ref, k_ref, v_ref), gains_ref, taps_ref = refs[0], refs[1:4], refs[4], refs[5]
+    across, dsts = refs[6:8], refs[8:]
+    gain = gain_ref[:1].astype(F32)
+    dx, _ = rms_back(x_ref[...].astype(F32), gain, dn_ref[...].astype(F32))
     out_ref[...] = grad_ref[...] + dx
     for src, dst in zip(srcs, dsts):
         dst[...] = src[...]
 
-
-def closing(x, dn, grad, gain, results):
+    @pl.when(pl.program_id(0) == 0)
+    def _():
+        q, v = q_ref.shape[0] // 2, v_ref.shape[1] // 2
+        halves = [qkv_ref[:, g * (2 * q + v) : (g + 1) * (2 * q + v)] for g in range(2)]
+        q_ref[...] = jnp.concatenate([a[:, :q] for a in halves], axis=1).T
+        k_ref[...] = jnp.concatenate([a[:, q : 2 * q] for a in halves], axis=1).T
+        v_ref[...] = jnp.concatenate([a[:, 2 * q :] for a in halves], axis=1)
+        norms = gains_ref.shape[0]
+        gains_ref[...] = small_ref[:norms]
+        taps_ref[...] = small_ref[norms : norms + taps_ref.shape[0], : taps_ref.shape[1]]
+
+    for i in range(2):
+
+        @pl.when(pl.program_id(0) == i + 1)
+        def _():
+            across[i][...] = turned[i][...].T
+
+
+def closing(x, dn, grad, gains, qkv, widths, small, taps, results, turned):
     steps = 4
 
     def rows(a):
         return pl.BlockSpec((a.shape[0] // steps, a.shape[1]), lambda i: (i, 0))
 
-    whole = pl.BlockSpec(gain.shape, lambda i: (0, 0))
-    shapes = [jax.ShapeDtypeStruct(x.shape, F32)]
-    shapes += [jax.ShapeDtypeStruct(r.shape, r.dtype) for r in results]
+    def whole(a):
+        return pl.BlockSpec(a.shape, lambda i: (0, 0))
+
+    height = qkv.shape[0]
+    fixed = [(widths[0], height), (widths[1], height), (height, widths[2]), gains.shape, taps.shape]
+    fixed += [r.shape[::-1] for r in turned]
+    fixed = [jax.ShapeDtypeStruct(k, F32) for k in fixed]
+    same = [jax.ShapeDtypeStruct(r.shape, F32) for r in results]
+    shape = jax.ShapeDtypeStruct(x.shape, F32)
     out = pl.pallas_call(
         partial(closing_kernel, len(results)),
         grid=(steps,),
-        in_specs=[rows(x), rows(dn), rows(grad), whole] + [rows(r) for r in results],
-        out_specs=[rows(a) for a in shapes],
-        out_shape=shapes,
+        in_specs=[rows(x), rows(dn), rows(grad), whole(gains), whole(qkv), whole(small)]
+        + [rows(r) for r in results]
+        + [whole(r) for r in turned],
+        out_specs=[rows(shape)] + [whole(k) for k in fixed] + [rows(a) for a in same],
+        out_shape=[shape] + fixed + same,
         compiler_params=pltpu.CompilerParams(vmem_limit_bytes=58 * MIB),
-    )(x, dn, grad, gain, *results)
-    return out[0], out[1:]
+    )(x, dn, grad, gains, qkv, small, *results, *turned)
+    return out[0], (out[1].T, out[2].T, out[3]), out[4], out[5], out[6:8], out[8:]
 
 
 def head_total(partial_sum):
@@ -847,22 +894,24 @@
     off = offsets.reshape(rows)
 
     paired = ring_size(n) and 2 * rows == n and qw == 4 * QK
-    if paired:
-        halves = [
-            a[:, g * a.shape[1] // 2 : (g + 1) * a.shape[1] // 2]
-            for g in range(2)
-            for a in (attn_query, attn_key, attn_value)
-        ]
-        qkv_s = jnp.concatenate(halves, axis=1)
-    else:
-        qkv_s = jnp.concatenate([attn_query, attn_key, attn_value], axis=1)
     gains = norm_gains.astype(F32)
     kernel_f = conv_kernel.astype(F32)
     acts_flat = activations.reshape(count, width)
     inputs = acts_flat.astype(F32)
     grad_four = cotangent.reshape(count, width)
-    outs_s = jnp.concatenate([attn_output.T, conv_output.T], axis=1)
-    normed_a, qkv_w = gather_beside_norm(acts_flat, gains[:1], qkv_s, 1)
+    if paired:
+        normed_a, qkv_w, outs_s = first_gather(
+            acts_flat,
+            norm_gains,
+            (attn_query.T, attn_key.T, attn_value),
+            (attn_output, conv_output),
+            1,
+        )
+    else:
+        normed_a = rms_norm(inputs, gains[0]).astype(BF)
+        qkv_s = jnp.concatenate([attn_query, attn_key, attn_value], axis=1)
+        (qkv_w,) = gather_all([qkv_s], 1)
+        outs_s = jnp.concatenate([attn_output.T, conv_output.T], axis=1)
 
     scal = jnp.concatenate([start[None].astype(jnp.int32), off])
     place = jnp.arange(n * tok, dtype=jnp.int32).reshape(1, n * tok)
@@ -991,39 +1040,42 @@
     )
     gains_grad, kernel_grad = sums_attn[2][:4], sums_attn[2][4 : 4 + taps, :cw]
     qkv_sum = sums_attn[0]
+    straight = (sums_one[0], sums_one[1], sums_conv[0], sums_conv[1], sums_two[0], sums_two[1])
+    straight += (sums_one[2], sums_two[2])
+    turned = (sums_conv[2], sums_attn[1])
     if paired:
-        edges = (0, qw // 2, qw, qw + vw // 2)
-        step = qw + vw // 2
-        query_sum, key_sum, value_sum = (
-            jnp.concatenate([qkv_sum[:, g * step + a : g * step + b] for g in range(2)], axis=1)
-            for a, b in zip(edges[:-1], edges[1:])
+        input_grad, by_kind, gains_grad, kernel_grad, turned, straight = closing(
+            acts_flat,
+            dn,
+            grad_one,
+            norm_gains,
+            qkv_sum,
+            (qw, qw, vw),
+            sums_attn[2],
+            conv_kernel,
+            straight,
+            turned,
         )
     else:
-        query_sum, key_sum = qkv_sum[:, :qw], qkv_sum[:, qw : 2 * qw]
-        value_sum = qkv_sum[:, 2 * qw :]
-    straight = (sums_one[0], sums_one[1], sums_conv[0], sums_conv[1], sums_two[0], sums_two[1])
-    if ring_size(n):
-        input_grad, straight = closing(acts_flat, dn, grad_one, gains[:1], straight)
-    else:
         input_grad = grad_one + rms_back(inputs, gains[0], dn.astype(F32))[0]
+        by_kind = (qkv_sum[:, :qw], qkv_sum[:, qw : 2 * qw], qkv_sum[:, 2 * qw :])
+        turned = [r.T for r in turned]
     input_grad = input_grad.reshape(activations.shape)
     return (
         block_output,
         input_grad,
-        query_sum,
-        key_sum,
-        value_sum,
-        sums_attn[1].T,
+        *by_kind,
+        turned[1],
         straight[0],
         straight[1],
-        sums_one[2].T,
+        straight[6].T,
         straight[2],
         straight[3],
-        sums_conv[2].T,
+        turned[0],
         kernel_grad,
         straight[4],
         straight[5],
-        sums_two[2].T,
+        straight[7].T,
         gains_grad,
     )
 

time: 924 us -> 907 us (0.982)
  local copies, waits for them, and re-layouts: 40.8 us -> 21.8 us
    unnamed x132 -> x114, local copies, waits for them, and re-layouts: 28.3 us -> 19.5 us
  transfers between devices with their start and end apart: 12 -> 12, of which waited for: 4 -> 5; matrix products, arithmetic and copies ran while one was open for 1% -> 0% of each run, Pallas kernels for 55% -> 56%
where the time goes in v7:
time: 907 us; the launch traced here: 901 us
  Pallas kernels  757 us (83%)
  matrix products  51.1 us (6%)
  other arithmetic  37.6 us (4%)
  local copies, waits for them, and re-layouts  21.8 us (2%)
  between operations  15.3 us (2%)
  waiting for transfers between devices  10.5 us (1%)
    pallas_call x10, Pallas kernels, run(): pl.pallas_call(partial(self.kernel, body), in_specs=[spec for _, spec in...  745 us
    dot_general x19, matrix products, dot(): lax.dot_general(a, b, (((ca,), (cb,)), ((), ())), preferred_element_type=...  51.1 us
    unnamed x114, local copies, waits for them, and re-layouts  19.5 us
  transfers between devices with their start and end apart: 12, of which 5 were waited for; matrix products, arithmetic and copies ran while one was open for 0% of the time, Pallas kernels for 56%

profile of v7, /device:TPU:0, one launch (start us, length us, event | category | flops | bytes accessed | tf_op | source)
XLA Modules:
  0.0 900.9 jit_solution(10068941725123193972)
XLA Ops:
  7.2 1.3 reshape.174.refs_0_
  8.5 32.1 %shard_map.305 = (bf16[512,1792]{1,0:T(8,128)(2,1)}, bf16[224,896]{1,0:T(8,128)(2,1)}, bf16[1792,576]{1,0:T(8,128)(2,1)}) custom-call(bf16[512,1792]{1,0:T(8,128)(2,1)} %bitcast.115, bf16[4,1792]{1,0:T(4,128)(2,1)} %refs_3_.1, bf16[64,224]{1,0:T(8,128)(2,1)} %bitcast.128, bf16[64,224]{1,0:T(8,128)(2,1)} %bitcast.129, bf16[224,448]{1,0:T(8,128)(2,1)} %refs_4_.2, ...), custom_call_target="tpu_custom_call" | custom-call | tf_op jit(solution)/shard_map/pallas_call | solution.py:229
  40.6 93.7 %shard_map.306 = (bf16[1792,896]{1,0:T(8,128)(2,1)}, bf16[1792,1152]{1,0:T(8,128)(2,1)}, bf16[512,448]{1,0:T(8,128)(2,1)}, bf16[288,1024]{1,0:T(8,128)(2,1)}, f32[224,1024]{1,0:T(8,128)}, /*index=5*/f32[8,1024]{1,0:T(8,128)}) custom-call(s32[4]{0:T(128)} %reshape.174.refs_0_, bf16[1792,576]{1,0:T(8,128)(2,1)} %get-tuple-element.79.refs_1_.refs_3_, ...), custom_call_target="tpu_custom_call" | custom-call | tf_op jit(solution)/shard_map/pallas_call | solution.py:229
  134.3 4.2 convolution_convert_fusion.3
  138.8 82.7 %shard_map.307 = (bf16[1792,1152]{1,0:T(8,128)(2,1)}, bf16[1792,1152]{1,0:T(8,128)(2,1)}) custom-call(bf16[224,1152]{1,0:T(8,128)(2,1)} %refs_0_, bf16[224,1152]{1,0:T(8,128)(2,1)} %bitcast.126), custom_call_target="tpu_custom_call" | custom-call | tf_op jit(solution)/shard_map/pallas_call | solution.py:229
  221.5 2.3 multiply_reduce_fusion.9
  223.9 1.0 multiply_convert_fusion.2.refs_0_.refs_7_
  224.8 1.7 copy-done.45
  226.6 2.5 fusion.20
  229.2 4.1 multiply_convert_fusion.8
  233.3 1.0 copy-done.36
  234.3 3.8 convolution_convert_fusion.2
  238.5 73.5 %shard_map.308 = (bf16[1792,448]{1,0:T(8,128)(2,1)}, bf16[1792,448]{1,0:T(8,128)(2,1)}, bf16[1792,1152]{1,0:T(8,128)(2,1)}) custom-call(bf16[224,448]{1,0:T(8,128)(2,1)} %refs_0_.1, bf16[224,448]{1,0:T(8,128)(2,1)} %refs_1_.2, bf16[224,1152]{1,0:T(8,128)(2,1)} %refs_2_), custom_call_target="tpu_custom_call" | custom-call | tf_op jit(solution)/shard_map/pallas_call | solution.py:229
  312.0 3.0 multiply_reduce_fusion.8
  315.4 2.4 copy-done.34
  317.8 1.1 fusion.21
  319.0 2.8 collective-permute-start
  321.8 1.4 collective-permute-done
  323.5 2.6 multiply_convert_fusion.10
  326.1 0.8 copy-done.33
  326.9 2.5 convolution_convert_fusion.1
  329.9 77.9 %shard_map.309 = (bf16[1792,1152]{1,0:T(8,128)(2,1)}, bf16[1792,1152]{1,0:T(8,128)(2,1)}) custom-call(bf16[224,1152]{1,0:T(8,128)(2,1)} %refs_0_.2, bf16[224,1152]{1,0:T(8,128)(2,1)} %bitcast.127), custom_call_target="tpu_custom_call" | custom-call | tf_op jit(solution)/shard_map/pallas_call | solution.py:229
  407.8 3.3 multiply_reduce_fusion.7
  412.7 2.3 copy-done.52
  414.9 2.5 fusion.22
  417.5 2.5 fusion.23
  420.2 3.2 multiply_convert_fusion.6
  423.5 2.6 fusion.24
  426.1 2.6 convolution_convert_fusion
  428.7 2.6 add_convert_fusion.3
  431.3 2.2 pad_maximum_fusion
  433.6 120.3 %shard_map.310 = (f32[224,1152]{1,0:T(8,128)}, f32[224,1152]{1,0:T(8,128)}, f32[224,1152]{1,0:T(8,128)}) custom-call(bf16[512,1792]{1,0:T(8,128)(2,1)} %copy-done.24, bf16[512,1792]{1,0:T(8,128)(2,1)} %bitcast.123, bf16[512,1152]{1,0:T(8,128)(2,1)} %copy-done.39, bf16[512,1152]{1,0:T(8,128)(2,1)} %copy-done.38, bf16[512,1152]{1,0:T(8,128)(2,1)} %copy-done.40), custom_call_target="tpu_custom_call" | custom-call | tf_op jit(solution)/shard_map/pallas_call | solution.py:229
  553.9 1.9 slice_convert_fusion
  556.5 1.2 copy-done.10
  557.7 1.1 multiply_reduce_fusion
  559.2 1.3 fusion.16.refs_1_
  561.1 1.2 fusion.6
  564.4 1.3 collective-permute-start.1
  566.0 4.0 collective-permute-done.1
  570.7 0.9 copy-done.35
  571.6 1.2 fusion.25
  573.3 2.4 add_convert_fusion.1
  576.2 52.5 %shard_map.311 = (f32[224,448]{1,0:T(8,128)}, f32[224,448]{1,0:T(8,128)}, f32[224,448]{1,0:T(8,128)}) custom-call(bf16[512,1792]{1,0:T(8,128)(2,1)} %copy-done.15, bf16[512,1792]{1,0:T(8,128)(2,1)} %copy-done.23, bf16[512,448]{1,0:T(8,128)(2,1)} %copy-done.27, bf16[512,448]{1,0:T(8,128)(2,1)} %copy-done.28, bf16[512,448]{1,0:T(8,128)(2,1)} %copy-done.33), custom_call_target="tpu_custom_call" | custom-call | tf_op jit(solution)/shard_map/pallas_call | solution.py:229
  628.7 1.9 convert_element_type.158
  630.6 0.7 copy-done.3
  631.3 1.0 multiply_reduce_fusion.1
  632.2 1.1 copy-done.6
  634.4 6.2 fusion.18
  640.6 3.1 multiply_convert_fusion.3
  643.8 2.6 fusion.26
  646.8 3.8 add_convert_fusion
  651.0 43.2 %shard_map.312.refs_6_ = f32[224,1152]{1,0:T(8,128)} custom-call(bf16[512,1792]{1,0:T(8,128)(2,1)} %copy-done.16, bf16[512,1152]{1,0:T(8,128)(2,1)} %copy-done.41), custom_call_target="tpu_custom_call" | custom-call | tf_op jit(solution)/shard_map/pallas_call | solution.py:229
  694.2 2.9 all-reduce.19.cloned.1.call-done
  697.1 1.9 convert_element_type.163
  699.1 1.4 multiply_reduce_fusion.2
  701.2 4.1 fusion.17
  705.3 112.3 %shard_map.313 = (f32[224,1152]{1,0:T(8,128)}, f32[224,1152]{1,0:T(8,128)}, bf16[512,576]{1,0:T(8,128)(2,1)}, bf16[512,1792]{1,0:T(8,128)(2,1)}) custom-call(s32[4]{0:T(128)} %reshape.174.refs_0_, bf16[512,1792]{1,0:T(8,128)(2,1)} %get-tuple-element.118.refs_1_.refs_2_, bf16[1792,896]{1,0:T(8,128)(2,1)} %get-tuple-element.83.refs_2_, ...), custom_call_target="tpu_custom_call" | custom-call | tf_op jit(solution)/shard_map/pallas_call | solution.py:229
  817.6 2.2 fusion.1
  819.8 0.7 all-reduce.21.cloned.1.call-update
  820.6 1.0 collective-permute-start.3
  821.5 1.4 collective-permute-start.4
  824.3 0.7 concatenate.35.refs_0_
  825.0 57.2 %shard_map.314 = (f32[224,576]{1,0:T(8,128)}, f32[224,448]{1,0:T(8,128)}, f32[8,1792]{1,0:T(8,128)}) custom-call(f32[8,1792]{1,0:T(8,128)} %concatenate.35.refs_0_, bf16[512,1792]{1,0:T(8,128)(2,1)} %get-tuple-element.117.refs_2_.refs_1_, bf16[512,1792]{1,0:T(8,128)(2,1)} %get-tuple-element.118.refs_1_.refs_2_, bf16[512,576]{1,0:T(8,128)(2,1)} %get-tuple-element.119.refs_3_, ...), custom_call_target="tpu_custom_call" | custom-call | tf_op jit(solution)/shard_map/pallas_call | solution.py:229
  882.2 11.7 %shard_map.315 = (f32[512,1792]{1,0:T(8,128)}, f32[64,224]{1,0:T(8,128)}, f32[64,224]{1,0:T(8,128)}, f32[224,448]{1,0:T(8,128)}, f32[4,1792]{1,0:T(4,128)}, /*in...) custom-call(bf16[512,1792]{1,0:T(8,128)(2,1)} %bitcast.116, ...), custom_call_target="tpu_custom_call" | custom-call | tf_op jit(solution)/shard_map/pallas_call | solution.py:805
  (165 shorter events, 13.7 us)
Async XLA Ops:
  7.2 214.3 %all-reduce.9.cloned.1.call-start = ((), (), s32[]{:S(2)}) async-start(), calls=%async_computation | async-start | bytes 3670016 | tf_op jit(solution)/shard_map/psum | solution.py:819
  134.3 4.4 copy-start.42
  134.3 87.2 %copy-start.4 = (bf16[2,2,128,1792]{3,2,1,0:T(8,128)(2,1)S(1)}, bf16[2,2,128,1792]{3,2,1,0:T(8,128)(2,1)}, u32[]{:S(2)}) copy-start(bf16[2,2,128,1792]{3,2,1,0:T(8,128)(2,1)} %param.18) | copy-start | bytes 5505028
  138.5 173.5 %all-reduce.11.cloned.1.call-start = ((), (), s32[]{:S(2)}) async-start(), calls=%async_computation.1 | async-start | bytes 3670016 | tf_op jit(solution)/shard_map/psum | solution.py:819
  221.5 2.3 copy-start.7
  223.8 2.7 copy-start.45
  224.8 4.3 copy-start.16
  226.6 2.6 copy-start.47
  229.1 4.2 copy-start.54
  229.1 5.1 copy-start.49
  234.3 3.9 copy-start.44
  238.1 169.7 %all-reduce.13.cloned.1.call-start = ((), (), s32[]{:S(2)}) async-start(), calls=%async_computation.2 | async-start | bytes 3670016 | tf_op jit(solution)/shard_map/psum | solution.py:819
  315.0 4.0 copy-start
  315.0 2.9 copy-start.34
  315.4 8.1 copy-start.15
  315.4 6.4 copy-start.43
  319.0 4.6 copy-start.25
  319.0 4.2 collective-permute-start
  323.5 2.6 copy-start.18
  323.5 2.6 copy-start.20
  323.5 3.4 copy-start.31
  329.5 224.4 %all-reduce.15.cloned.1.call-start = ((), (), s32[]{:S(2)}) async-start(), calls=%async_computation.3 | async-start | bytes 7340032 | tf_op jit(solution)/shard_map/psum | solution.py:967
  407.8 3.7 copy-start.1
  407.8 4.2 copy-start.9
  412.1 2.8 copy-start.52
  412.6 4.8 copy-start.24
  414.9 2.6 copy-start.51
  417.5 2.6 copy-start.12
  417.5 2.7 copy-start.53
  423.5 2.6 copy-start.39
  423.5 2.6 copy-start.40
  423.5 5.2 copy-start.38
  433.5 195.1 %all-reduce.17.cloned.1.call-start = ((), (), s32[]{:S(2)}) async-start(), calls=%async_computation.4 | async-start | bytes 3670016 | tf_op jit(solution)/shard_map/psum | solution.py:819
  553.9 2.6 copy-start.2
  553.9 3.8 copy-start.10
  555.8 2.9 copy-start.5
  559.2 1.9 copy-start.32
  561.1 3.3 copy-start.23
  561.1 1.9 copy-start.19
  561.1 2.2 copy-start.21
  561.1 2.5 copy-start.29
  561.1 2.8 copy-start.30
  564.4 8.3 copy-start.28
  564.4 5.6 collective-permute-start.1
  571.6 1.7 copy-start.26
  575.7 121.4 %all-reduce.19.cloned.1.call-start = ((), (), s32[]{:S(2)}) async-start(), calls=%async_computation.5 | async-start | bytes 3670016 | tf_op jit(solution)/shard_map/psum | solution.py:819
  628.7 2.6 copy-start.3
  631.3 2.0 copy-start.6
  631.3 2.6 copy-start.11
  631.3 3.2 copy-start.14
  634.4 6.2 copy-start.50
  634.4 6.2 copy-start.55
  634.4 6.2 copy-start.56
  640.6 3.1 copy-start.22
  640.6 3.1 copy-start.46
  643.7 2.6 copy-start.41
  643.7 2.6 copy-start.37
  643.8 3.0 copy-start.48
  697.1 2.1 copy-start.8
  699.1 2.0 copy-start.17
  819.7 62.4 %all-reduce.21.cloned.1.call-start = ((), (), s32[]{:S(2)}) async-start(), calls=%async_computation.6 | async-start | bytes 3670016 | tf_op jit(solution)/shard_map/psum | solution.py:1028
  820.5 3.1 collective-permute-start.2
  820.6 3.7 collective-permute-start.3
  821.5 2.7 collective-permute-start.4
  (5 other events, 6.0 us)
Sparse Core Ops, SparseCore 0:
  138.6 50.5 all-reduce.8
  238.3 46.2 all-reduce.10
  329.6 47.9 all-reduce.12
  433.6 76.0 all-reduce.14
  575.8 46.2 all-reduce.16
  650.7 46.3 all-reduce.18
  823.0 49.9 all-reduce.20

commit v8 on v7

--- a/solution.py
+++ b/solution.py
@@ -938,12 +938,14 @@
     resid_one = inputs + attn_sum
     part, kept_one = mlp_forward(resid_one, gains[1], ffn1)
     ffn1_sum = head_total(part)
-    inner_w, gate_w, gate_2 = gather_all(tie((conv_input, conv_gate, ffn2_gate), part), 4)
+    pair_s = jnp.concatenate([conv_input, conv_gate], axis=1)
+    pair_w, gate_2 = gather_all(tie((pair_s, ffn2_gate), part), 4)
     resid_two = resid_one + ffn1_sum
 
     normed_c = rms_norm(resid_two, gains[2]).astype(BF)
-    inner = dot(normed_c, inner_w, 1, 0).reshape(rows, tok, cw)
-    gate_c = dot(normed_c, gate_w, 1, 0).reshape(rows, tok, cw)
+    pair_c = dot(normed_c, pair_w, 1, 0)
+    inner = pair_c[:, :cw].reshape(rows, tok, cw)
+    gate_c = pair_c[:, cw:].reshape(rows, tok, cw)
     pos = start + jnp.arange(tok + taps - 1, dtype=jnp.int32)
     current = pos[None, :] >= off[:, None]
 
@@ -982,11 +984,12 @@
     )
     d_inner = d_inner.astype(BF).reshape(count, cw)
     kernel_grad = jnp.stack([jnp.sum(d_conv * moved[t], axis=(0, 1)) for t in range(taps)])
-    dn_part = (dot(d_inner, inner_w, 1, 1) + dot(d_gate_c, gate_w, 1, 1)).astype(BF)
+    d_pair = jnp.concatenate([d_inner, d_gate_c], axis=1)
+    dn_part = dot(d_pair, pair_w, 1, 1).astype(BF)
     dn = head_total(dn_part)
     sums_conv = scatter_all(
         tie((normed_c, grad_b), dn_part),
-        ((0, d_inner), (0, d_gate_c), (1, product)),
+        ((0, d_pair), (1, product)),
         6,
         1,
     )
@@ -1040,9 +1043,8 @@
     )
     gains_grad, kernel_grad = sums_attn[2][:4], sums_attn[2][4 : 4 + taps, :cw]
     qkv_sum = sums_attn[0]
-    straight = (sums_one[0], sums_one[1], sums_conv[0], sums_conv[1], sums_two[0], sums_two[1])
-    straight += (sums_one[2], sums_two[2])
-    turned = (sums_conv[2], sums_attn[1])
+    straight = (sums_one[0], sums_one[1], sums_two[0], sums_two[1], sums_one[2], sums_two[2])
+    turned = (sums_conv[1], sums_attn[1])
     if paired:
         input_grad, by_kind, gains_grad, kernel_grad, turned, straight = closing(
             acts_flat,
@@ -1068,14 +1070,14 @@
         turned[1],
         straight[0],
         straight[1],
-        straight[6].T,
+        straight[4].T,
+        sums_conv[0][:, :cw],
+        sums_conv[0][:, cw:],
+        turned[0],
+        kernel_grad,
         straight[2],
         straight[3],
-        turned[0],
-        kernel_grad,
-        straight[4],
-        straight[5],
-        straight[7].T,
+        straight[5].T,
         gains_grad,
     )
 

time: 907 us -> 900 us (level)
    dot_general x19 -> x17, matrix products: 51.1 us -> 49.2 us  [dot(): lax.dot_general(a, b, (((ca,), (cb,)), ((), ())), preferred_element_type=...]
    unnamed x114 -> x112, local copies, waits for them, and re-layouts: 19.5 us -> 20.6 us
  transfers between devices with their start and end apart: 12 -> 12, of which waited for: 5 -> 4; matrix products, arithmetic and copies ran while one was open for 0% -> 0% of each run, Pallas kernels for 56% -> 56%
where the time goes in v8:
time: 900 us; the launch traced here: 894 us
  Pallas kernels  749 us (83%)
  matrix products  49.2 us (5%)
  other arithmetic  40.7 us (5%)
  local copies, waits for them, and re-layouts  24.2 us (3%)
  between operations  15.3 us (2%)
    pallas_call x10, Pallas kernels, run(): pl.pallas_call(partial(self.kernel, body), in_specs=[spec for _, spec in...  738 us
    dot_general x17, matrix products, dot(): lax.dot_general(a, b, (((ca,), (cb,)), ((), ())), preferred_element_type=...  49.2 us
    unnamed x112, local copies, waits for them, and re-layouts  20.6 us
  transfers between devices with their start and end apart: 12, of which 4 were waited for; matrix products, arithmetic and copies ran while one was open for 0% of the time, Pallas kernels for 56%

profile of v8, /device:TPU:0, one launch (start us, length us, event | category | flops | bytes accessed | tf_op | source)
XLA Modules:
  0.0 893.5 jit_solution(4268645941577532719)
XLA Ops:
  7.2 1.3 reshape.174.refs_0_
  8.5 32.1 %shard_map.305 = (bf16[512,1792]{1,0:T(8,128)(2,1)}, bf16[224,896]{1,0:T(8,128)(2,1)}, bf16[1792,576]{1,0:T(8,128)(2,1)}) custom-call(bf16[512,1792]{1,0:T(8,128)(2,1)} %bitcast.111, bf16[4,1792]{1,0:T(4,128)(2,1)} %refs_3_.1, bf16[64,224]{1,0:T(8,128)(2,1)} %bitcast.124, bf16[64,224]{1,0:T(8,128)(2,1)} %bitcast.125, bf16[224,448]{1,0:T(8,128)(2,1)} %refs_4_.2, ...), custom_call_target="tpu_custom_call" | custom-call | tf_op jit(solution)/shard_map/pallas_call | solution.py:229
  40.6 93.7 %shard_map.306 = (bf16[1792,896]{1,0:T(8,128)(2,1)}, bf16[1792,1152]{1,0:T(8,128)(2,1)}, bf16[512,448]{1,0:T(8,128)(2,1)}, bf16[288,1024]{1,0:T(8,128)(2,1)}, f32[224,1024]{1,0:T(8,128)}, /*index=5*/f32[8,1024]{1,0:T(8,128)}) custom-call(s32[4]{0:T(128)} %reshape.174.refs_0_, bf16[1792,576]{1,0:T(8,128)(2,1)} %get-tuple-element.74.refs_1_.refs_3_, ...), custom_call_target="tpu_custom_call" | custom-call | tf_op jit(solution)/shard_map/pallas_call | solution.py:229
  134.4 4.2 convolution_convert_fusion.4
  138.8 82.6 %shard_map.307 = (bf16[1792,1152]{1,0:T(8,128)(2,1)}, bf16[1792,1152]{1,0:T(8,128)(2,1)}) custom-call(bf16[224,1152]{1,0:T(8,128)(2,1)} %refs_0_, bf16[224,1152]{1,0:T(8,128)(2,1)} %bitcast.122), custom_call_target="tpu_custom_call" | custom-call | tf_op jit(solution)/shard_map/pallas_call | solution.py:229
  221.6 0.9 pad_maximum_fusion.6.refs_0_
  222.5 2.3 multiply_reduce_fusion.9
  224.8 1.0 multiply_convert_fusion.2.refs_0_.refs_7_
  225.8 1.7 copy-done.42
  227.5 2.5 fusion.21
  230.1 4.0 multiply_convert_fusion.8
  234.1 1.0 copy-done.30
  235.2 3.8 convolution_convert_fusion.3
  239.4 68.9 %shard_map.308 = (bf16[1792,896]{1,0:T(8,128)(2,1)}, bf16[1792,1152]{1,0:T(8,128)(2,1)}) custom-call(bf16[224,896]{1,0:T(8,128)(2,1)} %pad_maximum_fusion.6.refs_0_, bf16[224,1152]{1,0:T(8,128)(2,1)} %refs_1_.2), custom_call_target="tpu_custom_call" | custom-call | tf_op jit(solution)/shard_map/pallas_call | solution.py:229
  308.3 3.0 multiply_reduce_fusion.8
  311.6 3.5 copy-done.51
  315.1 2.1 fusion.22
  317.4 3.3 collective-permute-start
  320.7 1.4 collective-permute-done
  322.4 1.6 multiply_convert_fusion.10
  324.0 1.3 copy-done.27
  325.3 2.5 convolution_convert_fusion.2
  328.2 77.3 %shard_map.309 = (bf16[1792,1152]{1,0:T(8,128)(2,1)}, bf16[1792,1152]{1,0:T(8,128)(2,1)}) custom-call(bf16[224,1152]{1,0:T(8,128)(2,1)} %refs_0_.1, bf16[224,1152]{1,0:T(8,128)(2,1)} %bitcast.123), custom_call_target="tpu_custom_call" | custom-call | tf_op jit(solution)/shard_map/pallas_call | solution.py:229
  405.6 3.3 multiply_reduce_fusion.7
  410.4 2.3 copy-done.49
  412.7 2.5 fusion.23
  415.3 2.5 fusion.24
  418.0 3.2 multiply_convert_fusion.6
  421.2 2.6 fusion.25
  423.8 2.6 convolution_convert_fusion.1
  426.4 2.6 add_convert_fusion.2
  429.1 2.2 pad_maximum_fusion
  431.3 120.3 %shard_map.310 = (f32[224,1152]{1,0:T(8,128)}, f32[224,1152]{1,0:T(8,128)}, f32[224,1152]{1,0:T(8,128)}) custom-call(bf16[512,1792]{1,0:T(8,128)(2,1)} %copy-done.23, bf16[512,1792]{1,0:T(8,128)(2,1)} %bitcast.116, bf16[512,1152]{1,0:T(8,128)(2,1)} %copy-done.33, bf16[512,1152]{1,0:T(8,128)(2,1)} %copy-done.32, bf16[512,1152]{1,0:T(8,128)(2,1)} %copy-done.34), custom_call_target="tpu_custom_call" | custom-call | tf_op jit(solution)/shard_map/pallas_call | solution.py:229
  551.7 1.9 slice_convert_fusion
  554.3 1.2 copy-done.10
  555.5 1.1 multiply_reduce_fusion
  557.0 1.3 fusion.16.refs_1_
  558.9 1.2 fusion.6
  560.1 0.9 copy-done.17
  561.6 0.7 multiply_reduce_fusion.12
  562.4 1.3 collective-permute-start.1
  564.0 4.0 collective-permute-done.1
  569.0 1.1 copy-done.52
  570.0 3.3 convolution_convert_fusion
  573.8 47.6 %shard_map.311 = (f32[224,896]{1,0:T(8,128)}, f32[224,448]{1,0:T(8,128)}) custom-call(bf16[512,1792]{1,0:T(8,128)(2,1)} %copy-done.24, bf16[512,1792]{1,0:T(8,128)(2,1)} %copy-done.22, bf16[512,896]{1,0:T(8,128)(2,1)} %copy-done.26, bf16[512,448]{1,0:T(8,128)(2,1)} %copy-done.29), custom_call_target="tpu_custom_call" | custom-call | tf_op jit(solution)/shard_map/pallas_call | solution.py:229
  621.5 1.9 convert_element_type.158
  624.1 1.0 multiply_reduce_fusion.1
  625.1 1.1 copy-done.6
  627.2 6.2 fusion.18
  633.5 3.1 multiply_convert_fusion.3
  636.6 2.6 fusion.26
  639.6 3.8 add_convert_fusion
  643.9 45.8 %shard_map.312.refs_6_ = f32[224,1152]{1,0:T(8,128)} custom-call(bf16[512,1792]{1,0:T(8,128)(2,1)} %copy-done.15, bf16[512,1152]{1,0:T(8,128)(2,1)} %copy-done.35), custom_call_target="tpu_custom_call" | custom-call | tf_op jit(solution)/shard_map/pallas_call | solution.py:229
  690.4 1.9 convert_element_type.163
  692.4 1.4 multiply_reduce_fusion.2
  694.4 4.1 fusion.17
  698.5 112.1 %shard_map.313 = (f32[224,1152]{1,0:T(8,128)}, f32[224,1152]{1,0:T(8,128)}, bf16[512,576]{1,0:T(8,128)(2,1)}, bf16[512,1792]{1,0:T(8,128)(2,1)}) custom-call(s32[4]{0:T(128)} %reshape.174.refs_0_, bf16[512,1792]{1,0:T(8,128)(2,1)} %get-tuple-element.110.refs_1_.refs_2_, bf16[1792,896]{1,0:T(8,128)(2,1)} %get-tuple-element.78.refs_2_, ...), custom_call_target="tpu_custom_call" | custom-call | tf_op jit(solution)/shard_map/pallas_call | solution.py:229
  810.7 2.2 fusion.1
  813.0 0.7 all-reduce.21.cloned.1.call-update
  813.8 0.9 collective-permute-start.3
  814.7 1.4 collective-permute-start.4
  816.1 1.1 fusion.19
  818.2 57.1 %shard_map.314 = (f32[224,576]{1,0:T(8,128)}, f32[224,448]{1,0:T(8,128)}, f32[8,1792]{1,0:T(8,128)}) custom-call(f32[8,1792]{1,0:T(8,128)} %concatenate.43.refs_0_, bf16[512,1792]{1,0:T(8,128)(2,1)} %get-tuple-element.109.refs_2_.refs_1_, bf16[512,1792]{1,0:T(8,128)(2,1)} %get-tuple-element.110.refs_1_.refs_2_, bf16[512,576]{1,0:T(8,128)(2,1)} %get-tuple-element.111.refs_3_, ...), custom_call_target="tpu_custom_call" | custom-call | tf_op jit(solution)/shard_map/pallas_call | solution.py:229
  875.3 11.1 %shard_map.315 = (f32[512,1792]{1,0:T(8,128)}, f32[64,224]{1,0:T(8,128)}, f32[64,224]{1,0:T(8,128)}, f32[224,448]{1,0:T(8,128)}, f32[4,1792]{1,0:T(4,128)}, /*in...) custom-call(bf16[512,1792]{1,0:T(8,128)(2,1)} %bitcast.112, ...), custom_call_target="tpu_custom_call" | custom-call | tf_op jit(solution)/shard_map/pallas_call | solution.py:805
  (166 shorter events, 13.1 us)
Async XLA Ops:
  7.2 215.3 %all-reduce.9.cloned.1.call-start = ((), (), s32[]{:S(2)}) async-start(), calls=%async_computation | async-start | bytes 3670016 | tf_op jit(solution)/shard_map/psum | solution.py:819
  134.3 4.5 copy-start.39
  134.3 87.2 %copy-start.37 = (bf16[224,448]{1,0:T(8,128)(2,1)S(1)}, bf16[224,448]{1,0:T(8,128)(2,1)}, u32[]{:S(2)}) copy-start(bf16[224,448]{1,0:T(8,128)(2,1)} %param.29) | copy-start | bytes 602116
  134.4 87.2 %copy-start.38 = (bf16[224,448]{1,0:T(8,128)(2,1)S(1)}, bf16[224,448]{1,0:T(8,128)(2,1)}, u32[]{:S(2)}) copy-start(bf16[224,448]{1,0:T(8,128)(2,1)} %param.28) | copy-start | bytes 602116
  134.4 88.1 %copy-start.4 = (bf16[2,2,128,1792]{3,2,1,0:T(8,128)(2,1)S(1)}, bf16[2,2,128,1792]{3,2,1,0:T(8,128)(2,1)}, u32[]{:S(2)}) copy-start(bf16[2,2,128,1792]{3,2,1,0:T(8,128)(2,1)} %param.18) | copy-start | bytes 5505028
  138.6 169.7 %all-reduce.11.cloned.1.call-start = ((), (), s32[]{:S(2)}) async-start(), calls=%async_computation.1 | async-start | bytes 3670016 | tf_op jit(solution)/shard_map/psum | solution.py:819
  222.5 2.3 copy-start.7
  224.8 2.7 copy-start.42
  225.8 4.3 copy-start.15
  227.5 2.6 copy-start.44
  230.1 4.0 copy-start.53
  230.1 5.1 copy-start.46
  235.2 3.9 copy-start.41
  239.0 166.6 %all-reduce.13.cloned.1.call-start = ((), (), s32[]{:S(2)}) async-start(), calls=%async_computation.2 | async-start | bytes 3670016 | tf_op jit(solution)/shard_map/psum | solution.py:819
  311.2 6.0 copy-start
  311.2 3.9 copy-start.51
  311.6 5.6 copy-start.24
  315.1 5.6 copy-start.40
  317.2 6.8 copy-start.16
  317.4 4.7 collective-permute-start
  322.4 2.9 copy-start.27
  324.0 81.5 %copy-start.29 = (bf16[512,448]{1,0:T(8,128)(2,1)}, bf16[512,448]{1,0:T(8,128)(2,1)S(1)}, u32[]{:S(2)}) copy-start(bf16[512,448]{1,0:T(8,128)(2,1)S(1)} %get-tuple-element.148.refs_3_) | copy-start | bytes 1376260
  327.8 223.9 %all-reduce.15.cloned.1.call-start = ((), (), s32[]{:S(2)}) async-start(), calls=%async_computation.3 | async-start | bytes 7340032 | tf_op jit(solution)/shard_map/psum | solution.py:969
  405.6 3.7 copy-start.1
  405.6 4.2 copy-start.9
  409.8 2.8 copy-start.49
  410.4 4.8 copy-start.23
  412.7 2.6 copy-start.48
  415.2 2.6 copy-start.12
  415.3 2.7 copy-start.50
  421.2 2.6 copy-start.33
  421.2 2.6 copy-start.34
  421.2 5.2 copy-start.32
  431.3 190.2 %all-reduce.17.cloned.1.call-start = ((), (), s32[]{:S(2)}) async-start(), calls=%async_computation.4 | async-start | bytes 3670016 | tf_op jit(solution)/shard_map/psum | solution.py:819
  551.7 2.6 copy-start.2
  551.7 3.8 copy-start.10
  553.6 2.9 copy-start.5
  558.9 3.5 copy-start.22
  558.9 2.2 copy-start.17
  558.9 2.4 copy-start.20
  558.9 2.7 copy-start.25
  562.4 5.6 collective-permute-start.1
  568.1 1.9 copy-start.52
  570.0 3.3 copy-start.26
  573.4 117.0 %all-reduce.19.cloned.1.call-start = ((), (), s32[]{:S(2)}) async-start(), calls=%async_computation.5 | async-start | bytes 3670016 | tf_op jit(solution)/shard_map/psum | solution.py:819
  621.5 2.6 copy-start.3
  624.1 2.0 copy-start.6
  624.1 2.6 copy-start.11
  624.1 3.2 copy-start.14
  627.2 6.2 copy-start.47
  627.2 6.2 copy-start.54
  627.2 6.2 copy-start.55
  633.4 3.1 copy-start.21
  633.5 3.1 copy-start.43
  636.6 2.6 copy-start.35
  636.6 2.6 copy-start.31
  636.6 3.0 copy-start.45
  690.3 2.1 copy-start.8
  692.4 2.0 copy-start.18
  810.6 5.5 copy-start.36
  812.9 62.4 %all-reduce.21.cloned.1.call-start = ((), (), s32[]{:S(2)}) async-start(), calls=%async_computation.6 | async-start | bytes 3670016 | tf_op jit(solution)/shard_map/psum | solution.py:1031
  813.7 3.5 collective-permute-start.2
  813.8 3.7 collective-permute-start.3
  814.7 2.7 collective-permute-start.4
  (4 other events, 6.0 us)
Sparse Core Ops, SparseCore 0:
  138.7 50.5 all-reduce.8
  239.1 46.2 all-reduce.10
  327.9 47.8 all-reduce.12
  431.4 75.9 all-reduce.14
  573.5 46.1 all-reduce.16
  643.6 46.7 all-reduce.18
  816.1 49.9 all-reduce.20

commit v9 on v8

--- a/solution.py
+++ b/solution.py
@@ -388,6 +388,8 @@
         names.append(call.give("small.sum", small.shape, F32))
 
     def body(at, rings):
+        if small is not None:
+            rings["small"] = rings.pop("small")
         in_turn(n)(at, rings)
         if small is not None:
             rings["small"].finish()

time: 900 us -> 904 us (level)
  no operation moved by 1% of the time
where the time goes in v9:
time: 904 us; the launch traced here: 897 us
  Pallas kernels  753 us (83%)
  matrix products  49.2 us (5%)
  other arithmetic  40.7 us (5%)
  local copies, waits for them, and re-layouts  24.2 us (3%)
  between operations  15.3 us (2%)
    pallas_call x10, Pallas kernels, run(): pl.pallas_call(partial(self.kernel, body), in_specs=[spec for _, spec in...  741 us
    dot_general x17, matrix products, dot(): lax.dot_general(a, b, (((ca,), (cb,)), ((), ())), preferred_element_type=...  49.2 us
    unnamed x112, local copies, waits for them, and re-layouts  20.6 us
  transfers between devices with their start and end apart: 12, of which 4 were waited for; matrix products, arithmetic and copies ran while one was open for 0% of the time, Pallas kernels for 56%

profile of v9, /device:TPU:0, one launch (start us, length us, event | category | flops | bytes accessed | tf_op | source)
XLA Modules:
  0.0 897.3 jit_solution(341926886061433204)
XLA Ops:
  7.2 1.3 reshape.174.refs_0_
  8.5 32.1 %shard_map.305 = (bf16[512,1792]{1,0:T(8,128)(2,1)}, bf16[224,896]{1,0:T(8,128)(2,1)}, bf16[1792,576]{1,0:T(8,128)(2,1)}) custom-call(bf16[512,1792]{1,0:T(8,128)(2,1)} %bitcast.111, bf16[4,1792]{1,0:T(4,128)(2,1)} %refs_3_.1, bf16[64,224]{1,0:T(8,128)(2,1)} %bitcast.124, bf16[64,224]{1,0:T(8,128)(2,1)} %bitcast.125, bf16[224,448]{1,0:T(8,128)(2,1)} %refs_4_.2, ...), custom_call_target="tpu_custom_call" | custom-call | tf_op jit(solution)/shard_map/pallas_call | solution.py:229
  40.6 93.7 %shard_map.306 = (bf16[1792,896]{1,0:T(8,128)(2,1)}, bf16[1792,1152]{1,0:T(8,128)(2,1)}, bf16[512,448]{1,0:T(8,128)(2,1)}, bf16[288,1024]{1,0:T(8,128)(2,1)}, f32[224,1024]{1,0:T(8,128)}, /*index=5*/f32[8,1024]{1,0:T(8,128)}) custom-call(s32[4]{0:T(128)} %reshape.174.refs_0_, bf16[1792,576]{1,0:T(8,128)(2,1)} %get-tuple-element.74.refs_1_.refs_3_, ...), custom_call_target="tpu_custom_call" | custom-call | tf_op jit(solution)/shard_map/pallas_call | solution.py:229
  134.4 4.2 convolution_convert_fusion.4
  138.8 82.6 %shard_map.307 = (bf16[1792,1152]{1,0:T(8,128)(2,1)}, bf16[1792,1152]{1,0:T(8,128)(2,1)}) custom-call(bf16[224,1152]{1,0:T(8,128)(2,1)} %refs_0_, bf16[224,1152]{1,0:T(8,128)(2,1)} %bitcast.122), custom_call_target="tpu_custom_call" | custom-call | tf_op jit(solution)/shard_map/pallas_call | solution.py:229
  221.6 0.9 pad_maximum_fusion.6.refs_0_
  222.5 2.3 multiply_reduce_fusion.9
  224.8 1.0 multiply_convert_fusion.2.refs_0_.refs_7_
  225.8 1.7 copy-done.42
  227.5 2.5 fusion.21
  230.1 4.0 multiply_convert_fusion.8
  234.1 1.0 copy-done.30
  235.2 3.8 convolution_convert_fusion.3
  239.4 68.9 %shard_map.308 = (bf16[1792,896]{1,0:T(8,128)(2,1)}, bf16[1792,1152]{1,0:T(8,128)(2,1)}) custom-call(bf16[224,896]{1,0:T(8,128)(2,1)} %pad_maximum_fusion.6.refs_0_, bf16[224,1152]{1,0:T(8,128)(2,1)} %refs_1_.2), custom_call_target="tpu_custom_call" | custom-call | tf_op jit(solution)/shard_map/pallas_call | solution.py:229
  308.3 3.0 multiply_reduce_fusion.8
  311.6 3.5 copy-done.51
  315.1 2.1 fusion.22
  317.4 3.3 collective-permute-start
  320.7 1.4 collective-permute-done
  322.4 1.6 multiply_convert_fusion.10
  324.0 1.3 copy-done.27
  325.3 2.5 convolution_convert_fusion.2
  328.2 77.3 %shard_map.309 = (bf16[1792,1152]{1,0:T(8,128)(2,1)}, bf16[1792,1152]{1,0:T(8,128)(2,1)}) custom-call(bf16[224,1152]{1,0:T(8,128)(2,1)} %refs_0_.1, bf16[224,1152]{1,0:T(8,128)(2,1)} %bitcast.123), custom_call_target="tpu_custom_call" | custom-call | tf_op jit(solution)/shard_map/pallas_call | solution.py:229
  405.6 3.3 multiply_reduce_fusion.7
  410.4 2.3 copy-done.49
  412.7 2.5 fusion.23
  415.3 2.5 fusion.24
  418.0 3.2 multiply_convert_fusion.6
  421.2 2.6 fusion.25
  423.8 2.6 convolution_convert_fusion.1
  426.4 2.6 add_convert_fusion.2
  429.1 2.2 pad_maximum_fusion
  431.3 120.3 %shard_map.310 = (f32[224,1152]{1,0:T(8,128)}, f32[224,1152]{1,0:T(8,128)}, f32[224,1152]{1,0:T(8,128)}) custom-call(bf16[512,1792]{1,0:T(8,128)(2,1)} %copy-done.23, bf16[512,1792]{1,0:T(8,128)(2,1)} %bitcast.116, bf16[512,1152]{1,0:T(8,128)(2,1)} %copy-done.33, bf16[512,1152]{1,0:T(8,128)(2,1)} %copy-done.32, bf16[512,1152]{1,0:T(8,128)(2,1)} %copy-done.34), custom_call_target="tpu_custom_call" | custom-call | tf_op jit(solution)/shard_map/pallas_call | solution.py:229
  551.7 1.9 slice_convert_fusion
  554.3 1.2 copy-done.10
  555.5 1.1 multiply_reduce_fusion
  557.0 1.3 fusion.16.refs_1_
  558.9 1.2 fusion.6
  560.1 0.9 copy-done.17
  561.6 0.7 multiply_reduce_fusion.12
  562.4 1.3 collective-permute-start.1
  564.0 4.0 collective-permute-done.1
  569.0 1.1 copy-done.52
  570.0 3.3 convolution_convert_fusion
  573.8 47.6 %shard_map.311 = (f32[224,896]{1,0:T(8,128)}, f32[224,448]{1,0:T(8,128)}) custom-call(bf16[512,1792]{1,0:T(8,128)(2,1)} %copy-done.24, bf16[512,1792]{1,0:T(8,128)(2,1)} %copy-done.22, bf16[512,896]{1,0:T(8,128)(2,1)} %copy-done.26, bf16[512,448]{1,0:T(8,128)(2,1)} %copy-done.29), custom_call_target="tpu_custom_call" | custom-call | tf_op jit(solution)/shard_map/pallas_call | solution.py:229
  621.5 1.9 convert_element_type.158
  624.1 1.0 multiply_reduce_fusion.1
  625.1 1.1 copy-done.6
  627.2 6.2 fusion.18
  633.5 3.1 multiply_convert_fusion.3
  636.6 2.6 fusion.26
  639.6 3.8 add_convert_fusion
  643.9 45.8 %shard_map.312.refs_6_ = f32[224,1152]{1,0:T(8,128)} custom-call(bf16[512,1792]{1,0:T(8,128)(2,1)} %copy-done.15, bf16[512,1152]{1,0:T(8,128)(2,1)} %copy-done.35), custom_call_target="tpu_custom_call" | custom-call | tf_op jit(solution)/shard_map/pallas_call | solution.py:229
  690.4 1.9 convert_element_type.163
  692.4 1.4 multiply_reduce_fusion.2
  694.4 4.1 fusion.17
  698.5 112.1 %shard_map.313 = (f32[224,1152]{1,0:T(8,128)}, f32[224,1152]{1,0:T(8,128)}, bf16[512,576]{1,0:T(8,128)(2,1)}, bf16[512,1792]{1,0:T(8,128)(2,1)}) custom-call(s32[4]{0:T(128)} %reshape.174.refs_0_, bf16[512,1792]{1,0:T(8,128)(2,1)} %get-tuple-element.110.refs_1_.refs_2_, bf16[1792,896]{1,0:T(8,128)(2,1)} %get-tuple-element.78.refs_2_, ...), custom_call_target="tpu_custom_call" | custom-call | tf_op jit(solution)/shard_map/pallas_call | solution.py:229
  810.7 2.2 fusion.1
  813.0 0.7 all-reduce.21.cloned.1.call-update
  813.8 0.9 collective-permute-start.3
  814.7 1.4 collective-permute-start.4
  816.1 1.1 fusion.19
  818.2 60.9 %shard_map.314 = (f32[224,576]{1,0:T(8,128)}, f32[224,448]{1,0:T(8,128)}, f32[8,1792]{1,0:T(8,128)}) custom-call(f32[8,1792]{1,0:T(8,128)} %concatenate.43.refs_0_, bf16[512,1792]{1,0:T(8,128)(2,1)} %get-tuple-element.109.refs_2_.refs_1_, bf16[512,1792]{1,0:T(8,128)(2,1)} %get-tuple-element.110.refs_1_.refs_2_, bf16[512,576]{1,0:T(8,128)(2,1)} %get-tuple-element.111.refs_3_, ...), custom_call_target="tpu_custom_call" | custom-call | tf_op jit(solution)/shard_map/pallas_call | solution.py:229
  879.1 11.1 %shard_map.315 = (f32[512,1792]{1,0:T(8,128)}, f32[64,224]{1,0:T(8,128)}, f32[64,224]{1,0:T(8,128)}, f32[224,448]{1,0:T(8,128)}, f32[4,1792]{1,0:T(4,128)}, /*in...) custom-call(bf16[512,1792]{1,0:T(8,128)(2,1)} %bitcast.112, ...), custom_call_target="tpu_custom_call" | custom-call | tf_op jit(solution)/shard_map/pallas_call | solution.py:807
  (166 shorter events, 13.1 us)
Async XLA Ops:
  7.2 215.3 %all-reduce.9.cloned.1.call-start = ((), (), s32[]{:S(2)}) async-start(), calls=%async_computation | async-start | bytes 3670016 | tf_op jit(solution)/shard_map/psum | solution.py:821
  134.3 4.5 copy-start.39
  134.3 87.2 %copy-start.37 = (bf16[224,448]{1,0:T(8,128)(2,1)S(1)}, bf16[224,448]{1,0:T(8,128)(2,1)}, u32[]{:S(2)}) copy-start(bf16[224,448]{1,0:T(8,128)(2,1)} %param.29) | copy-start | bytes 602116
  134.4 87.2 %copy-start.38 = (bf16[224,448]{1,0:T(8,128)(2,1)S(1)}, bf16[224,448]{1,0:T(8,128)(2,1)}, u32[]{:S(2)}) copy-start(bf16[224,448]{1,0:T(8,128)(2,1)} %param.28) | copy-start | bytes 602116
  134.4 88.1 %copy-start.4 = (bf16[2,2,128,1792]{3,2,1,0:T(8,128)(2,1)S(1)}, bf16[2,2,128,1792]{3,2,1,0:T(8,128)(2,1)}, u32[]{:S(2)}) copy-start(bf16[2,2,128,1792]{3,2,1,0:T(8,128)(2,1)} %param.18) | copy-start | bytes 5505028
  138.6 169.7 %all-reduce.11.cloned.1.call-start = ((), (), s32[]{:S(2)}) async-start(), calls=%async_computation.1 | async-start | bytes 3670016 | tf_op jit(solution)/shard_map/psum | solution.py:821
  222.5 2.3 copy-start.7
  224.8 2.7 copy-start.42
  225.8 4.3 copy-start.15
  227.5 2.6 copy-start.44
  230.1 4.0 copy-start.53
  230.1 5.1 copy-start.46
  235.2 3.9 copy-start.41
  239.0 166.6 %all-reduce.13.cloned.1.call-start = ((), (), s32[]{:S(2)}) async-start(), calls=%async_computation.2 | async-start | bytes 3670016 | tf_op jit(solution)/shard_map/psum | solution.py:821
  311.2 6.0 copy-start
  311.2 3.9 copy-start.51
  311.6 5.6 copy-start.24
  315.1 5.6 copy-start.40
  317.2 6.8 copy-start.16
  317.4 4.7 collective-permute-start
  322.4 2.9 copy-start.27
  324.0 81.5 %copy-start.29 = (bf16[512,448]{1,0:T(8,128)(2,1)}, bf16[512,448]{1,0:T(8,128)(2,1)S(1)}, u32[]{:S(2)}) copy-start(bf16[512,448]{1,0:T(8,128)(2,1)S(1)} %get-tuple-element.148.refs_3_) | copy-start | bytes 1376260
  327.8 223.9 %all-reduce.15.cloned.1.call-start = ((), (), s32[]{:S(2)}) async-start(), calls=%async_computation.3 | async-start | bytes 7340032 | tf_op jit(solution)/shard_map/psum | solution.py:971
  405.6 3.7 copy-start.1
  405.6 4.2 copy-start.9
  409.8 2.8 copy-start.49
  410.4 4.8 copy-start.23
  412.7 2.6 copy-start.48
  415.2 2.6 copy-start.12
  415.3 2.7 copy-start.50
  421.2 2.6 copy-start.33
  421.2 2.6 copy-start.34
  421.2 5.2 copy-start.32
  431.3 190.2 %all-reduce.17.cloned.1.call-start = ((), (), s32[]{:S(2)}) async-start(), calls=%async_computation.4 | async-start | bytes 3670016 | tf_op jit(solution)/shard_map/psum | solution.py:821
  551.7 2.6 copy-start.2
  551.7 3.8 copy-start.10
  553.6 2.9 copy-start.5
  558.9 3.5 copy-start.22
  558.9 2.2 copy-start.17
  558.9 2.4 copy-start.20
  558.9 2.7 copy-start.25
  562.4 5.6 collective-permute-start.1
  568.1 1.9 copy-start.52
  570.0 3.3 copy-start.26
  573.4 117.0 %all-reduce.19.cloned.1.call-start = ((), (), s32[]{:S(2)}) async-start(), calls=%async_computation.5 | async-start | bytes 3670016 | tf_op jit(solution)/shard_map/psum | solution.py:821
  621.5 2.6 copy-start.3
  624.1 2.0 copy-start.6
  624.1 2.6 copy-start.11
  624.1 3.2 copy-start.14
  627.2 6.2 copy-start.47
  627.2 6.2 copy-start.54
  627.2 6.2 copy-start.55
  633.4 3.1 copy-start.21
  633.5 3.1 copy-start.43
  636.6 2.6 copy-start.35
  636.6 2.6 copy-start.31
  636.6 3.0 copy-start.45
  690.3 2.1 copy-start.8
  692.4 2.0 copy-start.18
  810.6 5.5 copy-start.36
  812.9 66.2 %all-reduce.21.cloned.1.call-start = ((), (), s32[]{:S(2)}) async-start(), calls=%async_computation.6 | async-start | bytes 3670016 | tf_op jit(solution)/shard_map/psum | solution.py:1033
  813.7 3.5 collective-permute-start.2
  813.8 3.7 collective-permute-start.3
  814.7 2.7 collective-permute-start.4
  (4 other events, 6.0 us)
Sparse Core Ops, SparseCore 0:
  138.7 50.5 all-reduce.8
  239.1 46.2 all-reduce.10
  327.9 47.8 all-reduce.12
  431.4 75.9 all-reduce.14
  573.5 46.1 all-reduce.16
  643.6 46.7 all-reduce.18
  816.1 49.9 all-reduce.20
